TPU v7x, 32 devices: a whole 2x2x4 slice. The times are simulated.
32 devices in a mesh: members: 2 (over y), gx: 16 (over z, x, core).
Axes of the slice: x: 2, y: 2, z: 4, core: 2. Of those that a mesh axis runs over, the one named last changes fastest.
Arguments:
- pressure: float32 [64, 32, 128], P(('members', 'gx')), parts along dimension 0, may hold values from -6 to 6
- saturation: float32 [64, 32, 128], P(('members', 'gx')), parts along dimension 0, may hold values from 0.1 to 0.9
- lam_water: float32 [64, 32, 128], P(('members', 'gx')), parts along dimension 0, may hold values from -6 to 6
- lam_oil: float32 [64, 32, 128], P(('members', 'gx')), parts along dimension 0, may hold values from -6 to 6
- perm_x: float32 [64, 32, 128], P(('members', 'gx')), parts along dimension 0, may hold values from 0.1 to 10
- perm_y: float32 [64, 32, 128], P(('members', 'gx')), parts along dimension 0, may hold values from 0.1 to 10
- perm_z: float32 [64, 32, 128], P(('members', 'gx')), parts along dimension 0, may hold values from 0.05 to 2
- pore_volume: float32 [64, 32, 128], P(('members', 'gx')), parts along dimension 0, may hold values from 0.3 to 3
- perf_cell: int32 [8192], P(('members', 'gx')), parts along dimension 0, may hold values from 0 to 8191
- perf_well: int32 [8192], P(('members', 'gx')), parts along dimension 0, may hold values from 0 to 255
- well_index: float32 [8192], P(('members', 'gx')), parts along dimension 0, may hold values from 0.5 to 5
- well_pressure: float32 [512], P(('members', 'gx')), parts along dimension 0, may hold values from -6 to 6
Outputs:
- grad_sat: float32 [64, 32, 128], P(('members', 'gx')), parts along dimension 0
- grad_bhp: float32 [512], P(('members', 'gx')), parts along dimension 0
- pressure_adj: float32 [64, 128, 32], P(('members', 'gx')), parts along dimension 0
There are 2 independent parts, one for each index of `members`. A program takes and returns all parts, laid end to end along the dimension named above; each array names one. Nothing has to cross between parts.
Inputs may be any that keep to these rules, and one draw needn't show every extreme that they name: `perf_cell`: perforation r lies in the box of device r // 256; the number counts cells of that box with x slowest and z fastest.
All inputs are finite; a program needn't handle non-finite values.
Results may differ from a plain program's by a relative error of at most 0.0001.
Values sent between devices are 32-bit elements; how exact they have to be, the bound alone decides.
No kernel may reach another device: no remote copies, remote signals or barrier semaphores. Data moves between devices by JAX's collectives and lax.ppermute only.
A program may use at most 64 MiB of HBM per device.

v0:
```python
import functools

import jax
import jax.numpy as jnp
from jax import lax
from jax.experimental import pallas as pl
from jax.experimental.pallas import tpu as pltpu
from jax.sharding import PartitionSpec as P

water_viscosity = 0.5
oil_viscosity = 2.0
compressibility = 0.2
SWEEPS = 4

LANES = 128
TILE = 8
HALO = 3
ROWS = 5
RHS, DIAG, SAT, LAMW, LAMO, PERMX, CY, CZ = range(8)
OUTSIDE = (0.0, 1.0, 0.0, 0.0, 0.0, 1.0, 0.0, 0.0)
FIELDS = 8
WELL_ROW = CZ * 2 * ROWS
CHUNK = FIELDS * 2 * ROWS


def mobilities(s):
    return s * s * (1.0 / water_viscosity), (1.0 - s) * (1.0 - s) * (1.0 / oil_viscosity)


def slopes(s):
    return s * (2.0 / water_viscosity), (s - 1.0) * (2.0 / oil_viscosity)


def split(x):
    first = x.astype(jnp.bfloat16)
    rest = x - first.astype(jnp.float32)
    second = rest.astype(jnp.bfloat16)
    third = (rest - second.astype(jnp.float32)).astype(jnp.bfloat16)
    return first, second, third


def dot(a, b, over):
    return lax.dot_general(a, b, (over, ((), ())), preferred_element_type=jnp.float32)


def add_thirds(x):
    n = x.shape[0] // 3
    return x[:n] + x[n : 2 * n] + x[2 * n :]


def marks(index, count):
    return (lax.broadcasted_iota(jnp.int32, (count, index.shape[1]), 0) == index).astype(jnp.float32)


def scatter_cells(values, row_marks, lane_marks):
    left = jnp.concatenate([(row_marks * part.astype(jnp.float32)).astype(jnp.bfloat16) for part in split(values)])
    return add_thirds(dot(left, lane_marks.astype(jnp.bfloat16), ((1,), (1,))))


def upper(x, axis):
    return pltpu.roll(x, x.shape[axis] - 1, axis)


def lower(x, axis):
    return pltpu.roll(x, 1, axis)


def transmissibility(k, axis):
    kn = upper(k, axis)
    at = lax.broadcasted_iota(jnp.int32, k.shape, axis)
    return jnp.where(at < k.shape[axis] - 1, 2.0 * k * kn / (k + kn), 0.0)


def face(here, there, trans):
    lw, lo, mw, mo = here
    lwn, lon, mwn, mon = there
    fw = mw + mwn
    fo = mo + mon
    return trans * (fw * (lw - lwn) + fo * (lo - lon)), trans * (fw + fo)


def pack_kernel(groups, *refs):
    sources, (packed, weight, above, below) = refs[:12], refs[12:16]
    loaded, padded, well_rows, sems = refs[16:28], refs[28], refs[29], refs[30]
    copies = [pltpu.make_async_copy(src, dst, sems.at[i]) for i, (src, dst) in enumerate(zip(sources, loaded))]
    for i in (8, 10, 9, 11, 1, 2, 3, 5, 6, 7, 4, 0):
        copies[i].start()
    press, sat, lamw, lamo, permx, permy, permz, pore, cell, well, index, bhp = loaded
    ny = sat.shape[1]
    for i in (8, 10):
        copies[i].wait()
    cells = cell[...]
    row_marks = marks(cells // LANES, 2 * ny)
    lane_marks = marks(cells % LANES, LANES)
    perf_weight = scatter_cells(index[...], row_marks, lane_marks)
    weight[...] = perf_weight
    for i in (0, 1, 2, 3, 4, 5, 6, 7, 9, 11):
        copies[i].wait()

    flows = []
    for x in range(2):
        s, lw, lo = sat[x], lamw[x], lamo[x]
        mw, mo = mobilities(s)
        here = (lw, lo, mw, mo)
        flow = mw * lw + mo * lo
        flows.append(flow)
        w = perf_weight[x * ny : (x + 1) * ny]
        rhs = flow * w
        diag = compressibility * pore[x] + (mw + mo) * w
        couplings = []
        for k, axis in ((permy[x], 0), (permz[x], 1)):
            there = tuple(upper(f, axis) for f in here)
            g, c = face(here, there, 0.5 * transmissibility(k, axis))
            rhs = rhs + g - lower(g, axis)
            diag = diag + c + lower(c, axis)
            couplings.append(c)
        for field, value in enumerate((rhs, diag, s, lw, lo, permx[x], *couplings)):
            edge = jnp.full((TILE, LANES), OUTSIDE[field], jnp.float32)
            padded[field, x, :TILE] = edge
            padded[field, x, TILE : TILE + ny] = value
            padded[field, x, TILE + ny :] = edge
    for member, field in enumerate((press, sat, lamw, lamo, permx)):
        above[member] = field[1]
        below[member] = field[0]

    flow_parts = jnp.concatenate(split(jnp.concatenate(flows)))
    row_parts = jnp.concatenate([row_marks.astype(jnp.bfloat16)] * 3)
    by_lane = dot(flow_parts, row_parts, ((0,), (0,)))
    inflow = index[...] * jnp.sum(by_lane * lane_marks, axis=0, keepdims=True)
    wells_each = bhp.shape[1]
    owners = marks(well[...] // wells_each, groups)
    places = marks(well[...] % wells_each + wells_each, LANES)
    well_rows[...] = scatter_cells(inflow, owners, places)
    well_rows[:, :wells_each] = jnp.broadcast_to(bhp[...], (groups, wells_each))

    def chip(c, _):
        for parity in range(2):
            d = 2 * c + parity
            start = TILE + 4 * c - HALO + ROWS * parity
            for field in range(FIELDS):
                for x in range(2):
                    at = (2 * field + x) * ROWS
                    if at == WELL_ROW:
                        packed[d, at + 1 : at + ROWS] = padded[field, x, pl.ds(start + 1 - parity, ROWS - 1)]
                    else:
                        packed[d, at : at + ROWS] = padded[field, x, pl.ds(start, ROWS)]
            packed[d, WELL_ROW : WELL_ROW + 1] = well_rows[pl.ds(d, 1)]
        return 0

    if groups <= 16:
        for c in range(groups // 2):
            chip(c, 0)
    else:
        lax.fori_loop(0, groups // 2, chip, 0)


def sat_kernel(press, sat, lamw, lamo, permx, permy, permz, pore, weight, from_below, from_above, out):
    ny = sat.shape[1]

    def parts(here, there, trans):
        p, lw, lo = here
        pn, lwn, lon = there
        t = trans * (p - pn)
        return t * (lw - lwn), t * (lo - lon)

    layers = [tuple(r[x] for r in (press, lamw, lamo)) for x in range(2)]
    ends = [tuple(r[m] for m in (0, 2, 3)) for r in (from_below, from_above)]
    chain = (ends[0], *layers, ends[1])
    perms = (from_below[4], permx[0], permx[1], from_above[4])
    across = []
    for i in range(3):
        k, kn = perms[i], perms[i + 1]
        across.append(parts(chain[i], chain[i + 1], k * kn / (k + kn)))
    for x in range(2):
        p, lw, lo = layers[x]
        water, oil = (a + b for a, b in zip(across[x], across[x + 1]))
        for k, axis in ((permy[x], 0), (permz[x], 1)):
            there = tuple(upper(f, axis) for f in layers[x])
            a, b = parts(layers[x], there, 0.5 * transmissibility(k, axis))
            water = water + a + lower(a, axis)
            oil = oil + b + lower(b, axis)
        dw, do = slopes(sat[x])
        well = weight[x * ny : (x + 1) * ny] * p
        out[x] = pore[x] * (lw - lo) + dw * (water + well * lw) + do * (oil + well * lo)


def well_kernel(partial, sat, lamw, lamo, cell, well, index, well_rows, out, grad_bhp):
    ny = sat.shape[1]
    groups = well_rows.shape[0]
    wells_each = grad_bhp.shape[1]
    rows = well_rows[...]
    place = well[...] % wells_each
    owners = marks(well[...] // wells_each, groups)
    by_owner = add_thirds(
        dot(jnp.concatenate(split(rows)), marks(place, LANES).astype(jnp.bfloat16), ((1,), (0,)))
    )
    pressure = jnp.sum(by_owner * owners, axis=0, keepdims=True)
    cells = cell[...]
    drop = scatter_cells(index[...] * pressure, marks(cells // LANES, 2 * ny), marks(cells % LANES, LANES))
    for x in range(2):
        dw, do = slopes(sat[x])
        out[x] = partial[x] - (dw * lamw[x] + do * lamo[x]) * drop[x * ny : (x + 1) * ny]
    total = -jnp.sum(rows, axis=0, keepdims=True)
    grad_bhp[...] = total[:, wells_each : 2 * wells_each]


def swap(x):
    return pltpu.roll(x, 4, 0)


def sublane():
    return lax.broadcasted_iota(jnp.int32, (TILE, LANES), 0)


def core():
    return lax.axis_index("gx") % 2


def face_kernel(received, _, own, send, well_rows):
    total = received.shape[0]
    groups = total // CHUNK
    low = sublane() < 4

    def body(parity):
        def tile(x, field):
            at = (x // 2) * CHUNK + (2 * field + x % 2) * ROWS
            start = at - HALO * parity
            if field == CZ and x % 2 == 0:
                start += parity
            inside = min(max(start, 0), total - TILE)
            rows = received[inside : inside + TILE]
            return rows if inside == start else pltpu.roll(rows, (inside - start) % TILE, 0)

        count = 2 * groups
        cells = []
        for x in range(count):
            cells.append((tile(x, LAMW), tile(x, LAMO), *mobilities(tile(x, SAT)), tile(x, PERMX)))
        before = None
        waiting = []
        for x in range(count):
            rhs, diag = tile(x, RHS), tile(x, DIAG)
            if before is not None:
                rhs, diag = rhs - before[0], diag + before[1]
            if x < count - 1:
                k, kn = cells[x][4], cells[x + 1][4]
                before = face(cells[x][:4], cells[x + 1][:4], k * kn / (k + kn))
                rhs, diag, link = rhs + before[0], diag + before[1], before[1]
            else:
                link = jnp.zeros_like(rhs)
            fields = (rhs, diag, link, tile(x, CY), tile(x, CZ))
            for f, value in enumerate(fields):
                own[f, x * TILE : (x + 1) * TILE] = value
            waiting += fields
            while len(waiting) >= 2:
                a, b = waiting[:2]
                waiting = waiting[2:]
                at = ((5 * x + 5 - len(waiting)) // 2 - 1) * TILE
                send[at : at + TILE] = jnp.where(low, pltpu.roll(a, TILE - 2, 0), pltpu.roll(b, 2, 0))

    for parity in range(2):
        pl.when(core() == parity)(functools.partial(body, parity))
    for s in range(groups):
        well_rows[s : s + 1] = received[s * CHUNK + WELL_ROW : s * CHUNK + WELL_ROW + 1]


def sweep(targets, weights, inverses, middle):
    count = len(targets)
    half = count // 2
    b = list(targets)
    for j in range(1, half):
        b[j] = b[j] + weights[j - 1] * b[j - 1]
        m = count - 1 - j
        b[m] = b[m] + weights[m + 1] * b[m + 1]
    da, db, c, inverse = middle
    u = [None] * count
    u[half - 1] = (b[half - 1] * db + c * b[half]) * inverse
    u[half] = (b[half] * da + c * b[half - 1]) * inverse
    for j in range(half - 2, -1, -1):
        u[j] = inverses[j] * b[j] + weights[j] * u[j + 1]
        m = count - 1 - j
        u[m] = inverses[m] * b[m] + weights[m] * u[m - 1]
    return u


def sweep_kernel(sweeps, own, other, out):
    count = own.shape[1] // TILE
    half = count // 2
    row = sublane()
    first = core() == 0
    kept = jnp.logical_and(row >= jnp.where(first, 0, HALO), row < jnp.where(first, ROWS, TILE))
    fields = [[], [], [], [], []]
    for i in range(5 * count // 2):
        packed = other[i * TILE : (i + 1) * TILE]
        turned = swap(packed)
        for n, value in ((2 * i, jnp.where(first, turned, packed)), (2 * i + 1, jnp.where(first, packed, turned))):
            x, f = n // 5, n % 5
            fields[f].append(jnp.where(kept, own[f, x * TILE : (x + 1) * TILE], value))
    rhs, diag, link, cy, cz = fields
    weights, inverses = [None] * count, [None] * count
    da, db = diag[0], diag[count - 1]
    for j in range(half - 1):
        m = count - 1 - j
        inverses[j], inverses[m] = 1.0 / da, 1.0 / db
        weights[j], weights[m] = link[j] * inverses[j], link[m - 1] * inverses[m]
        da = diag[j + 1] - link[j] * weights[j]
        db = diag[m - 1] - link[m - 1] * weights[m]
    c = link[half - 1]
    middle = (da, db, c, 1.0 / (da * db - c * c))

    u = sweep(rhs, weights, inverses, middle)
    for _ in range(1, sweeps):
        targets = []
        for x in range(count):
            t = rhs[x] + cy[x] * upper(u[x], 0) + lower(cy[x] * u[x], 0)
            targets.append(t + cz[x] * upper(u[x], 1) + lower(cz[x] * u[x], 1))
        u = sweep(targets, weights, inverses, middle)
    for x in range(count):
        for y in range(2):
            out[y, x : x + 1] = u[x][HALO + y : HALO + y + 1]


def call(kernel, outs, *args, scratch=(), source=pltpu.VMEM, limit=40 << 20):
    return pl.pallas_call(
        kernel,
        out_shape=tuple(o if isinstance(o, jax.ShapeDtypeStruct) else jax.ShapeDtypeStruct(o, jnp.float32) for o in outs),
        in_specs=[pl.BlockSpec(memory_space=source)] * len(args),
        out_specs=tuple(pl.BlockSpec(memory_space=pltpu.VMEM) for _ in outs),
        scratch_shapes=[pltpu.VMEM(o, jnp.float32) if isinstance(o, tuple) else o for o in scratch],
        compiler_params=pltpu.CompilerParams(vmem_limit_bytes=limit),
    )(*args)


def on_device(
    pressure, saturation, lam_water, lam_oil, perm_x, perm_y, perm_z, pore_volume,
    perf_cell, perf_well, well_index, well_pressure,
):
    groups = lax.axis_size("gx")
    ny = pressure.shape[1]
    wells_each = well_pressure.shape[0]
    fields = (pressure, saturation, lam_water, lam_oil, perm_x, perm_y, perm_z, pore_volume)
    cell, well, index, bhp = (v.reshape(1, -1) for v in (perf_cell, perf_well, well_index, well_pressure))
    given = fields + (cell, well, index, bhp)
    up = [(i, i + 1) for i in range(groups - 1)]
    down = [(i + 1, i) for i in range(groups - 1)]
    pairs = [(i, i + 1 - 2 * (i % 2)) for i in range(groups)]
    box = (2, ny, LANES)

    packed, weight, top, bottom = call(
        functools.partial(pack_kernel, groups),
        [(groups, CHUNK, LANES), (2 * ny, LANES), (5, ny, LANES), (5, ny, LANES)],
        *(pltpu.with_memory_space_constraint(v, pltpu.HBM) for v in given),
        scratch=[pltpu.VMEM(v.shape, v.dtype) for v in given]
        + [(FIELDS, 2, ny + 2 * TILE, LANES), (groups, LANES), pltpu.SemaphoreType.DMA((len(given),))],
        source=pltpu.HBM,
    )
    received = lax.all_to_all(packed, "gx", split_axis=0, concat_axis=0, tiled=True)
    from_below = lax.ppermute(top, "gx", up)
    from_above = lax.ppermute(bottom, "gx", down)
    (partial,) = call(sat_kernel, [box], *fields, weight, from_below, from_above)

    count = 2 * groups
    own, send, well_rows = call(
        face_kernel,
        [(5, count * TILE, LANES), (5 * count // 2 * TILE, LANES), (groups, LANES)],
        received.reshape(groups * CHUNK, LANES),
        partial,
    )
    other = lax.ppermute(send, "gx", pairs)
    grad_sat, grad_bhp = call(
        well_kernel, [box, (1, wells_each)],
        partial, saturation, lam_water, lam_oil, cell, well, index, well_rows,
    )
    (columns,) = call(functools.partial(sweep_kernel, SWEEPS), [(2, count, LANES)], own, other)
    return grad_sat, grad_bhp.reshape(wells_each), jnp.transpose(columns, (0, 2, 1))


def solution(mesh):
    cells = P(("members", "gx"), None, None)
    line = P(("members", "gx"))
    return jax.shard_map(
        on_device,
        mesh=mesh,
        in_specs=(cells,) * 8 + (line,) * 4,
        out_specs=(cells, line, cells),
        check_vma=False,
    )
```

profile of v0, /device:TPU:17, one launch (start us, length us, event | category | flops | bytes accessed | tf_op | source)
XLA Modules:
  0.0 30.7 jit_solution(3967502756021201828)
XLA Ops:
  0.6 2.4 %shard_map.139 = (f32[16,80,128]{2,1,0:T(8,128)}, f32[64,128]{1,0:T(8,128)S(1)}, f32[5,32,128]{2,1,0:T(8,128)S(1)}, f32[5,32,128]{2,1,0:T(8,128)S(1)}) custom-call(f32[2,32,128]{2,1,0:T(8,128)} %press.1, f32[2,32,128]{2,1,0:T(8,128)} %sat.3, f32[2,32,128]{2,1,0:T(8,128)} %lamw.3, f32[2,32,128]{2,1,0:T(8,128)} %lamo.3, f32[2,32,128]{2,1,0:T(8,128)} %permx.1, ...), custom_call_target="tpu_custom_call" | custom-call | tf_op jit(solution)/shard_map/pallas_call | solution.py:323
  3.0 0.0 copy-start
  3.0 0.0 copy-start.1
  3.0 0.0 copy-start.2
  3.0 0.0 copy-start.3
  3.0 0.0 copy-start.4
  3.0 0.0 copy-start.5
  3.1 0.0 copy-start.6
  3.1 0.0 copy-start.7
  3.1 6.6 %all-to-all-start = ((f32[16,80,128]{2,1,0:T(8,128)}), f32[16,80,128]{2,1,0:T(8,128)S(1)}, u32[]{:S(2)}, u32[]{:S(2)}) async-start(f32[16,80,128]{2,1,0:T(8,128)} %get-tuple-element.15), calls=%async_computation | async-start | bytes 1310720 | tf_op jit(solution)/shard_map/all_to_all | solution.py:356
  9.7 3.3 %collective-permute-start = (f32[5,32,128]{2,1,0:T(8,128)S(1)}, f32[5,32,128]{2,1,0:T(8,128)S(1)}, u32[]{:S(2)}, u32[]{:S(2)}) collective-permute-start(f32[5,32,128]{2,1,0:T(8,128)S(1)} %get-tuple-element.13), channel_id=1, source_target_pairs={{0,1},{1,2},{2,3},{3,4},{4,5},{5,6},{6,7},{7,8},{8,9},{9,10},{10,1... | collective-permute-start | bytes 245768 | tf_op jit(solution)/shard_map/ppermute | solution.py:357
  13.0 1.9 %collective-permute-start.1 = (f32[5,32,128]{2,1,0:T(8,128)S(1)}, f32[5,32,128]{2,1,0:T(8,128)S(1)}, u32[]{:S(2)}, u32[]{:S(2)}) collective-permute-start(f32[5,32,128]{2,1,0:T(8,128)S(1)} %get-tuple-element.14), channel_id=1, source_target_pairs={{1,0},{2,1},{3,2},{4,3},{5,4},{6,5},{7,6},{8,7},{9,8},{10,9},{11,1... | collective-permute-start | bytes 245768 | tf_op jit(solution)/shard_map/ppermute | solution.py:358
  15.0 0.0 collective-permute-done.from_below
  15.0 5.1 %collective-permute-done.1.from_above = f32[5,32,128]{2,1,0:T(8,128)S(1)} collective-permute-done((f32[5,32,128]{2,1,0:T(8,128)S(1)}, f32[5,32,128]{2,1,0:T(8,128)S(1)}, u32[]{:S(2)}, u32[]{:S(2)}) %collective-permute-start.1) | collective-permute-done | bytes 81952 | tf_op jit(solution)/shard_map/ppermute | solution.py:358
  20.1 0.0 copy-done
  20.1 0.0 copy-done.1
  20.1 0.0 copy-done.2
  20.1 0.0 copy-done.3
  20.1 0.0 copy-done.4
  20.1 0.0 copy-done.5
  20.1 0.0 copy-done.6
  20.1 0.0 copy-done.7
  20.1 0.2 shard_map.140._.partial
  20.3 5.3 %all-to-all-done = f32[16,80,128]{2,1,0:T(8,128)S(1)} async-done(((f32[16,80,128]{2,1,0:T(8,128)}), f32[16,80,128]{2,1,0:T(8,128)S(1)}, u32[]{:S(2)}, u32[]{:S(2)}) %all-to-all-start) | async-done | bytes 655392 | tf_op jit(solution)/shard_map/all_to_all | solution.py:356
  25.6 0.1 shard_map.141
  25.8 0.0 copy-start.9
  25.8 0.0 copy-start.10
  25.8 0.0 copy-start.8
  25.8 2.4 %collective-permute-start.2 = (f32[640,128]{1,0:T(8,128)S(1)}, f32[640,128]{1,0:T(8,128)S(1)}, u32[]{:S(2)}, u32[]{:S(2)}) collective-permute-start(f32[640,128]{1,0:T(8,128)S(1)} %get-tuple-element.20), channel_id=1, source_target_pairs={{0,1},{1,0},{2,3},{3,2},{4,5},{5,4},{6,7},{7,6},{8,9},{9,8},{10,11... | collective-permute-start | bytes 983048 | tf_op jit(solution)/shard_map/ppermute | solution.py:368
  28.2 0.0 copy-done.9
  28.2 0.0 copy-done.10
  28.2 0.0 copy-done.8
  28.2 1.0 %shard_map.142 = (f32[2,32,128]{2,1,0:T(8,128)}, f32[1,16]{1,0:T(1,128)}) custom-call(f32[2,32,128]{2,1,0:T(8,128)S(1)} %shard_map.140._.partial, f32[2,32,128]{2,1,0:T(8,128)S(1)} %copy-done, f32[2,32,128]{2,1,0:T(8,128)S(1)} %copy-done.1, f32[2,32,128]{2,1,0:T(8,128)S(1)} %copy-done.2, s32[1,256]{1,0:T(1,128)S(1)} %bitcast.9, s32[1,256]{1,0:T(1,128)S(1)} %bitcast.11, ...), custom_call_target="tpu_custom_call" | custom-call | tf_op jit(solution)/shard_map/pallas_call | solution.py:323
  29.1 0.3 collective-permute-done.2.other
  29.4 1.3 %shard_map.143 = f32[2,32,128]{2,1,0:T(8,128)} custom-call(f32[5,256,128]{2,1,0:T(8,128)S(1)} %get-tuple-element.19.own, f32[640,128]{1,0:T(8,128)S(1)} %collective-permute-done.2.other), custom_call_target="tpu_custom_call" | custom-call | tf_op jit(solution)/shard_map/pallas_call | solution.py:323
Async XLA Ops:
  3.0 17.1 %copy-start = (f32[2,32,128]{2,1,0:T(8,128)S(1)}, f32[2,32,128]{2,1,0:T(8,128)}, u32[]{:S(2)}) copy-start(f32[2,32,128]{2,1,0:T(8,128)} %sat.3) | copy-start | bytes 98308
  3.0 17.1 %copy-start.1 = (f32[2,32,128]{2,1,0:T(8,128)S(1)}, f32[2,32,128]{2,1,0:T(8,128)}, u32[]{:S(2)}) copy-start(f32[2,32,128]{2,1,0:T(8,128)} %lamw.3) | copy-start | bytes 98308
  3.0 17.1 %copy-start.2 = (f32[2,32,128]{2,1,0:T(8,128)S(1)}, f32[2,32,128]{2,1,0:T(8,128)}, u32[]{:S(2)}) copy-start(f32[2,32,128]{2,1,0:T(8,128)} %lamo.3) | copy-start | bytes 98308
  3.0 17.1 %copy-start.3 = (f32[2,32,128]{2,1,0:T(8,128)S(1)}, f32[2,32,128]{2,1,0:T(8,128)}, u32[]{:S(2)}) copy-start(f32[2,32,128]{2,1,0:T(8,128)} %press.1) | copy-start | bytes 98308
  3.0 17.1 %copy-start.4 = (f32[2,32,128]{2,1,0:T(8,128)S(1)}, f32[2,32,128]{2,1,0:T(8,128)}, u32[]{:S(2)}) copy-start(f32[2,32,128]{2,1,0:T(8,128)} %permx.1) | copy-start | bytes 98308
  3.0 17.1 %copy-start.5 = (f32[2,32,128]{2,1,0:T(8,128)S(1)}, f32[2,32,128]{2,1,0:T(8,128)}, u32[]{:S(2)}) copy-start(f32[2,32,128]{2,1,0:T(8,128)} %permy.1) | copy-start | bytes 98308
  3.1 17.1 %copy-start.6 = (f32[2,32,128]{2,1,0:T(8,128)S(1)}, f32[2,32,128]{2,1,0:T(8,128)}, u32[]{:S(2)}) copy-start(f32[2,32,128]{2,1,0:T(8,128)} %permz.1) | copy-start | bytes 98308
  3.1 17.1 %copy-start.7 = (f32[2,32,128]{2,1,0:T(8,128)S(1)}, f32[2,32,128]{2,1,0:T(8,128)}, u32[]{:S(2)}) copy-start(f32[2,32,128]{2,1,0:T(8,128)} %pore.1) | copy-start | bytes 98308
  3.1 22.5 %all-to-all-start = ((f32[16,80,128]{2,1,0:T(8,128)}), f32[16,80,128]{2,1,0:T(8,128)S(1)}, u32[]{:S(2)}, u32[]{:S(2)}) async-start(f32[16,80,128]{2,1,0:T(8,128)} %get-tuple-element.15), calls=%async_computation | async-start | bytes 1310720 | tf_op jit(solution)/shard_map/all_to_all | solution.py:356
  9.7 5.3 %collective-permute-start = (f32[5,32,128]{2,1,0:T(8,128)S(1)}, f32[5,32,128]{2,1,0:T(8,128)S(1)}, u32[]{:S(2)}, u32[]{:S(2)}) collective-permute-start(f32[5,32,128]{2,1,0:T(8,128)S(1)} %get-tuple-element.13), channel_id=1, source_target_pairs={{0,1},{1,2},{2,3},{3,4},{4,5},{5,6},{6,7},{7,8},{8,9},{9,10},{10,1... | collective-permute-start | bytes 245768 | tf_op jit(solution)/shard_map/ppermute | solution.py:357
  13.0 7.1 %collective-permute-start.1 = (f32[5,32,128]{2,1,0:T(8,128)S(1)}, f32[5,32,128]{2,1,0:T(8,128)S(1)}, u32[]{:S(2)}, u32[]{:S(2)}) collective-permute-start(f32[5,32,128]{2,1,0:T(8,128)S(1)} %get-tuple-element.14), channel_id=1, source_target_pairs={{1,0},{2,1},{3,2},{4,3},{5,4},{6,5},{7,6},{8,7},{9,8},{10,9},{11,1... | collective-permute-start | bytes 245768 | tf_op jit(solution)/shard_map/ppermute | solution.py:358
  25.8 2.4 %copy-start.9 = (s32[256]{0:T(256)S(1)}, s32[256]{0:T(256)}, u32[]{:S(2)}) copy-start(s32[256]{0:T(256)} %param.21) | copy-start | bytes 3076
  25.8 2.4 %copy-start.10 = (f32[256]{0:T(256)S(1)}, f32[256]{0:T(256)}, u32[]{:S(2)}) copy-start(f32[256]{0:T(256)} %param.22) | copy-start | bytes 3076
  25.8 2.4 %copy-start.8 = (s32[256]{0:T(256)S(1)}, s32[256]{0:T(256)}, u32[]{:S(2)}) copy-start(s32[256]{0:T(256)} %param.20) | copy-start | bytes 3076
  25.8 3.6 %collective-permute-start.2 = (f32[640,128]{1,0:T(8,128)S(1)}, f32[640,128]{1,0:T(8,128)S(1)}, u32[]{:S(2)}, u32[]{:S(2)}) collective-permute-start(f32[640,128]{1,0:T(8,128)S(1)} %get-tuple-element.20), channel_id=1, source_target_pairs={{0,1},{1,0},{2,3},{3,2},{4,5},{5,4},{6,7},{7,6},{8,9},{9,8},{10,11... | collective-permute-start | bytes 983048 | tf_op jit(solution)/shard_map/ppermute | solution.py:368
where the time goes:
time: 31.1 us; the launch traced here: 30.7 us
  starting transfers between devices  14.2 us (46%)
  waiting for transfers between devices  10.7 us (34%)
  Pallas kernels  4.9 us (16%)
  between operations  0.81 us (3%)
    all_to_all x1, starting transfers between devices, on_device(): lax.all_to_all(packed, 'gx', split_axis=0, concat_axis=0, tiled=True)  6.61 us
    all_to_all x1, waiting for transfers between devices, on_device(): lax.all_to_all(packed, 'gx', split_axis=0, concat_axis=0, tiled=True)  5.28 us
    ppermute x1, waiting for transfers between devices, on_device(): from_above = lax.ppermute(bottom, 'gx', down)  5.12 us
    pallas_call x5, Pallas kernels, call(): pl.pallas_call(kernel, out_shape=tuple((o if isinstance(o, jax.ShapeDtype...  4.9 us
    ppermute x1, starting transfers between devices, on_device(): from_below = lax.ppermute(top, 'gx', up)  3.33 us
    ppermute x1, starting transfers between devices, on_device(): other = lax.ppermute(send, 'gx', pairs)  2.38 us
    ppermute x1, starting transfers between devices, on_device(): from_above = lax.ppermute(bottom, 'gx', down)  1.92 us
  transfers between devices with their start and end apart: 4, of which 3 were waited for; matrix products, arithmetic and copies ran while one was open for 0% of the time, Pallas kernels for 4%

commit v1 on v0

--- a/solution.py
+++ b/solution.py
@@ -80,8 +80,8 @@
 
 
 def pack_kernel(groups, *refs):
-    sources, (packed, weight, above, below) = refs[:12], refs[12:16]
-    loaded, padded, well_rows, sems = refs[16:28], refs[28], refs[29], refs[30]
+    sources, loaded, (packed, weight, above, below) = refs[:12], refs[12:24], refs[24:28]
+    padded, well_rows, sems = refs[28:]
     copies = [pltpu.make_async_copy(src, dst, sems.at[i]) for i, (src, dst) in enumerate(zip(sources, loaded))]
     for i in (8, 10, 9, 11, 1, 2, 3, 5, 6, 7, 4, 0):
         copies[i].start()
@@ -119,7 +119,7 @@
             padded[field, x, :TILE] = edge
             padded[field, x, TILE : TILE + ny] = value
             padded[field, x, TILE + ny :] = edge
-    for member, field in enumerate((press, sat, lamw, lamo, permx)):
+    for member, field in enumerate((press, lamw, lamo, permx)):
         above[member] = field[1]
         below[member] = field[0]
 
@@ -154,29 +154,24 @@
         lax.fori_loop(0, groups // 2, chip, 0)
 
 
-def sat_kernel(press, sat, lamw, lamo, permx, permy, permz, pore, weight, from_below, from_above, out):
+def sat_parts(here, there, trans):
+    p, lw, lo = here
+    pn, lwn, lon = there
+    t = trans * (p - pn)
+    return t * (lw - lwn), t * (lo - lon)
+
+
+def sat_kernel(press, sat, lamw, lamo, permx, permy, permz, pore, weight, out):
     ny = sat.shape[1]
-
-    def parts(here, there, trans):
-        p, lw, lo = here
-        pn, lwn, lon = there
-        t = trans * (p - pn)
-        return t * (lw - lwn), t * (lo - lon)
-
     layers = [tuple(r[x] for r in (press, lamw, lamo)) for x in range(2)]
-    ends = [tuple(r[m] for m in (0, 2, 3)) for r in (from_below, from_above)]
-    chain = (ends[0], *layers, ends[1])
-    perms = (from_below[4], permx[0], permx[1], from_above[4])
-    across = []
-    for i in range(3):
-        k, kn = perms[i], perms[i + 1]
-        across.append(parts(chain[i], chain[i + 1], k * kn / (k + kn)))
+    k, kn = permx[0], permx[1]
+    inner = sat_parts(layers[0], layers[1], k * kn / (k + kn))
     for x in range(2):
         p, lw, lo = layers[x]
-        water, oil = (a + b for a, b in zip(across[x], across[x + 1]))
+        water, oil = inner
         for k, axis in ((permy[x], 0), (permz[x], 1)):
             there = tuple(upper(f, axis) for f in layers[x])
-            a, b = parts(layers[x], there, 0.5 * transmissibility(k, axis))
+            a, b = sat_parts(layers[x], there, 0.5 * transmissibility(k, axis))
             water = water + a + lower(a, axis)
             oil = oil + b + lower(b, axis)
         dw, do = slopes(sat[x])
@@ -202,6 +197,15 @@
         out[x] = partial[x] - (dw * lamw[x] + do * lamo[x]) * drop[x * ny : (x + 1) * ny]
     total = -jnp.sum(rows, axis=0, keepdims=True)
     grad_bhp[...] = total[:, wells_each : 2 * wells_each]
+
+
+def outer_kernel(partial, press, sat, lamw, lamo, permx, from_below, from_above, _, out):
+    for x, end in enumerate((from_below, from_above)):
+        k, kn = permx[x], end[3]
+        there = tuple(end[m] for m in range(3))
+        water, oil = sat_parts((press[x], lamw[x], lamo[x]), there, k * kn / (k + kn))
+        dw, do = slopes(sat[x])
+        out[x] = partial[x] + dw * water + do * oil
 
 
 def swap(x):
@@ -319,11 +323,13 @@
             out[y, x : x + 1] = u[x][HALO + y : HALO + y + 1]
 
 
-def call(kernel, outs, *args, scratch=(), source=pltpu.VMEM, limit=40 << 20):
+def call(kernel, outs, *args, scratch=(), in_hbm=0, limit=40 << 20):
+    places = [pltpu.VMEM] * (len(args) - in_hbm) + [pltpu.HBM] * in_hbm
+    args = [pltpu.with_memory_space_constraint(v, place) if place == pltpu.HBM else v for v, place in zip(args, places)]
     return pl.pallas_call(
         kernel,
         out_shape=tuple(o if isinstance(o, jax.ShapeDtypeStruct) else jax.ShapeDtypeStruct(o, jnp.float32) for o in outs),
-        in_specs=[pl.BlockSpec(memory_space=source)] * len(args),
+        in_specs=[pl.BlockSpec(memory_space=place) for place in places],
         out_specs=tuple(pl.BlockSpec(memory_space=pltpu.VMEM) for _ in outs),
         scratch_shapes=[pltpu.VMEM(o, jnp.float32) if isinstance(o, tuple) else o for o in scratch],
         compiler_params=pltpu.CompilerParams(vmem_limit_bytes=limit),
@@ -345,18 +351,19 @@
     pairs = [(i, i + 1 - 2 * (i % 2)) for i in range(groups)]
     box = (2, ny, LANES)
 
-    packed, weight, top, bottom = call(
+    *loaded, packed, weight, top, bottom = call(
         functools.partial(pack_kernel, groups),
-        [(groups, CHUNK, LANES), (2 * ny, LANES), (5, ny, LANES), (5, ny, LANES)],
-        *(pltpu.with_memory_space_constraint(v, pltpu.HBM) for v in given),
-        scratch=[pltpu.VMEM(v.shape, v.dtype) for v in given]
-        + [(FIELDS, 2, ny + 2 * TILE, LANES), (groups, LANES), pltpu.SemaphoreType.DMA((len(given),))],
-        source=pltpu.HBM,
-    )
+        [jax.ShapeDtypeStruct(v.shape, v.dtype) for v in given]
+        + [(groups, CHUNK, LANES), (2 * ny, LANES), (4, ny, LANES), (4, ny, LANES)],
+        *given,
+        scratch=[(FIELDS, 2, ny + 2 * TILE, LANES), (groups, LANES), pltpu.SemaphoreType.DMA((len(given),))],
+        in_hbm=len(given),
+    )
+    press, sat, lamw, lamo, permx, permy, permz, pore, cell, well, index, _ = loaded
     received = lax.all_to_all(packed, "gx", split_axis=0, concat_axis=0, tiled=True)
     from_below = lax.ppermute(top, "gx", up)
     from_above = lax.ppermute(bottom, "gx", down)
-    (partial,) = call(sat_kernel, [box], *fields, weight, from_below, from_above)
+    (partial,) = call(sat_kernel, [box], press, sat, lamw, lamo, permx, permy, permz, pore, weight)
 
     count = 2 * groups
     own, send, well_rows = call(
@@ -366,11 +373,13 @@
         partial,
     )
     other = lax.ppermute(send, "gx", pairs)
-    grad_sat, grad_bhp = call(
-        well_kernel, [box, (1, wells_each)],
-        partial, saturation, lam_water, lam_oil, cell, well, index, well_rows,
+    partial, grad_bhp = call(
+        well_kernel, [box, (1, wells_each)], partial, sat, lamw, lamo, cell, well, index, well_rows
     )
     (columns,) = call(functools.partial(sweep_kernel, SWEEPS), [(2, count, LANES)], own, other)
+    (grad_sat,) = call(
+        outer_kernel, [box], partial, press, sat, lamw, lamo, permx, from_below, from_above, columns, in_hbm=1
+    )
     return grad_sat, grad_bhp.reshape(wells_each), jnp.transpose(columns, (0, 2, 1))
 
 

time: 31.1 us -> 37.7 us (1.21)
  the two profiles are of different devices: /device:TPU:17 before, /device:TPU:3 now
where the time goes in v1:
time: 37.7 us; the launch traced here: 37.4 us
  waiting for transfers between devices  18.4 us (49%)
  starting transfers between devices  13 us (34%)
  Pallas kernels  5.29 us (14%)
  between operations  0.68 us (2%)
    all_to_all x1, waiting for transfers between devices, on_device(): lax.all_to_all(packed, 'gx', split_axis=0, concat_axis=0, tiled=True)  15.9 us
    all_to_all x1, starting transfers between devices, on_device(): lax.all_to_all(packed, 'gx', split_axis=0, concat_axis=0, tiled=True)  6.68 us
    pallas_call x6, Pallas kernels, call(): pl.pallas_call(kernel, out_shape=tuple((o if isinstance(o, jax.ShapeDtype...  5.29 us
    ppermute x1, starting transfers between devices, on_device(): from_below = lax.ppermute(top, 'gx', up)  4.31 us
    ppermute x1, waiting for transfers between devices, on_device(): from_above = lax.ppermute(bottom, 'gx', down)  2.58 us
    ppermute x1, starting transfers between devices, on_device(): from_above = lax.ppermute(bottom, 'gx', down)  1.92 us
  transfers between devices with their start and end apart: 4, of which 2 were waited for; matrix products, arithmetic and copies ran while one was open for 0% of the time, Pallas kernels for 6%

profile of v1, /device:TPU:3, one launch (start us, length us, event | category | flops | bytes accessed | tf_op | source)
XLA Modules:
  0.0 37.4 jit_solution(16376130896642687440)
XLA Ops:
  0.6 2.4 %shard_map.139 = (f32[2,32,128]{2,1,0:T(8,128)S(1)}, f32[2,32,128]{2,1,0:T(8,128)S(1)}, f32[2,32,128]{2,1,0:T(8,128)S(1)}, f32[2,32,128]{2,1,0:T(8,128)S(1)}, f3...) custom-call(f32[2,32,128]{2,1,0:T(8,128)} %refs_0_.1, ...), custom_call_target="tpu_custom_call" | custom-call | tf_op jit(solution)/shard_map/pallas_call | solution.py:329
  3.0 6.7 %all-to-all-start = ((f32[16,80,128]{2,1,0:T(8,128)}), f32[16,80,128]{2,1,0:T(8,128)S(1)}, u32[]{:S(2)}, u32[]{:S(2)}) async-start(f32[16,80,128]{2,1,0:T(8,128)} %get-tuple-element.35), calls=%async_computation | async-start | bytes 1310720 | tf_op jit(solution)/shard_map/all_to_all | solution.py:363
  9.7 0.2 shard_map.140._.partial
  9.9 15.9 %all-to-all-done = f32[16,80,128]{2,1,0:T(8,128)S(1)} async-done(((f32[16,80,128]{2,1,0:T(8,128)}), f32[16,80,128]{2,1,0:T(8,128)S(1)}, u32[]{:S(2)}, u32[]{:S(2)}) %all-to-all-start) | async-done | bytes 655392 | tf_op jit(solution)/shard_map/all_to_all | solution.py:363
  25.7 0.1 shard_map.141
  25.9 0.1 collective-permute-start.2
  26.0 4.3 %collective-permute-start = (f32[4,32,128]{2,1,0:T(8,128)S(1)}, f32[4,32,128]{2,1,0:T(8,128)S(1)}, u32[]{:S(2)}, u32[]{:S(2)}) collective-permute-start(f32[4,32,128]{2,1,0:T(8,128)S(1)} %get-tuple-element.38), channel_id=1, source_target_pairs={{0,1},{1,2},{2,3},{3,4},{4,5},{5,6},{6,7},{7,8},{8,9},{9,10},{10,1... | collective-permute-start | bytes 196616 | tf_op jit(solution)/shard_map/ppermute | solution.py:364
  30.3 1.9 %collective-permute-start.1 = (f32[4,32,128]{2,1,0:T(8,128)S(1)}, f32[4,32,128]{2,1,0:T(8,128)S(1)}, u32[]{:S(2)}, u32[]{:S(2)}) collective-permute-start(f32[4,32,128]{2,1,0:T(8,128)S(1)} %get-tuple-element.39), channel_id=1, source_target_pairs={{1,0},{2,1},{3,2},{4,3},{5,4},{6,5},{7,6},{8,7},{9,8},{10,9},{11,1... | collective-permute-start | bytes 196616 | tf_op jit(solution)/shard_map/ppermute | solution.py:365
  32.2 0.7 %shard_map.142 = (f32[2,32,128]{2,1,0:T(8,128)S(1)}, f32[1,16]{1,0:T(1,128)}) custom-call(f32[2,32,128]{2,1,0:T(8,128)S(1)} %shard_map.140._.partial, f32[2,32,128]{2,1,0:T(8,128)S(1)} %get-tuple-element.24.sat, f32[2,32,128]{2,1,0:T(8,128)S(1)} %get-tuple-element.25.lamw, f32[2,32,128]{2,1,0:T(8,128)S(1)} %get-tuple-element.26.lamo, ...), custom_call_target="tpu_custom_call" | custom-call | tf_op jit(solution)/shard_map/pallas_call | solution.py:329
  32.9 0.0 collective-permute-done.2.other
  32.9 1.3 %shard_map.143._ = f32[2,32,128]{2,1,0:T(8,128)} custom-call(f32[5,256,128]{2,1,0:T(8,128)S(1)} %get-tuple-element.40.own, f32[640,128]{1,0:T(8,128)S(1)} %collective-permute-done.2.other), custom_call_target="tpu_custom_call" | custom-call | tf_op jit(solution)/shard_map/pallas_call | solution.py:329
  34.2 0.0 collective-permute-done.from_below
  34.2 2.6 %collective-permute-done.1.from_above = f32[4,32,128]{2,1,0:T(8,128)S(1)} collective-permute-done((f32[4,32,128]{2,1,0:T(8,128)S(1)}, f32[4,32,128]{2,1,0:T(8,128)S(1)}, u32[]{:S(2)}, u32[]{:S(2)}) %collective-permute-start.1) | collective-permute-done | bytes 65568 | tf_op jit(solution)/shard_map/ppermute | solution.py:365
  36.7 0.6 %shard_map.144 = f32[2,32,128]{2,1,0:T(8,128)} custom-call(f32[2,32,128]{2,1,0:T(8,128)S(1)} %get-tuple-element.37.partial, f32[2,32,128]{2,1,0:T(8,128)S(1)} %get-tuple-element.23.press, f32[2,32,128]{2,1,0:T(8,128)S(1)} %get-tuple-element.24.sat, f32[2,32,128]{2,1,0:T(8,128)S(1)} %get-tuple-element.25.lamw, f32[2,32,128]{2,1,0:T(8,128)S(1)} %get-tuple-element.26.lamo, ...), custom_call_target="tpu_custom_call" | custom-call | tf_op jit(solution)/shard_map/pallas_call | solution.py:329
Async XLA Ops:
  3.0 22.7 %all-to-all-start = ((f32[16,80,128]{2,1,0:T(8,128)}), f32[16,80,128]{2,1,0:T(8,128)S(1)}, u32[]{:S(2)}, u32[]{:S(2)}) async-start(f32[16,80,128]{2,1,0:T(8,128)} %get-tuple-element.35), calls=%async_computation | async-start | bytes 1310720 | tf_op jit(solution)/shard_map/all_to_all | solution.py:363
  25.9 7.0 %collective-permute-start.2 = (f32[640,128]{1,0:T(8,128)S(1)}, f32[640,128]{1,0:T(8,128)S(1)}, u32[]{:S(2)}, u32[]{:S(2)}) collective-permute-start(f32[640,128]{1,0:T(8,128)S(1)} %get-tuple-element.41), channel_id=1, source_target_pairs={{0,1},{1,0},{2,3},{3,2},{4,5},{5,4},{6,7},{7,6},{8,9},{9,8},{10,11... | collective-permute-start | bytes 983048 | tf_op jit(solution)/shard_map/ppermute | solution.py:375
  26.0 8.2 %collective-permute-start = (f32[4,32,128]{2,1,0:T(8,128)S(1)}, f32[4,32,128]{2,1,0:T(8,128)S(1)}, u32[]{:S(2)}, u32[]{:S(2)}) collective-permute-start(f32[4,32,128]{2,1,0:T(8,128)S(1)} %get-tuple-element.38), channel_id=1, source_target_pairs={{0,1},{1,2},{2,3},{3,4},{4,5},{5,6},{6,7},{7,8},{8,9},{9,10},{10,1... | collective-permute-start | bytes 196616 | tf_op jit(solution)/shard_map/ppermute | solution.py:364
  30.3 6.5 %collective-permute-start.1 = (f32[4,32,128]{2,1,0:T(8,128)S(1)}, f32[4,32,128]{2,1,0:T(8,128)S(1)}, u32[]{:S(2)}, u32[]{:S(2)}) collective-permute-start(f32[4,32,128]{2,1,0:T(8,128)S(1)} %get-tuple-element.39), channel_id=1, source_target_pairs={{1,0},{2,1},{3,2},{4,3},{5,4},{6,5},{7,6},{8,7},{9,8},{10,9},{11,1... | collective-permute-start | bytes 196616 | tf_op jit(solution)/shard_map/ppermute | solution.py:365

commit v2 on v1

--- a/solution.py
+++ b/solution.py
@@ -179,7 +179,9 @@
         out[x] = pore[x] * (lw - lo) + dw * (water + well * lw) + do * (oil + well * lo)
 
 
-def well_kernel(partial, sat, lamw, lamo, cell, well, index, well_rows, out, grad_bhp):
+def well_kernel(
+    partial, press, sat, lamw, lamo, permx, cell, well, index, well_rows, from_below, from_above, out, grad_bhp
+):
     ny = sat.shape[1]
     groups = well_rows.shape[0]
     wells_each = grad_bhp.shape[1]
@@ -192,20 +194,15 @@
     pressure = jnp.sum(by_owner * owners, axis=0, keepdims=True)
     cells = cell[...]
     drop = scatter_cells(index[...] * pressure, marks(cells // LANES, 2 * ny), marks(cells % LANES, LANES))
-    for x in range(2):
+    for x, end in enumerate((from_below, from_above)):
+        k, kn = permx[x], end[3]
+        lw, lo = lamw[x], lamo[x]
+        water, oil = sat_parts((press[x], lw, lo), tuple(end[m] for m in range(3)), k * kn / (k + kn))
         dw, do = slopes(sat[x])
-        out[x] = partial[x] - (dw * lamw[x] + do * lamo[x]) * drop[x * ny : (x + 1) * ny]
+        well = drop[x * ny : (x + 1) * ny]
+        out[x] = partial[x] + dw * (water - well * lw) + do * (oil - well * lo)
     total = -jnp.sum(rows, axis=0, keepdims=True)
     grad_bhp[...] = total[:, wells_each : 2 * wells_each]
-
-
-def outer_kernel(partial, press, sat, lamw, lamo, permx, from_below, from_above, _, out):
-    for x, end in enumerate((from_below, from_above)):
-        k, kn = permx[x], end[3]
-        there = tuple(end[m] for m in range(3))
-        water, oil = sat_parts((press[x], lamw[x], lamo[x]), there, k * kn / (k + kn))
-        dw, do = slopes(sat[x])
-        out[x] = partial[x] + dw * water + do * oil
 
 
 def swap(x):
@@ -323,7 +320,7 @@
             out[y, x : x + 1] = u[x][HALO + y : HALO + y + 1]
 
 
-def call(kernel, outs, *args, scratch=(), in_hbm=0, limit=40 << 20):
+def call(kernel, outs, *args, scratch=(), in_hbm=0):
     places = [pltpu.VMEM] * (len(args) - in_hbm) + [pltpu.HBM] * in_hbm
     args = [pltpu.with_memory_space_constraint(v, place) if place == pltpu.HBM else v for v, place in zip(args, places)]
     return pl.pallas_call(
@@ -332,7 +329,7 @@
         in_specs=[pl.BlockSpec(memory_space=place) for place in places],
         out_specs=tuple(pl.BlockSpec(memory_space=pltpu.VMEM) for _ in outs),
         scratch_shapes=[pltpu.VMEM(o, jnp.float32) if isinstance(o, tuple) else o for o in scratch],
-        compiler_params=pltpu.CompilerParams(vmem_limit_bytes=limit),
+        compiler_params=pltpu.CompilerParams(vmem_limit_bytes=40 << 20),
     )(*args)
 
 
@@ -373,13 +370,11 @@
         partial,
     )
     other = lax.ppermute(send, "gx", pairs)
-    partial, grad_bhp = call(
-        well_kernel, [box, (1, wells_each)], partial, sat, lamw, lamo, cell, well, index, well_rows
+    grad_sat, grad_bhp = call(
+        well_kernel, [box, (1, wells_each)],
+        partial, press, sat, lamw, lamo, permx, cell, well, index, well_rows, from_below, from_above,
     )
     (columns,) = call(functools.partial(sweep_kernel, SWEEPS), [(2, count, LANES)], own, other)
-    (grad_sat,) = call(
-        outer_kernel, [box], partial, press, sat, lamw, lamo, permx, from_below, from_above, columns, in_hbm=1
-    )
     return grad_sat, grad_bhp.reshape(wells_each), jnp.transpose(columns, (0, 2, 1))
 
 

time: 37.7 us -> 39.3 us (1.042)
  waiting for transfers between devices: 18.4 us -> 20.4 us
    ppermute x1, waiting for transfers between devices: 2.58 us -> 4.54 us  [on_device(): from_above = lax.ppermute(bottom, 'gx', down)]
    pallas_call x6 -> x5, Pallas kernels: 5.29 us -> 4.9 us  [call(): pl.pallas_call(kernel, out_shape=tuple((o if isinstance(o, jax.ShapeDtype...]
  transfers between devices with their start and end apart: 4 -> 4, of which waited for: 2 -> 2; matrix products, arithmetic and copies ran while one was open for 0% -> 0% of each run, Pallas kernels for 6% -> 3%
where the time goes in v2:
time: 39.3 us; the launch traced here: 39 us
  waiting for transfers between devices  20.4 us (52%)
  starting transfers between devices  13 us (33%)
  Pallas kernels  4.9 us (12%)
  between operations  0.69 us (2%)
    all_to_all x1, waiting for transfers between devices, on_device(): lax.all_to_all(packed, 'gx', split_axis=0, concat_axis=0, tiled=True)  15.9 us
    all_to_all x1, starting transfers between devices, on_device(): lax.all_to_all(packed, 'gx', split_axis=0, concat_axis=0, tiled=True)  6.68 us
    pallas_call x5, Pallas kernels, call(): pl.pallas_call(kernel, out_shape=tuple((o if isinstance(o, jax.ShapeDtype...  4.9 us
    ppermute x1, waiting for transfers between devices, on_device(): from_above = lax.ppermute(bottom, 'gx', down)  4.54 us
    ppermute x1, starting transfers between devices, on_device(): from_below = lax.ppermute(top, 'gx', up)  4.31 us
    ppermute x1, starting transfers between devices, on_device(): from_above = lax.ppermute(bottom, 'gx', down)  1.92 us
  transfers between devices with their start and end apart: 4, of which 2 were waited for; matrix products, arithmetic and copies ran while one was open for 0% of the time, Pallas kernels for 3%

profile of v2, /device:TPU:3, one launch (start us, length us, event | category | flops | bytes accessed | tf_op | source)
XLA Modules:
  0.0 39.0 jit_solution(1550764703346664518)
XLA Ops:
  0.6 2.4 %shard_map.139 = (f32[2,32,128]{2,1,0:T(8,128)S(1)}, f32[2,32,128]{2,1,0:T(8,128)S(1)}, f32[2,32,128]{2,1,0:T(8,128)S(1)}, f32[2,32,128]{2,1,0:T(8,128)S(1)}, f3...) custom-call(f32[2,32,128]{2,1,0:T(8,128)} %refs_0_.1, ...), custom_call_target="tpu_custom_call" | custom-call | tf_op jit(solution)/shard_map/pallas_call | solution.py:326
  3.0 6.7 %all-to-all-start = ((f32[16,80,128]{2,1,0:T(8,128)}), f32[16,80,128]{2,1,0:T(8,128)S(1)}, u32[]{:S(2)}, u32[]{:S(2)}) async-start(f32[16,80,128]{2,1,0:T(8,128)} %get-tuple-element.35), calls=%async_computation | async-start | bytes 1310720 | tf_op jit(solution)/shard_map/all_to_all | solution.py:360
  9.7 0.2 shard_map.140._.partial
  9.9 15.9 %all-to-all-done = f32[16,80,128]{2,1,0:T(8,128)S(1)} async-done(((f32[16,80,128]{2,1,0:T(8,128)}), f32[16,80,128]{2,1,0:T(8,128)S(1)}, u32[]{:S(2)}, u32[]{:S(2)}) %all-to-all-start) | async-done | bytes 655392 | tf_op jit(solution)/shard_map/all_to_all | solution.py:360
  25.7 0.1 shard_map.141
  25.9 0.1 collective-permute-start.2
  26.0 4.3 %collective-permute-start = (f32[4,32,128]{2,1,0:T(8,128)S(1)}, f32[4,32,128]{2,1,0:T(8,128)S(1)}, u32[]{:S(2)}, u32[]{:S(2)}) collective-permute-start(f32[4,32,128]{2,1,0:T(8,128)S(1)} %get-tuple-element.37), channel_id=1, source_target_pairs={{0,1},{1,2},{2,3},{3,4},{4,5},{5,6},{6,7},{7,8},{8,9},{9,10},{10,1... | collective-permute-start | bytes 196616 | tf_op jit(solution)/shard_map/ppermute | solution.py:361
  30.3 1.9 %collective-permute-start.1 = (f32[4,32,128]{2,1,0:T(8,128)S(1)}, f32[4,32,128]{2,1,0:T(8,128)S(1)}, u32[]{:S(2)}, u32[]{:S(2)}) collective-permute-start(f32[4,32,128]{2,1,0:T(8,128)S(1)} %get-tuple-element.38), channel_id=1, source_target_pairs={{1,0},{2,1},{3,2},{4,3},{5,4},{6,5},{7,6},{8,7},{9,8},{10,9},{11,1... | collective-permute-start | bytes 196616 | tf_op jit(solution)/shard_map/ppermute | solution.py:362
  32.2 0.0 collective-permute-done.from_below
  32.2 4.5 %collective-permute-done.1.from_above = f32[4,32,128]{2,1,0:T(8,128)S(1)} collective-permute-done((f32[4,32,128]{2,1,0:T(8,128)S(1)}, f32[4,32,128]{2,1,0:T(8,128)S(1)}, u32[]{:S(2)}, u32[]{:S(2)}) %collective-permute-start.1) | collective-permute-done | bytes 65568 | tf_op jit(solution)/shard_map/ppermute | solution.py:362
  36.7 1.0 %shard_map.142 = (f32[2,32,128]{2,1,0:T(8,128)}, f32[1,16]{1,0:T(1,128)}) custom-call(f32[2,32,128]{2,1,0:T(8,128)S(1)} %shard_map.140._.partial, f32[2,32,128]{2,1,0:T(8,128)S(1)} %get-tuple-element.23.press, f32[2,32,128]{2,1,0:T(8,128)S(1)} %get-tuple-element.24.sat, f32[2,32,128]{2,1,0:T(8,128)S(1)} %get-tuple-element.25.lamw, ...), custom_call_target="tpu_custom_call" | custom-call | tf_op jit(solution)/shard_map/pallas_call | solution.py:326
  37.7 0.0 collective-permute-done.2.other
  37.7 1.3 %shard_map.143 = f32[2,32,128]{2,1,0:T(8,128)} custom-call(f32[5,256,128]{2,1,0:T(8,128)S(1)} %get-tuple-element.41.own, f32[640,128]{1,0:T(8,128)S(1)} %collective-permute-done.2.other), custom_call_target="tpu_custom_call" | custom-call | tf_op jit(solution)/shard_map/pallas_call | solution.py:326
Async XLA Ops:
  3.0 22.7 %all-to-all-start = ((f32[16,80,128]{2,1,0:T(8,128)}), f32[16,80,128]{2,1,0:T(8,128)S(1)}, u32[]{:S(2)}, u32[]{:S(2)}) async-start(f32[16,80,128]{2,1,0:T(8,128)} %get-tuple-element.35), calls=%async_computation | async-start | bytes 1310720 | tf_op jit(solution)/shard_map/all_to_all | solution.py:360
  25.9 11.8 %collective-permute-start.2 = (f32[640,128]{1,0:T(8,128)S(1)}, f32[640,128]{1,0:T(8,128)S(1)}, u32[]{:S(2)}, u32[]{:S(2)}) collective-permute-start(f32[640,128]{1,0:T(8,128)S(1)} %get-tuple-element.42), channel_id=1, source_target_pairs={{0,1},{1,0},{2,3},{3,2},{4,5},{5,4},{6,7},{7,6},{8,9},{9,8},{10,11... | collective-permute-start | bytes 983048 | tf_op jit(solution)/shard_map/ppermute | solution.py:372
  26.0 6.2 %collective-permute-start = (f32[4,32,128]{2,1,0:T(8,128)S(1)}, f32[4,32,128]{2,1,0:T(8,128)S(1)}, u32[]{:S(2)}, u32[]{:S(2)}) collective-permute-start(f32[4,32,128]{2,1,0:T(8,128)S(1)} %get-tuple-element.37), channel_id=1, source_target_pairs={{0,1},{1,2},{2,3},{3,4},{4,5},{5,6},{6,7},{7,8},{8,9},{9,10},{10,1... | collective-permute-start | bytes 196616 | tf_op jit(solution)/shard_map/ppermute | solution.py:361
  30.3 6.5 %collective-permute-start.1 = (f32[4,32,128]{2,1,0:T(8,128)S(1)}, f32[4,32,128]{2,1,0:T(8,128)S(1)}, u32[]{:S(2)}, u32[]{:S(2)}) collective-permute-start(f32[4,32,128]{2,1,0:T(8,128)S(1)} %get-tuple-element.38), channel_id=1, source_target_pairs={{1,0},{2,1},{3,2},{4,3},{5,4},{6,5},{7,6},{8,7},{9,8},{10,9},{11,1... | collective-permute-start | bytes 196616 | tf_op jit(solution)/shard_map/ppermute | solution.py:362

commit v3 on v2

--- a/solution.py
+++ b/solution.py
@@ -57,6 +57,10 @@
     return add_thirds(dot(left, lane_marks.astype(jnp.bfloat16), ((1,), (1,))))
 
 
+def core():
+    return lax.axis_index("gx") % 2
+
+
 def upper(x, axis):
     return pltpu.roll(x, x.shape[axis] - 1, axis)
 
@@ -80,7 +84,7 @@
 
 
 def pack_kernel(groups, *refs):
-    sources, loaded, (packed, weight, above, below) = refs[:12], refs[12:24], refs[24:28]
+    sources, loaded, (packed, weight, chip_edge, outer_edge) = refs[:12], refs[12:24], refs[24:28]
     padded, well_rows, sems = refs[28:]
     copies = [pltpu.make_async_copy(src, dst, sems.at[i]) for i, (src, dst) in enumerate(zip(sources, loaded))]
     for i in (8, 10, 9, 11, 1, 2, 3, 5, 6, 7, 4, 0):
@@ -120,8 +124,8 @@
             padded[field, x, TILE : TILE + ny] = value
             padded[field, x, TILE + ny :] = edge
     for member, field in enumerate((press, lamw, lamo, permx)):
-        above[member] = field[1]
-        below[member] = field[0]
+        chip_edge[member] = field[1 - core()]
+        outer_edge[member] = field[core()]
 
     flow_parts = jnp.concatenate(split(jnp.concatenate(flows)))
     row_parts = jnp.concatenate([row_marks.astype(jnp.bfloat16)] * 3)
@@ -161,17 +165,24 @@
     return t * (lw - lwn), t * (lo - lon)
 
 
-def sat_kernel(press, sat, lamw, lamo, permx, permy, permz, pore, weight, out):
+def sat_kernel(press, sat, lamw, lamo, permx, permy, permz, pore, weight, from_chip, from_outside, out):
     ny = sat.shape[1]
-    layers = [tuple(r[x] for r in (press, lamw, lamo)) for x in range(2)]
-    k, kn = permx[0], permx[1]
-    inner = sat_parts(layers[0], layers[1], k * kn / (k + kn))
+    first = core() == 0
+    layers = [tuple(r[x] for r in (press, lamw, lamo, permx)) for x in range(2)]
+    ends = [tuple(r[m] for m in range(4)) for r in (from_outside, from_chip)]
+    below = tuple(jnp.where(first, a, b) for a, b in zip(*ends))
+    above = tuple(jnp.where(first, b, a) for a, b in zip(*ends))
+    chain = (below, *layers, above)
+    across = []
+    for here, there in zip(chain, chain[1:]):
+        k, kn = here[3], there[3]
+        across.append(sat_parts(here[:3], there[:3], k * kn / (k + kn)))
     for x in range(2):
-        p, lw, lo = layers[x]
-        water, oil = inner
+        p, lw, lo, _ = layers[x]
+        water, oil = (a + b for a, b in zip(across[x], across[x + 1]))
         for k, axis in ((permy[x], 0), (permz[x], 1)):
-            there = tuple(upper(f, axis) for f in layers[x])
-            a, b = sat_parts(layers[x], there, 0.5 * transmissibility(k, axis))
+            there = tuple(upper(f, axis) for f in (p, lw, lo))
+            a, b = sat_parts((p, lw, lo), there, 0.5 * transmissibility(k, axis))
             water = water + a + lower(a, axis)
             oil = oil + b + lower(b, axis)
         dw, do = slopes(sat[x])
@@ -179,9 +190,7 @@
         out[x] = pore[x] * (lw - lo) + dw * (water + well * lw) + do * (oil + well * lo)
 
 
-def well_kernel(
-    partial, press, sat, lamw, lamo, permx, cell, well, index, well_rows, from_below, from_above, out, grad_bhp
-):
+def well_kernel(partial, sat, lamw, lamo, cell, well, index, well_rows, out, grad_bhp):
     ny = sat.shape[1]
     groups = well_rows.shape[0]
     wells_each = grad_bhp.shape[1]
@@ -194,13 +203,9 @@
     pressure = jnp.sum(by_owner * owners, axis=0, keepdims=True)
     cells = cell[...]
     drop = scatter_cells(index[...] * pressure, marks(cells // LANES, 2 * ny), marks(cells % LANES, LANES))
-    for x, end in enumerate((from_below, from_above)):
-        k, kn = permx[x], end[3]
-        lw, lo = lamw[x], lamo[x]
-        water, oil = sat_parts((press[x], lw, lo), tuple(end[m] for m in range(3)), k * kn / (k + kn))
+    for x in range(2):
         dw, do = slopes(sat[x])
-        well = drop[x * ny : (x + 1) * ny]
-        out[x] = partial[x] + dw * (water - well * lw) + do * (oil - well * lo)
+        out[x] = partial[x] - (dw * lamw[x] + do * lamo[x]) * drop[x * ny : (x + 1) * ny]
     total = -jnp.sum(rows, axis=0, keepdims=True)
     grad_bhp[...] = total[:, wells_each : 2 * wells_each]
 
@@ -211,10 +216,6 @@
 
 def sublane():
     return lax.broadcasted_iota(jnp.int32, (TILE, LANES), 0)
-
-
-def core():
-    return lax.axis_index("gx") % 2
 
 
 def face_kernel(received, _, own, send, well_rows):
@@ -343,12 +344,11 @@
     fields = (pressure, saturation, lam_water, lam_oil, perm_x, perm_y, perm_z, pore_volume)
     cell, well, index, bhp = (v.reshape(1, -1) for v in (perf_cell, perf_well, well_index, well_pressure))
     given = fields + (cell, well, index, bhp)
-    up = [(i, i + 1) for i in range(groups - 1)]
-    down = [(i + 1, i) for i in range(groups - 1)]
-    pairs = [(i, i + 1 - 2 * (i % 2)) for i in range(groups)]
+    chip_pairs = [(i, i + 1 - 2 * (i % 2)) for i in range(groups)]
+    outer_pairs = [(i, i - 1 + 2 * (i % 2)) for i in range(1, groups - 1)]
     box = (2, ny, LANES)
 
-    *loaded, packed, weight, top, bottom = call(
+    *loaded, packed, weight, chip_edge, outer_edge = call(
         functools.partial(pack_kernel, groups),
         [jax.ShapeDtypeStruct(v.shape, v.dtype) for v in given]
         + [(groups, CHUNK, LANES), (2 * ny, LANES), (4, ny, LANES), (4, ny, LANES)],
@@ -358,9 +358,11 @@
     )
     press, sat, lamw, lamo, permx, permy, permz, pore, cell, well, index, _ = loaded
     received = lax.all_to_all(packed, "gx", split_axis=0, concat_axis=0, tiled=True)
-    from_below = lax.ppermute(top, "gx", up)
-    from_above = lax.ppermute(bottom, "gx", down)
-    (partial,) = call(sat_kernel, [box], press, sat, lamw, lamo, permx, permy, permz, pore, weight)
+    from_outside = lax.ppermute(outer_edge, "gx", outer_pairs)
+    from_chip = lax.ppermute(chip_edge, "gx", chip_pairs)
+    (partial,) = call(
+        sat_kernel, [box], press, sat, lamw, lamo, permx, permy, permz, pore, weight, from_chip, from_outside
+    )
 
     count = 2 * groups
     own, send, well_rows = call(
@@ -369,10 +371,9 @@
         received.reshape(groups * CHUNK, LANES),
         partial,
     )
-    other = lax.ppermute(send, "gx", pairs)
+    other = lax.ppermute(send, "gx", chip_pairs)
     grad_sat, grad_bhp = call(
-        well_kernel, [box, (1, wells_each)],
-        partial, press, sat, lamw, lamo, permx, cell, well, index, well_rows, from_below, from_above,
+        well_kernel, [box, (1, wells_each)], partial, sat, lamw, lamo, cell, well, index, well_rows
     )
     (columns,) = call(functools.partial(sweep_kernel, SWEEPS), [(2, count, LANES)], own, other)
     return grad_sat, grad_bhp.reshape(wells_each), jnp.transpose(columns, (0, 2, 1))

time: 39.3 us -> 30.5 us (0.78)
  the two profiles are of different devices: /device:TPU:3 before, /device:TPU:0 now
where the time goes in v3:
time: 30.5 us; the launch traced here: 30.1 us
  waiting for transfers between devices  15.9 us (52%)
  starting transfers between devices  8.57 us (28%)
  Pallas kernels  4.88 us (16%)
  between operations  0.68 us (2%)
    all_to_all x1, waiting for transfers between devices, on_device(): lax.all_to_all(packed, 'gx', split_axis=0, concat_axis=0, tiled=True)  15.1 us
    all_to_all x1, starting transfers between devices, on_device(): lax.all_to_all(packed, 'gx', split_axis=0, concat_axis=0, tiled=True)  7.37 us
    pallas_call x5, Pallas kernels, call(): pl.pallas_call(kernel, out_shape=tuple((o if isinstance(o, jax.ShapeDtype...  4.88 us
    ppermute x1, starting transfers between devices, on_device(): from_outside = lax.ppermute(outer_edge, 'gx', outer_pairs)  0.65 us
  transfers between devices with their start and end apart: 4, of which 3 were waited for; matrix products, arithmetic and copies ran while one was open for 0% of the time, Pallas kernels for 4%

profile of v3, /device:TPU:0, one launch (start us, length us, event | category | flops | bytes accessed | tf_op | source)
XLA Modules:
  0.0 30.1 jit_solution(15289036621365100772)
XLA Ops:
  0.6 2.3 %shard_map.139 = (f32[2,32,128]{2,1,0:T(8,128)S(1)}, f32[2,32,128]{2,1,0:T(8,128)S(1)}, f32[2,32,128]{2,1,0:T(8,128)S(1)}, f32[2,32,128]{2,1,0:T(8,128)S(1)}, f3...) custom-call(f32[2,32,128]{2,1,0:T(8,128)} %refs_0_.1, ...), custom_call_target="tpu_custom_call" | custom-call | tf_op jit(solution)/shard_map/pallas_call | solution.py:327
  3.0 7.4 %all-to-all-start = ((f32[16,80,128]{2,1,0:T(8,128)}), f32[16,80,128]{2,1,0:T(8,128)S(1)}, u32[]{:S(2)}, u32[]{:S(2)}) async-start(f32[16,80,128]{2,1,0:T(8,128)} %get-tuple-element.37), calls=%async_computation | async-start | bytes 1310720 | tf_op jit(solution)/shard_map/all_to_all | solution.py:360
  10.4 0.4 %collective-permute-start = (f32[4,32,128]{2,1,0:T(8,128)S(1)}, f32[4,32,128]{2,1,0:T(8,128)S(1)}, u32[]{:S(2)}, u32[]{:S(2)}) collective-permute-start(f32[4,32,128]{2,1,0:T(8,128)S(1)} %get-tuple-element.32), channel_id=1, source_target_pairs={{0,1},{1,0},{2,3},{3,2},{4,5},{5,4},{6,7},{7,6},{8,9},{9,8},{10,11... | collective-permute-start | bytes 196616 | tf_op jit(solution)/shard_map/ppermute | solution.py:362
  10.8 0.7 %collective-permute-start.1 = (f32[4,32,128]{2,1,0:T(8,128)S(1)}, f32[4,32,128]{2,1,0:T(8,128)S(1)}, u32[]{:S(2)}, u32[]{:S(2)}) collective-permute-start(f32[4,32,128]{2,1,0:T(8,128)S(1)} %get-tuple-element.33), channel_id=1, source_target_pairs={{1,2},{2,1},{3,4},{4,3},{5,6},{6,5},{7,8},{8,7},{9,10},{10,9},{11,... | collective-permute-start | bytes 196616 | tf_op jit(solution)/shard_map/ppermute | solution.py:361
  11.4 0.2 collective-permute-done.from_chip
  11.7 0.0 collective-permute-done.1.from_outside
  11.7 0.2 shard_map.140._.partial
  11.9 15.1 %all-to-all-done = f32[16,80,128]{2,1,0:T(8,128)S(1)} async-done(((f32[16,80,128]{2,1,0:T(8,128)}), f32[16,80,128]{2,1,0:T(8,128)S(1)}, u32[]{:S(2)}, u32[]{:S(2)}) %all-to-all-start) | async-done | bytes 655392 | tf_op jit(solution)/shard_map/all_to_all | solution.py:360
  27.0 0.1 shard_map.141
  27.1 0.1 collective-permute-start.2
  27.3 1.0 %shard_map.142 = (f32[2,32,128]{2,1,0:T(8,128)}, f32[1,16]{1,0:T(1,128)}) custom-call(f32[2,32,128]{2,1,0:T(8,128)S(1)} %shard_map.140._.partial, f32[2,32,128]{2,1,0:T(8,128)S(1)} %get-tuple-element.24.sat, f32[2,32,128]{2,1,0:T(8,128)S(1)} %get-tuple-element.25.lamw, f32[2,32,128]{2,1,0:T(8,128)S(1)} %get-tuple-element.26.lamo, ...), custom_call_target="tpu_custom_call" | custom-call | tf_op jit(solution)/shard_map/pallas_call | solution.py:327
  28.2 0.6 %collective-permute-done.2.other = f32[640,128]{1,0:T(8,128)S(1)} collective-permute-done((f32[640,128]{1,0:T(8,128)S(1)}, f32[640,128]{1,0:T(8,128)S(1)}, u32[]{:S(2)}, u32[]{:S(2)}) %collective-permute-start.2) | collective-permute-done | bytes 327712 | tf_op jit(solution)/shard_map/ppermute | solution.py:374
  28.8 1.3 %shard_map.143 = f32[2,32,128]{2,1,0:T(8,128)} custom-call(f32[5,256,128]{2,1,0:T(8,128)S(1)} %get-tuple-element.41.own, f32[640,128]{1,0:T(8,128)S(1)} %collective-permute-done.2.other), custom_call_target="tpu_custom_call" | custom-call | tf_op jit(solution)/shard_map/pallas_call | solution.py:327
Async XLA Ops:
  3.0 24.0 %all-to-all-start = ((f32[16,80,128]{2,1,0:T(8,128)}), f32[16,80,128]{2,1,0:T(8,128)S(1)}, u32[]{:S(2)}, u32[]{:S(2)}) async-start(f32[16,80,128]{2,1,0:T(8,128)} %get-tuple-element.37), calls=%async_computation | async-start | bytes 1310720 | tf_op jit(solution)/shard_map/all_to_all | solution.py:360
  10.4 1.3 %collective-permute-start = (f32[4,32,128]{2,1,0:T(8,128)S(1)}, f32[4,32,128]{2,1,0:T(8,128)S(1)}, u32[]{:S(2)}, u32[]{:S(2)}) collective-permute-start(f32[4,32,128]{2,1,0:T(8,128)S(1)} %get-tuple-element.32), channel_id=1, source_target_pairs={{0,1},{1,0},{2,3},{3,2},{4,5},{5,4},{6,7},{7,6},{8,9},{9,8},{10,11... | collective-permute-start | bytes 196616 | tf_op jit(solution)/shard_map/ppermute | solution.py:362
  10.8 0.9 %collective-permute-start.1 = (f32[4,32,128]{2,1,0:T(8,128)S(1)}, f32[4,32,128]{2,1,0:T(8,128)S(1)}, u32[]{:S(2)}, u32[]{:S(2)}) collective-permute-start(f32[4,32,128]{2,1,0:T(8,128)S(1)} %get-tuple-element.33), channel_id=1, source_target_pairs={{1,2},{2,1},{3,4},{4,3},{5,6},{6,5},{7,8},{8,7},{9,10},{10,9},{11,... | collective-permute-start | bytes 196616 | tf_op jit(solution)/shard_map/ppermute | solution.py:361
  27.1 1.7 %collective-permute-start.2 = (f32[640,128]{1,0:T(8,128)S(1)}, f32[640,128]{1,0:T(8,128)S(1)}, u32[]{:S(2)}, u32[]{:S(2)}) collective-permute-start(f32[640,128]{1,0:T(8,128)S(1)} %get-tuple-element.42), channel_id=1, source_target_pairs={{0,1},{1,0},{2,3},{3,2},{4,5},{5,4},{6,7},{7,6},{8,9},{9,8},{10,11... | collective-permute-start | bytes 983048 | tf_op jit(solution)/shard_map/ppermute | solution.py:374

commit v4 on v3

--- a/solution.py
+++ b/solution.py
@@ -16,11 +16,10 @@
 TILE = 8
 HALO = 3
 ROWS = 5
-RHS, DIAG, SAT, LAMW, LAMO, PERMX, CY, CZ = range(8)
-OUTSIDE = (0.0, 1.0, 0.0, 0.0, 0.0, 1.0, 0.0, 0.0)
-FIELDS = 8
-WELL_ROW = CZ * 2 * ROWS
-CHUNK = FIELDS * 2 * ROWS
+RHS, DIAG, CY, CZ, INNER, SAT, LAMW, LAMO, PERMX, CHIP = 0, 2, 4, 6, 8, 9, 10, 11, 12, 13
+FIELDS = 14
+WELL_ROW = FIELDS * ROWS
+CHUNK = WELL_ROW + 2
 
 
 def mobilities(s):
@@ -83,49 +82,48 @@
     return trans * (fw * (lw - lwn) + fo * (lo - lon)), trans * (fw + fo)
 
 
-def pack_kernel(groups, *refs):
-    sources, loaded, (packed, weight, chip_edge, outer_edge) = refs[:12], refs[12:24], refs[24:28]
-    padded, well_rows, sems = refs[28:]
-    copies = [pltpu.make_async_copy(src, dst, sems.at[i]) for i, (src, dst) in enumerate(zip(sources, loaded))]
-    for i in (8, 10, 9, 11, 1, 2, 3, 5, 6, 7, 4, 0):
-        copies[i].start()
-    press, sat, lamw, lamo, permx, permy, permz, pore, cell, well, index, bhp = loaded
+def load_kernel(*refs):
+    sources, loaded, edge, sems = refs[:12], refs[12:24], refs[24], refs[25]
+    pairs = [(sources[i].at[1 - core()], edge.at[i]) for i in range(5)] + list(zip(sources, loaded))
+    copies = [pltpu.make_async_copy(src, dst, sems.at[i]) for i, (src, dst) in enumerate(pairs)]
+    for copy in copies:
+        copy.start()
+    for copy in copies:
+        copy.wait()
+
+
+def cell_kernel(
+    groups, sat, lamw, lamo, permx, permy, permz, pore, cell, well, index, bhp,
+    rhs_out, diag_out, cy_out, cz_out, inner_out, weight, well_rows,
+):
     ny = sat.shape[1]
-    for i in (8, 10):
-        copies[i].wait()
     cells = cell[...]
     row_marks = marks(cells // LANES, 2 * ny)
     lane_marks = marks(cells % LANES, LANES)
     perf_weight = scatter_cells(index[...], row_marks, lane_marks)
     weight[...] = perf_weight
-    for i in (0, 1, 2, 3, 4, 5, 6, 7, 9, 11):
-        copies[i].wait()
-
-    flows = []
+    flows, layers, rhs, diag = [], [], [], []
     for x in range(2):
         s, lw, lo = sat[x], lamw[x], lamo[x]
         mw, mo = mobilities(s)
-        here = (lw, lo, mw, mo)
+        layers.append((lw, lo, mw, mo))
         flow = mw * lw + mo * lo
         flows.append(flow)
         w = perf_weight[x * ny : (x + 1) * ny]
-        rhs = flow * w
-        diag = compressibility * pore[x] + (mw + mo) * w
-        couplings = []
-        for k, axis in ((permy[x], 0), (permz[x], 1)):
-            there = tuple(upper(f, axis) for f in here)
-            g, c = face(here, there, 0.5 * transmissibility(k, axis))
-            rhs = rhs + g - lower(g, axis)
-            diag = diag + c + lower(c, axis)
-            couplings.append(c)
-        for field, value in enumerate((rhs, diag, s, lw, lo, permx[x], *couplings)):
-            edge = jnp.full((TILE, LANES), OUTSIDE[field], jnp.float32)
-            padded[field, x, :TILE] = edge
-            padded[field, x, TILE : TILE + ny] = value
-            padded[field, x, TILE + ny :] = edge
-    for member, field in enumerate((press, lamw, lamo, permx)):
-        chip_edge[member] = field[1 - core()]
-        outer_edge[member] = field[core()]
+        rhs.append(flow * w)
+        diag.append(compressibility * pore[x] + (mw + mo) * w)
+        for k, axis, out in ((permy[x], 0, cy_out), (permz[x], 1, cz_out)):
+            there = tuple(upper(f, axis) for f in layers[x])
+            g, c = face(layers[x], there, 0.5 * transmissibility(k, axis))
+            rhs[x] += g - lower(g, axis)
+            diag[x] += c + lower(c, axis)
+            out[x] = c
+    k, kn = permx[0], permx[1]
+    g, c = face(layers[0], layers[1], k * kn / (k + kn))
+    inner_out[...] = c
+    for x in range(2):
+        rhs_out[x] = rhs[x] + (1 - 2 * x) * g
+        diag_out[x] = diag[x] + c
 
     flow_parts = jnp.concatenate(split(jnp.concatenate(flows)))
     row_parts = jnp.concatenate([row_marks.astype(jnp.bfloat16)] * 3)
@@ -137,18 +135,46 @@
     well_rows[...] = scatter_cells(inflow, owners, places)
     well_rows[:, :wells_each] = jnp.broadcast_to(bhp[...], (groups, wells_each))
 
+
+def pack_kernel(
+    groups, press, sat, lamw, lamo, permx, from_chip, rhs, diag, cy, cz, inner, well_rows,
+    packed, outer_a, outer_b, padded,
+):
+    ny = sat.shape[1]
+    near, far = 1 - core(), core()
+    k, kn = permx[near], from_chip[4]
+    here = (lamw[near], lamo[near], *mobilities(sat[near]))
+    there = (from_chip[2], from_chip[3], *mobilities(from_chip[1]))
+    g, c = face(here, there, k * kn / (k + kn))
+    for i, ref in enumerate((press, lamw)):
+        outer_a[i] = ref[far]
+    for i, ref in enumerate((lamo, permx)):
+        outer_b[i] = ref[far]
+
+    values = [None] * FIELDS
+    for x in range(2):
+        touches = near == x
+        values[RHS + x] = rhs[x] + jnp.where(touches, g, 0.0)
+        values[DIAG + x] = diag[x] + jnp.where(touches, c, 0.0)
+        values[CY + x] = cy[x]
+        values[CZ + x] = cz[x]
+    values[INNER] = inner[...]
+    values[SAT], values[LAMW], values[LAMO], values[PERMX] = sat[far], lamw[far], lamo[far], permx[far]
+    values[CHIP] = c
+    for f, value in enumerate(values):
+        edge = jnp.full((TILE, LANES), 1.0 if f in (DIAG, DIAG + 1, PERMX) else 0.0, jnp.float32)
+        padded[f, :TILE] = edge
+        padded[f, TILE : TILE + ny] = value
+        padded[f, TILE + ny :] = edge
+
     def chip(c, _):
         for parity in range(2):
             d = 2 * c + parity
             start = TILE + 4 * c - HALO + ROWS * parity
-            for field in range(FIELDS):
-                for x in range(2):
-                    at = (2 * field + x) * ROWS
-                    if at == WELL_ROW:
-                        packed[d, at + 1 : at + ROWS] = padded[field, x, pl.ds(start + 1 - parity, ROWS - 1)]
-                    else:
-                        packed[d, at : at + ROWS] = padded[field, x, pl.ds(start, ROWS)]
+            for f in range(FIELDS):
+                packed[d, f * ROWS : (f + 1) * ROWS] = padded[f, pl.ds(start, ROWS)]
             packed[d, WELL_ROW : WELL_ROW + 1] = well_rows[pl.ds(d, 1)]
+            packed[d, WELL_ROW + 1 :] = jnp.zeros((1, LANES), jnp.float32)
         return 0
 
     if groups <= 16:
@@ -165,11 +191,11 @@
     return t * (lw - lwn), t * (lo - lon)
 
 
-def sat_kernel(press, sat, lamw, lamo, permx, permy, permz, pore, weight, from_chip, from_outside, out):
+def sat_kernel(press, sat, lamw, lamo, permx, permy, permz, pore, weight, from_chip, outside_a, outside_b, out):
     ny = sat.shape[1]
     first = core() == 0
     layers = [tuple(r[x] for r in (press, lamw, lamo, permx)) for x in range(2)]
-    ends = [tuple(r[m] for m in range(4)) for r in (from_outside, from_chip)]
+    ends = (outside_a[0], outside_a[1], outside_b[0], outside_b[1]), tuple(from_chip[m] for m in (0, 2, 3, 4))
     below = tuple(jnp.where(first, a, b) for a, b in zip(*ends))
     above = tuple(jnp.where(first, b, a) for a, b in zip(*ends))
     chain = (below, *layers, above)
@@ -224,32 +250,35 @@
     low = sublane() < 4
 
     def body(parity):
-        def tile(x, field):
-            at = (x // 2) * CHUNK + (2 * field + x % 2) * ROWS
-            start = at - HALO * parity
-            if field == CZ and x % 2 == 0:
-                start += parity
+        def tile(s, field):
+            start = s * CHUNK + field * ROWS - HALO * parity
             inside = min(max(start, 0), total - TILE)
             rows = received[inside : inside + TILE]
             return rows if inside == start else pltpu.roll(rows, (inside - start) % TILE, 0)
 
         count = 2 * groups
-        cells = []
-        for x in range(count):
-            cells.append((tile(x, LAMW), tile(x, LAMO), *mobilities(tile(x, SAT)), tile(x, PERMX)))
-        before = None
+        below = None
         waiting = []
         for x in range(count):
-            rhs, diag = tile(x, RHS), tile(x, DIAG)
-            if before is not None:
-                rhs, diag = rhs - before[0], diag + before[1]
-            if x < count - 1:
-                k, kn = cells[x][4], cells[x + 1][4]
-                before = face(cells[x][:4], cells[x + 1][:4], k * kn / (k + kn))
-                rhs, diag, link = rhs + before[0], diag + before[1], before[1]
+            s = x // 2
+            rhs, diag = tile(s, RHS + x % 2), tile(s, DIAG + x % 2)
+            if below is not None:
+                rhs, diag = rhs - below[0], diag + below[1]
+            below = None
+            if x % 2 == 0:
+                link = tile(s, INNER)
+            elif x % 4 == 1:
+                link = tile(s, CHIP)
+            elif x < count - 1:
+                near, far = (
+                    (tile(t, LAMW), tile(t, LAMO), *mobilities(tile(t, SAT)), tile(t, PERMX)) for t in (s, s + 1)
+                )
+                k, kn = near[4], far[4]
+                below = face(near[:4], far[:4], k * kn / (k + kn))
+                rhs, diag, link = rhs + below[0], diag + below[1], below[1]
             else:
                 link = jnp.zeros_like(rhs)
-            fields = (rhs, diag, link, tile(x, CY), tile(x, CZ))
+            fields = (rhs, diag, link, tile(s, CY + x % 2), tile(s, CZ + x % 2))
             for f, value in enumerate(fields):
                 own[f, x * TILE : (x + 1) * TILE] = value
             waiting += fields
@@ -348,20 +377,32 @@
     outer_pairs = [(i, i - 1 + 2 * (i % 2)) for i in range(1, groups - 1)]
     box = (2, ny, LANES)
 
-    *loaded, packed, weight, chip_edge, outer_edge = call(
+    *loaded, chip_edge = call(
+        load_kernel,
+        [jax.ShapeDtypeStruct(v.shape, v.dtype) for v in given] + [(5, ny, LANES)],
+        *given,
+        scratch=[pltpu.SemaphoreType.DMA((len(given) + 5,))],
+        in_hbm=len(given),
+    )
+    press, sat, lamw, lamo, permx, permy, permz, pore, cell, well, index, bhp = loaded
+    from_chip = lax.ppermute(chip_edge, "gx", chip_pairs)
+    rhs, diag, cy, cz, inner, weight, well_rows = call(
+        functools.partial(cell_kernel, groups),
+        [box] * 4 + [(ny, LANES), (2 * ny, LANES), (groups, LANES)],
+        sat, lamw, lamo, permx, permy, permz, pore, cell, well, index, bhp,
+    )
+    packed, outer_a, outer_b = call(
         functools.partial(pack_kernel, groups),
-        [jax.ShapeDtypeStruct(v.shape, v.dtype) for v in given]
-        + [(groups, CHUNK, LANES), (2 * ny, LANES), (4, ny, LANES), (4, ny, LANES)],
-        *given,
-        scratch=[(FIELDS, 2, ny + 2 * TILE, LANES), (groups, LANES), pltpu.SemaphoreType.DMA((len(given),))],
-        in_hbm=len(given),
-    )
-    press, sat, lamw, lamo, permx, permy, permz, pore, cell, well, index, _ = loaded
+        [(groups, CHUNK, LANES), box, box],
+        press, sat, lamw, lamo, permx, from_chip, rhs, diag, cy, cz, inner, well_rows,
+        scratch=[(FIELDS, ny + 2 * TILE, LANES)],
+    )
     received = lax.all_to_all(packed, "gx", split_axis=0, concat_axis=0, tiled=True)
-    from_outside = lax.ppermute(outer_edge, "gx", outer_pairs)
-    from_chip = lax.ppermute(chip_edge, "gx", chip_pairs)
+    outside_a = lax.ppermute(outer_a, "gx", outer_pairs)
+    outside_b = lax.ppermute(outer_b, "gx", outer_pairs)
     (partial,) = call(
-        sat_kernel, [box], press, sat, lamw, lamo, permx, permy, permz, pore, weight, from_chip, from_outside
+        sat_kernel, [box],
+        press, sat, lamw, lamo, permx, permy, permz, pore, weight, from_chip, outside_a, outside_b,
     )
 
     count = 2 * groups

time: 30.5 us -> 30.3 us (level)
  waiting for transfers between devices: 15.9 us -> 15.2 us
  starting transfers between devices: 8.57 us -> 9.18 us
    all_to_all x1, waiting for transfers between devices: 15.1 us -> 14 us  [on_device(): lax.all_to_all(packed, 'gx', split_axis=0, concat_axis=0, tiled=True)]
    ppermute x1 -> x2, starting transfers between devices: 0.65 us -> 1.33 us  [the longest x1 0.66 us: on_device(): outside_a = lax.ppermute(outer_a, 'gx', outer_pairs)]
    pallas_call x5 -> x7, Pallas kernels: 4.88 us -> 4.93 us  [call(): pl.pallas_call(kernel, out_shape=tuple((o if isinstance(o, jax.ShapeDtype...]
  transfers between devices with their start and end apart: 4 -> 5, of which waited for: 3 -> 3; matrix products, arithmetic and copies ran while one was open for 0% -> 0% of each run, Pallas kernels for 4% -> 5%
where the time goes in v4:
time: 30.3 us; the launch traced here: 30 us
  waiting for transfers between devices  15.2 us (50%)
  starting transfers between devices  9.18 us (30%)
  Pallas kernels  4.93 us (16%)
  between operations  0.7 us (2%)
    all_to_all x1, waiting for transfers between devices, on_device(): lax.all_to_all(packed, 'gx', split_axis=0, concat_axis=0, tiled=True)  14 us
    all_to_all x1, starting transfers between devices, on_device(): lax.all_to_all(packed, 'gx', split_axis=0, concat_axis=0, tiled=True)  7.26 us
    pallas_call x7, Pallas kernels, call(): pl.pallas_call(kernel, out_shape=tuple((o if isinstance(o, jax.ShapeDtype...  4.93 us
    ppermute x1, starting transfers between devices, on_device(): outside_a = lax.ppermute(outer_a, 'gx', outer_pairs)  0.66 us
    ppermute x1, starting transfers between devices, on_device(): outside_b = lax.ppermute(outer_b, 'gx', outer_pairs)  0.66 us
    ppermute x1, waiting for transfers between devices, on_device(): other = lax.ppermute(send, 'gx', chip_pairs)  0.66 us
  transfers between devices with their start and end apart: 5, of which 3 were waited for; matrix products, arithmetic and copies ran while one was open for 0% of the time, Pallas kernels for 5%

profile of v4, /device:TPU:0, one launch (start us, length us, event | category | flops | bytes accessed | tf_op | source)
XLA Modules:
  0.0 30.0 jit_solution(15268619084290935258)
XLA Ops:
  0.6 1.1 %shard_map.139 = (f32[2,32,128]{2,1,0:T(8,128)S(1)}, f32[2,32,128]{2,1,0:T(8,128)S(1)}, f32[2,32,128]{2,1,0:T(8,128)S(1)}, f32[2,32,128]{2,1,0:T(8,128)S(1)}, f3...) custom-call(f32[2,32,128]{2,1,0:T(8,128)} %refs_0_.1, ...), custom_call_target="tpu_custom_call" | custom-call | tf_op jit(solution)/shard_map/pallas_call | solution.py:356
  1.8 0.5 %collective-permute-start = (f32[5,32,128]{2,1,0:T(8,128)S(1)}, f32[5,32,128]{2,1,0:T(8,128)S(1)}, u32[]{:S(2)}, u32[]{:S(2)}) collective-permute-start(f32[5,32,128]{2,1,0:T(8,128)S(1)} %get-tuple-element.44), channel_id=1, source_target_pairs={{0,1},{1,0},{2,3},{3,2},{4,5},{5,4},{6,7},{7,6},{8,9},{9,8},{10,11... | collective-permute-start | bytes 245768 | tf_op jit(solution)/shard_map/ppermute | solution.py:388
  2.3 0.4 %shard_map.140 = (f32[2,32,128]{2,1,0:T(8,128)S(1)}, f32[2,32,128]{2,1,0:T(8,128)S(1)}, f32[2,32,128]{2,1,0:T(8,128)S(1)}, f32[2,32,128]{2,1,0:T(8,128)S(1)}, f3...) custom-call(f32[2,32,128]{2,1,0:T(8,128)S(1)} %get-tuple-element.32.sat, ...), custom_call_target="tpu_custom_call" | custom-call | tf_op jit(solution)/shard_map/pallas_call | solution.py:356
  2.7 0.5 %collective-permute-done.from_chip = f32[5,32,128]{2,1,0:T(8,128)S(1)} collective-permute-done((f32[5,32,128]{2,1,0:T(8,128)S(1)}, f32[5,32,128]{2,1,0:T(8,128)S(1)}, u32[]{:S(2)}, u32[]{:S(2)}) %collective-permute-start) | collective-permute-done | bytes 81952 | tf_op jit(solution)/shard_map/ppermute | solution.py:388
  3.2 0.9 %shard_map.141 = (f32[16,72,128]{2,1,0:T(8,128)}, f32[2,32,128]{2,1,0:T(8,128)S(1)}, f32[2,32,128]{2,1,0:T(8,128)S(1)}) custom-call(f32[2,32,128]{2,1,0:T(8,128)S(1)} %get-tuple-element.31.press, f32[2,32,128]{2,1,0:T(8,128)S(1)} %get-tuple-element.32.sat, f32[2,32,128]{2,1,0:T(8,128)S(1)} %get-tuple-element.33.lamw, ...), custom_call_target="tpu_custom_call" | custom-call | tf_op jit(solution)/shard_map/pallas_call | solution.py:356
  4.1 7.3 %all-to-all-start = ((f32[16,72,128]{2,1,0:T(8,128)}), f32[16,72,128]{2,1,0:T(8,128)S(1)}, u32[]{:S(2)}, u32[]{:S(2)}) async-start(f32[16,72,128]{2,1,0:T(8,128)} %get-tuple-element.53), calls=%async_computation | async-start | bytes 1179648 | tf_op jit(solution)/shard_map/all_to_all | solution.py:400
  11.4 0.7 %collective-permute-start.1 = (f32[2,32,128]{2,1,0:T(8,128)S(1)}, f32[2,32,128]{2,1,0:T(8,128)S(1)}, u32[]{:S(2)}, u32[]{:S(2)}) collective-permute-start(f32[2,32,128]{2,1,0:T(8,128)S(1)} %get-tuple-element.51), channel_id=1, source_target_pairs={{1,2},{2,1},{3,4},{4,3},{5,6},{6,5},{7,8},{8,7},{9,10},{10,9},{11,... | collective-permute-start | bytes 98312 | tf_op jit(solution)/shard_map/ppermute | solution.py:401
  12.1 0.7 %collective-permute-start.2 = (f32[2,32,128]{2,1,0:T(8,128)S(1)}, f32[2,32,128]{2,1,0:T(8,128)S(1)}, u32[]{:S(2)}, u32[]{:S(2)}) collective-permute-start(f32[2,32,128]{2,1,0:T(8,128)S(1)} %get-tuple-element.52), channel_id=1, source_target_pairs={{1,2},{2,1},{3,4},{4,3},{5,6},{6,5},{7,8},{8,7},{9,10},{10,9},{11,... | collective-permute-start | bytes 98312 | tf_op jit(solution)/shard_map/ppermute | solution.py:402
  12.8 0.0 collective-permute-done.1.outside_a
  12.8 0.0 collective-permute-done.2.outside_b
  12.8 0.2 shard_map.142._.partial
  13.0 14.0 %all-to-all-done = f32[16,72,128]{2,1,0:T(8,128)S(1)} async-done(((f32[16,72,128]{2,1,0:T(8,128)}), f32[16,72,128]{2,1,0:T(8,128)S(1)}, u32[]{:S(2)}, u32[]{:S(2)}) %all-to-all-start) | async-done | bytes 589856 | tf_op jit(solution)/shard_map/all_to_all | solution.py:400
  27.0 0.1 shard_map.143
  27.1 0.1 collective-permute-start.3
  27.1 1.0 %shard_map.144 = (f32[2,32,128]{2,1,0:T(8,128)}, f32[1,16]{1,0:T(1,128)}) custom-call(f32[2,32,128]{2,1,0:T(8,128)S(1)} %shard_map.142._.partial, f32[2,32,128]{2,1,0:T(8,128)S(1)} %get-tuple-element.32.sat, f32[2,32,128]{2,1,0:T(8,128)S(1)} %get-tuple-element.33.lamw, f32[2,32,128]{2,1,0:T(8,128)S(1)} %get-tuple-element.34.lamo, ...), custom_call_target="tpu_custom_call" | custom-call | tf_op jit(solution)/shard_map/pallas_call | solution.py:356
  28.1 0.7 %collective-permute-done.3.other = f32[640,128]{1,0:T(8,128)S(1)} collective-permute-done((f32[640,128]{1,0:T(8,128)S(1)}, f32[640,128]{1,0:T(8,128)S(1)}, u32[]{:S(2)}, u32[]{:S(2)}) %collective-permute-start.3) | collective-permute-done | bytes 327712 | tf_op jit(solution)/shard_map/ppermute | solution.py:415
  28.7 1.3 %shard_map.145 = f32[2,32,128]{2,1,0:T(8,128)} custom-call(f32[5,256,128]{2,1,0:T(8,128)S(1)} %get-tuple-element.57.own, f32[640,128]{1,0:T(8,128)S(1)} %collective-permute-done.3.other), custom_call_target="tpu_custom_call" | custom-call | tf_op jit(solution)/shard_map/pallas_call | solution.py:356
Async XLA Ops:
  1.8 1.4 %collective-permute-start = (f32[5,32,128]{2,1,0:T(8,128)S(1)}, f32[5,32,128]{2,1,0:T(8,128)S(1)}, u32[]{:S(2)}, u32[]{:S(2)}) collective-permute-start(f32[5,32,128]{2,1,0:T(8,128)S(1)} %get-tuple-element.44), channel_id=1, source_target_pairs={{0,1},{1,0},{2,3},{3,2},{4,5},{5,4},{6,7},{7,6},{8,9},{9,8},{10,11... | collective-permute-start | bytes 245768 | tf_op jit(solution)/shard_map/ppermute | solution.py:388
  4.1 22.8 %all-to-all-start = ((f32[16,72,128]{2,1,0:T(8,128)}), f32[16,72,128]{2,1,0:T(8,128)S(1)}, u32[]{:S(2)}, u32[]{:S(2)}) async-start(f32[16,72,128]{2,1,0:T(8,128)} %get-tuple-element.53), calls=%async_computation | async-start | bytes 1179648 | tf_op jit(solution)/shard_map/all_to_all | solution.py:400
  11.4 1.3 %collective-permute-start.1 = (f32[2,32,128]{2,1,0:T(8,128)S(1)}, f32[2,32,128]{2,1,0:T(8,128)S(1)}, u32[]{:S(2)}, u32[]{:S(2)}) collective-permute-start(f32[2,32,128]{2,1,0:T(8,128)S(1)} %get-tuple-element.51), channel_id=1, source_target_pairs={{1,2},{2,1},{3,4},{4,3},{5,6},{6,5},{7,8},{8,7},{9,10},{10,9},{11,... | collective-permute-start | bytes 98312 | tf_op jit(solution)/shard_map/ppermute | solution.py:401
  12.1 0.7 %collective-permute-start.2 = (f32[2,32,128]{2,1,0:T(8,128)S(1)}, f32[2,32,128]{2,1,0:T(8,128)S(1)}, u32[]{:S(2)}, u32[]{:S(2)}) collective-permute-start(f32[2,32,128]{2,1,0:T(8,128)S(1)} %get-tuple-element.52), channel_id=1, source_target_pairs={{1,2},{2,1},{3,4},{4,3},{5,6},{6,5},{7,8},{8,7},{9,10},{10,9},{11,... | collective-permute-start | bytes 98312 | tf_op jit(solution)/shard_map/ppermute | solution.py:402
  27.1 1.7 %collective-permute-start.3 = (f32[640,128]{1,0:T(8,128)S(1)}, f32[640,128]{1,0:T(8,128)S(1)}, u32[]{:S(2)}, u32[]{:S(2)}) collective-permute-start(f32[640,128]{1,0:T(8,128)S(1)} %get-tuple-element.58), channel_id=1, source_target_pairs={{0,1},{1,0},{2,3},{3,2},{4,5},{5,4},{6,7},{7,6},{8,9},{9,8},{10,11... | collective-permute-start | bytes 983048 | tf_op jit(solution)/shard_map/ppermute | solution.py:415

commit v5 on v4

--- a/solution.py
+++ b/solution.py
@@ -355,7 +355,7 @@
     args = [pltpu.with_memory_space_constraint(v, place) if place == pltpu.HBM else v for v, place in zip(args, places)]
     return pl.pallas_call(
         kernel,
-        out_shape=tuple(o if isinstance(o, jax.ShapeDtypeStruct) else jax.ShapeDtypeStruct(o, jnp.float32) for o in outs),
+        out_shape=tuple(jax.ShapeDtypeStruct(o, jnp.float32) if isinstance(o, tuple) else o for o in outs),
         in_specs=[pl.BlockSpec(memory_space=place) for place in places],
         out_specs=tuple(pl.BlockSpec(memory_space=pltpu.VMEM) for _ in outs),
         scratch_shapes=[pltpu.VMEM(o, jnp.float32) if isinstance(o, tuple) else o for o in scratch],
@@ -393,7 +393,7 @@
     )
     packed, outer_a, outer_b = call(
         functools.partial(pack_kernel, groups),
-        [(groups, CHUNK, LANES), box, box],
+        [pltpu.VMEM((groups, CHUNK, LANES), jnp.float32), box, box],
         press, sat, lamw, lamo, permx, from_chip, rhs, diag, cy, cz, inner, well_rows,
         scratch=[(FIELDS, ny + 2 * TILE, LANES)],
     )

time: 30.3 us -> 30.3 us (level)
  no operation moved by 1% of the time
where the time goes in v5:
time: 30.3 us; the launch traced here: 30 us
  waiting for transfers between devices  15.2 us (50%)
  starting transfers between devices  9.18 us (30%)
  Pallas kernels  4.93 us (16%)
  between operations  0.7 us (2%)
    all_to_all x1, waiting for transfers between devices, on_device(): lax.all_to_all(packed, 'gx', split_axis=0, concat_axis=0, tiled=True)  14 us
    all_to_all x1, starting transfers between devices, on_device(): lax.all_to_all(packed, 'gx', split_axis=0, concat_axis=0, tiled=True)  7.26 us
    pallas_call x7, Pallas kernels, call(): pl.pallas_call(kernel, out_shape=tuple((jax.ShapeDtypeStruct(o, jnp.float...  4.93 us
    ppermute x1, starting transfers between devices, on_device(): outside_a = lax.ppermute(outer_a, 'gx', outer_pairs)  0.66 us
    ppermute x1, starting transfers between devices, on_device(): outside_b = lax.ppermute(outer_b, 'gx', outer_pairs)  0.66 us
    ppermute x1, waiting for transfers between devices, on_device(): other = lax.ppermute(send, 'gx', chip_pairs)  0.66 us
  transfers between devices with their start and end apart: 5, of which 3 were waited for; matrix products, arithmetic and copies ran while one was open for 0% of the time, Pallas kernels for 5%

profile of v5, /device:TPU:0, one launch (start us, length us, event | category | flops | bytes accessed | tf_op | source)
XLA Modules:
  0.0 30.0 jit_solution(15268619084290935258)
XLA Ops:
  0.6 1.1 %shard_map.139 = (f32[2,32,128]{2,1,0:T(8,128)S(1)}, f32[2,32,128]{2,1,0:T(8,128)S(1)}, f32[2,32,128]{2,1,0:T(8,128)S(1)}, f32[2,32,128]{2,1,0:T(8,128)S(1)}, f3...) custom-call(f32[2,32,128]{2,1,0:T(8,128)} %refs_0_.1, ...), custom_call_target="tpu_custom_call" | custom-call | tf_op jit(solution)/shard_map/pallas_call | solution.py:356
  1.8 0.5 %collective-permute-start = (f32[5,32,128]{2,1,0:T(8,128)S(1)}, f32[5,32,128]{2,1,0:T(8,128)S(1)}, u32[]{:S(2)}, u32[]{:S(2)}) collective-permute-start(f32[5,32,128]{2,1,0:T(8,128)S(1)} %get-tuple-element.44), channel_id=1, source_target_pairs={{0,1},{1,0},{2,3},{3,2},{4,5},{5,4},{6,7},{7,6},{8,9},{9,8},{10,11... | collective-permute-start | bytes 245768 | tf_op jit(solution)/shard_map/ppermute | solution.py:388
  2.3 0.4 %shard_map.140 = (f32[2,32,128]{2,1,0:T(8,128)S(1)}, f32[2,32,128]{2,1,0:T(8,128)S(1)}, f32[2,32,128]{2,1,0:T(8,128)S(1)}, f32[2,32,128]{2,1,0:T(8,128)S(1)}, f3...) custom-call(f32[2,32,128]{2,1,0:T(8,128)S(1)} %get-tuple-element.32.sat, ...), custom_call_target="tpu_custom_call" | custom-call | tf_op jit(solution)/shard_map/pallas_call | solution.py:356
  2.7 0.5 %collective-permute-done.from_chip = f32[5,32,128]{2,1,0:T(8,128)S(1)} collective-permute-done((f32[5,32,128]{2,1,0:T(8,128)S(1)}, f32[5,32,128]{2,1,0:T(8,128)S(1)}, u32[]{:S(2)}, u32[]{:S(2)}) %collective-permute-start) | collective-permute-done | bytes 81952 | tf_op jit(solution)/shard_map/ppermute | solution.py:388
  3.2 0.9 %shard_map.141 = (f32[16,72,128]{2,1,0:T(8,128)}, f32[2,32,128]{2,1,0:T(8,128)S(1)}, f32[2,32,128]{2,1,0:T(8,128)S(1)}) custom-call(f32[2,32,128]{2,1,0:T(8,128)S(1)} %get-tuple-element.31.press, f32[2,32,128]{2,1,0:T(8,128)S(1)} %get-tuple-element.32.sat, f32[2,32,128]{2,1,0:T(8,128)S(1)} %get-tuple-element.33.lamw, ...), custom_call_target="tpu_custom_call" | custom-call | tf_op jit(solution)/shard_map/pallas_call | solution.py:356
  4.1 7.3 %all-to-all-start = ((f32[16,72,128]{2,1,0:T(8,128)}), f32[16,72,128]{2,1,0:T(8,128)S(1)}, u32[]{:S(2)}, u32[]{:S(2)}) async-start(f32[16,72,128]{2,1,0:T(8,128)} %get-tuple-element.53), calls=%async_computation | async-start | bytes 1179648 | tf_op jit(solution)/shard_map/all_to_all | solution.py:400
  11.4 0.7 %collective-permute-start.1 = (f32[2,32,128]{2,1,0:T(8,128)S(1)}, f32[2,32,128]{2,1,0:T(8,128)S(1)}, u32[]{:S(2)}, u32[]{:S(2)}) collective-permute-start(f32[2,32,128]{2,1,0:T(8,128)S(1)} %get-tuple-element.51), channel_id=1, source_target_pairs={{1,2},{2,1},{3,4},{4,3},{5,6},{6,5},{7,8},{8,7},{9,10},{10,9},{11,... | collective-permute-start | bytes 98312 | tf_op jit(solution)/shard_map/ppermute | solution.py:401
  12.1 0.7 %collective-permute-start.2 = (f32[2,32,128]{2,1,0:T(8,128)S(1)}, f32[2,32,128]{2,1,0:T(8,128)S(1)}, u32[]{:S(2)}, u32[]{:S(2)}) collective-permute-start(f32[2,32,128]{2,1,0:T(8,128)S(1)} %get-tuple-element.52), channel_id=1, source_target_pairs={{1,2},{2,1},{3,4},{4,3},{5,6},{6,5},{7,8},{8,7},{9,10},{10,9},{11,... | collective-permute-start | bytes 98312 | tf_op jit(solution)/shard_map/ppermute | solution.py:402
  12.8 0.0 collective-permute-done.1.outside_a
  12.8 0.0 collective-permute-done.2.outside_b
  12.8 0.2 shard_map.142._.partial
  13.0 14.0 %all-to-all-done = f32[16,72,128]{2,1,0:T(8,128)S(1)} async-done(((f32[16,72,128]{2,1,0:T(8,128)}), f32[16,72,128]{2,1,0:T(8,128)S(1)}, u32[]{:S(2)}, u32[]{:S(2)}) %all-to-all-start) | async-done | bytes 589856 | tf_op jit(solution)/shard_map/all_to_all | solution.py:400
  27.0 0.1 shard_map.143
  27.1 0.1 collective-permute-start.3
  27.1 1.0 %shard_map.144 = (f32[2,32,128]{2,1,0:T(8,128)}, f32[1,16]{1,0:T(1,128)}) custom-call(f32[2,32,128]{2,1,0:T(8,128)S(1)} %shard_map.142._.partial, f32[2,32,128]{2,1,0:T(8,128)S(1)} %get-tuple-element.32.sat, f32[2,32,128]{2,1,0:T(8,128)S(1)} %get-tuple-element.33.lamw, f32[2,32,128]{2,1,0:T(8,128)S(1)} %get-tuple-element.34.lamo, ...), custom_call_target="tpu_custom_call" | custom-call | tf_op jit(solution)/shard_map/pallas_call | solution.py:356
  28.1 0.7 %collective-permute-done.3.other = f32[640,128]{1,0:T(8,128)S(1)} collective-permute-done((f32[640,128]{1,0:T(8,128)S(1)}, f32[640,128]{1,0:T(8,128)S(1)}, u32[]{:S(2)}, u32[]{:S(2)}) %collective-permute-start.3) | collective-permute-done | bytes 327712 | tf_op jit(solution)/shard_map/ppermute | solution.py:415
  28.7 1.3 %shard_map.145 = f32[2,32,128]{2,1,0:T(8,128)} custom-call(f32[5,256,128]{2,1,0:T(8,128)S(1)} %get-tuple-element.57.own, f32[640,128]{1,0:T(8,128)S(1)} %collective-permute-done.3.other), custom_call_target="tpu_custom_call" | custom-call | tf_op jit(solution)/shard_map/pallas_call | solution.py:356
Async XLA Ops:
  1.8 1.4 %collective-permute-start = (f32[5,32,128]{2,1,0:T(8,128)S(1)}, f32[5,32,128]{2,1,0:T(8,128)S(1)}, u32[]{:S(2)}, u32[]{:S(2)}) collective-permute-start(f32[5,32,128]{2,1,0:T(8,128)S(1)} %get-tuple-element.44), channel_id=1, source_target_pairs={{0,1},{1,0},{2,3},{3,2},{4,5},{5,4},{6,7},{7,6},{8,9},{9,8},{10,11... | collective-permute-start | bytes 245768 | tf_op jit(solution)/shard_map/ppermute | solution.py:388
  4.1 22.8 %all-to-all-start = ((f32[16,72,128]{2,1,0:T(8,128)}), f32[16,72,128]{2,1,0:T(8,128)S(1)}, u32[]{:S(2)}, u32[]{:S(2)}) async-start(f32[16,72,128]{2,1,0:T(8,128)} %get-tuple-element.53), calls=%async_computation | async-start | bytes 1179648 | tf_op jit(solution)/shard_map/all_to_all | solution.py:400
  11.4 1.3 %collective-permute-start.1 = (f32[2,32,128]{2,1,0:T(8,128)S(1)}, f32[2,32,128]{2,1,0:T(8,128)S(1)}, u32[]{:S(2)}, u32[]{:S(2)}) collective-permute-start(f32[2,32,128]{2,1,0:T(8,128)S(1)} %get-tuple-element.51), channel_id=1, source_target_pairs={{1,2},{2,1},{3,4},{4,3},{5,6},{6,5},{7,8},{8,7},{9,10},{10,9},{11,... | collective-permute-start | bytes 98312 | tf_op jit(solution)/shard_map/ppermute | solution.py:401
  12.1 0.7 %collective-permute-start.2 = (f32[2,32,128]{2,1,0:T(8,128)S(1)}, f32[2,32,128]{2,1,0:T(8,128)S(1)}, u32[]{:S(2)}, u32[]{:S(2)}) collective-permute-start(f32[2,32,128]{2,1,0:T(8,128)S(1)} %get-tuple-element.52), channel_id=1, source_target_pairs={{1,2},{2,1},{3,4},{4,3},{5,6},{6,5},{7,8},{8,7},{9,10},{10,9},{11,... | collective-permute-start | bytes 98312 | tf_op jit(solution)/shard_map/ppermute | solution.py:402
  27.1 1.7 %collective-permute-start.3 = (f32[640,128]{1,0:T(8,128)S(1)}, f32[640,128]{1,0:T(8,128)S(1)}, u32[]{:S(2)}, u32[]{:S(2)}) collective-permute-start(f32[640,128]{1,0:T(8,128)S(1)} %get-tuple-element.58), channel_id=1, source_target_pairs={{0,1},{1,0},{2,3},{3,2},{4,5},{5,4},{6,7},{7,6},{8,9},{9,8},{10,11... | collective-permute-start | bytes 983048 | tf_op jit(solution)/shard_map/ppermute | solution.py:415

commit v6 on v4

--- a/solution.py
+++ b/solution.py
@@ -11,6 +11,7 @@
 oil_viscosity = 2.0
 compressibility = 0.2
 SWEEPS = 4
+REDUCTIONS = 2
 
 LANES = 128
 TILE = 8
@@ -138,7 +139,7 @@
 
 def pack_kernel(
     groups, press, sat, lamw, lamo, permx, from_chip, rhs, diag, cy, cz, inner, well_rows,
-    packed, outer_a, outer_b, padded,
+    packed, outer, padded,
 ):
     ny = sat.shape[1]
     near, far = 1 - core(), core()
@@ -146,10 +147,8 @@
     here = (lamw[near], lamo[near], *mobilities(sat[near]))
     there = (from_chip[2], from_chip[3], *mobilities(from_chip[1]))
     g, c = face(here, there, k * kn / (k + kn))
-    for i, ref in enumerate((press, lamw)):
-        outer_a[i] = ref[far]
-    for i, ref in enumerate((lamo, permx)):
-        outer_b[i] = ref[far]
+    for i, ref in enumerate((press, lamw, lamo, permx)):
+        outer[i] = ref[far]
 
     values = [None] * FIELDS
     for x in range(2):
@@ -191,11 +190,11 @@
     return t * (lw - lwn), t * (lo - lon)
 
 
-def sat_kernel(press, sat, lamw, lamo, permx, permy, permz, pore, weight, from_chip, outside_a, outside_b, out):
+def sat_kernel(press, sat, lamw, lamo, permx, permy, permz, pore, weight, from_chip, from_outside, out):
     ny = sat.shape[1]
     first = core() == 0
     layers = [tuple(r[x] for r in (press, lamw, lamo, permx)) for x in range(2)]
-    ends = (outside_a[0], outside_a[1], outside_b[0], outside_b[1]), tuple(from_chip[m] for m in (0, 2, 3, 4))
+    ends = tuple(from_outside[m] for m in range(4)), tuple(from_chip[m] for m in (0, 2, 3, 4))
     below = tuple(jnp.where(first, a, b) for a, b in zip(*ends))
     above = tuple(jnp.where(first, b, a) for a, b in zip(*ends))
     chain = (below, *layers, above)
@@ -294,28 +293,66 @@
         well_rows[s : s + 1] = received[s * CHUNK + WELL_ROW : s * CHUNK + WELL_ROW + 1]
 
 
-def sweep(targets, weights, inverses, middle):
-    count = len(targets)
+def solver(diag, link, levels):
+    count = len(diag)
+    if levels:
+        inverse = {j: 1.0 / diag[j] for j in range(1, count, 2)}
+        left = {j: link[j - 1] * inverse[j] for j in inverse}
+        right = {j: link[j] * inverse[j] for j in inverse if j < count - 1}
+        kept_diag, kept_link = [], []
+        for i in range(0, count, 2):
+            d = diag[i] - link[i] * left[i + 1]
+            kept_diag.append(d - link[i - 1] * right[i - 1] if i else d)
+            if i < count - 2:
+                kept_link.append(link[i] * right[i + 1])
+        inner = solver(kept_diag, kept_link, levels - 1)
+
+        def solve(b):
+            reduced = []
+            for i in range(0, count, 2):
+                t = b[i] + left[i + 1] * b[i + 1]
+                reduced.append(t + right[i - 1] * b[i - 1] if i else t)
+            u = [None] * count
+            u[::2] = inner(reduced)
+            for j in inverse:
+                t = inverse[j] * b[j] + left[j] * u[j - 1]
+                u[j] = t + right[j] * u[j + 1] if j < count - 1 else t
+            return u
+
+        return solve
+
     half = count // 2
-    b = list(targets)
-    for j in range(1, half):
-        b[j] = b[j] + weights[j - 1] * b[j - 1]
+    weights, inverses = [None] * count, [None] * count
+    da, db = diag[0], diag[count - 1]
+    for j in range(half - 1):
         m = count - 1 - j
-        b[m] = b[m] + weights[m + 1] * b[m + 1]
-    da, db, c, inverse = middle
-    u = [None] * count
-    u[half - 1] = (b[half - 1] * db + c * b[half]) * inverse
-    u[half] = (b[half] * da + c * b[half - 1]) * inverse
-    for j in range(half - 2, -1, -1):
-        u[j] = inverses[j] * b[j] + weights[j] * u[j + 1]
-        m = count - 1 - j
-        u[m] = inverses[m] * b[m] + weights[m] * u[m - 1]
-    return u
+        inverses[j], inverses[m] = 1.0 / da, 1.0 / db
+        weights[j], weights[m] = link[j] * inverses[j], link[m - 1] * inverses[m]
+        da = diag[j + 1] - link[j] * weights[j]
+        db = diag[m - 1] - link[m - 1] * weights[m]
+    c = link[half - 1]
+    inverse = 1.0 / (da * db - c * c)
+
+    def solve(b):
+        b = list(b)
+        for j in range(1, half):
+            b[j] = b[j] + weights[j - 1] * b[j - 1]
+            m = count - 1 - j
+            b[m] = b[m] + weights[m + 1] * b[m + 1]
+        u = [None] * count
+        u[half - 1] = (b[half - 1] * db + c * b[half]) * inverse
+        u[half] = (b[half] * da + c * b[half - 1]) * inverse
+        for j in range(half - 2, -1, -1):
+            u[j] = inverses[j] * b[j] + weights[j] * u[j + 1]
+            m = count - 1 - j
+            u[m] = inverses[m] * b[m] + weights[m] * u[m - 1]
+        return u
+
+    return solve
 
 
 def sweep_kernel(sweeps, own, other, out):
     count = own.shape[1] // TILE
-    half = count // 2
     row = sublane()
     first = core() == 0
     kept = jnp.logical_and(row >= jnp.where(first, 0, HALO), row < jnp.where(first, ROWS, TILE))
@@ -327,24 +364,14 @@
             x, f = n // 5, n % 5
             fields[f].append(jnp.where(kept, own[f, x * TILE : (x + 1) * TILE], value))
     rhs, diag, link, cy, cz = fields
-    weights, inverses = [None] * count, [None] * count
-    da, db = diag[0], diag[count - 1]
-    for j in range(half - 1):
-        m = count - 1 - j
-        inverses[j], inverses[m] = 1.0 / da, 1.0 / db
-        weights[j], weights[m] = link[j] * inverses[j], link[m - 1] * inverses[m]
-        da = diag[j + 1] - link[j] * weights[j]
-        db = diag[m - 1] - link[m - 1] * weights[m]
-    c = link[half - 1]
-    middle = (da, db, c, 1.0 / (da * db - c * c))
-
-    u = sweep(rhs, weights, inverses, middle)
+    solve = solver(diag, link, REDUCTIONS)
+    u = solve(rhs)
     for _ in range(1, sweeps):
         targets = []
         for x in range(count):
             t = rhs[x] + cy[x] * upper(u[x], 0) + lower(cy[x] * u[x], 0)
             targets.append(t + cz[x] * upper(u[x], 1) + lower(cz[x] * u[x], 1))
-        u = sweep(targets, weights, inverses, middle)
+        u = solve(targets)
     for x in range(count):
         for y in range(2):
             out[y, x : x + 1] = u[x][HALO + y : HALO + y + 1]
@@ -391,18 +418,17 @@
         [box] * 4 + [(ny, LANES), (2 * ny, LANES), (groups, LANES)],
         sat, lamw, lamo, permx, permy, permz, pore, cell, well, index, bhp,
     )
-    packed, outer_a, outer_b = call(
+    packed, outer = call(
         functools.partial(pack_kernel, groups),
-        [(groups, CHUNK, LANES), box, box],
+        [(groups, CHUNK, LANES), (4, ny, LANES)],
         press, sat, lamw, lamo, permx, from_chip, rhs, diag, cy, cz, inner, well_rows,
         scratch=[(FIELDS, ny + 2 * TILE, LANES)],
     )
     received = lax.all_to_all(packed, "gx", split_axis=0, concat_axis=0, tiled=True)
-    outside_a = lax.ppermute(outer_a, "gx", outer_pairs)
-    outside_b = lax.ppermute(outer_b, "gx", outer_pairs)
+    from_outside = lax.ppermute(outer, "gx", outer_pairs)
     (partial,) = call(
         sat_kernel, [box],
-        press, sat, lamw, lamo, permx, permy, permz, pore, weight, from_chip, outside_a, outside_b,
+        press, sat, lamw, lamo, permx, permy, permz, pore, weight, from_chip, from_outside,
     )
 
     count = 2 * groups

time: 30.3 us -> 30.3 us (level)
  waiting for transfers between devices: 15.2 us -> 15.9 us
  starting transfers between devices: 9.18 us -> 8.52 us
    all_to_all x1, waiting for transfers between devices: 14 us -> 14.7 us  [on_device(): lax.all_to_all(packed, 'gx', split_axis=0, concat_axis=0, tiled=True)]
    ppermute x2 -> x1, starting transfers between devices: 1.33 us -> 0.66 us  [on_device(): from_outside = lax.ppermute(outer, 'gx', outer_pairs)]
  transfers between devices with their start and end apart: 5 -> 4, of which waited for: 3 -> 3; matrix products, arithmetic and copies ran while one was open for 0% -> 0% of each run, Pallas kernels for 5% -> 5%
where the time goes in v6:
time: 30.3 us; the launch traced here: 29.9 us
  waiting for transfers between devices  15.9 us (52%)
  starting transfers between devices  8.52 us (28%)
  Pallas kernels  4.87 us (16%)
  between operations  0.69 us (2%)
    all_to_all x1, waiting for transfers between devices, on_device(): lax.all_to_all(packed, 'gx', split_axis=0, concat_axis=0, tiled=True)  14.7 us
    all_to_all x1, starting transfers between devices, on_device(): lax.all_to_all(packed, 'gx', split_axis=0, concat_axis=0, tiled=True)  7.26 us
    pallas_call x7, Pallas kernels, call(): pl.pallas_call(kernel, out_shape=tuple((o if isinstance(o, jax.ShapeDtype...  4.87 us
    ppermute x1, starting transfers between devices, on_device(): from_outside = lax.ppermute(outer, 'gx', outer_pairs)  0.66 us
    ppermute x1, waiting for transfers between devices, on_device(): other = lax.ppermute(send, 'gx', chip_pairs)  0.65 us
  transfers between devices with their start and end apart: 4, of which 3 were waited for; matrix products, arithmetic and copies ran while one was open for 0% of the time, Pallas kernels for 5%

profile of v6, /device:TPU:0, one launch (start us, length us, event | category | flops | bytes accessed | tf_op | source)
XLA Modules:
  0.0 29.9 jit_solution(2089237754016671914)
XLA Ops:
  0.6 1.1 %shard_map.139 = (f32[2,32,128]{2,1,0:T(8,128)S(1)}, f32[2,32,128]{2,1,0:T(8,128)S(1)}, f32[2,32,128]{2,1,0:T(8,128)S(1)}, f32[2,32,128]{2,1,0:T(8,128)S(1)}, f3...) custom-call(f32[2,32,128]{2,1,0:T(8,128)} %refs_0_.1, ...), custom_call_target="tpu_custom_call" | custom-call | tf_op jit(solution)/shard_map/pallas_call | solution.py:383
  1.8 0.5 %collective-permute-start = (f32[5,32,128]{2,1,0:T(8,128)S(1)}, f32[5,32,128]{2,1,0:T(8,128)S(1)}, u32[]{:S(2)}, u32[]{:S(2)}) collective-permute-start(f32[5,32,128]{2,1,0:T(8,128)S(1)} %get-tuple-element.43), channel_id=1, source_target_pairs={{0,1},{1,0},{2,3},{3,2},{4,5},{5,4},{6,7},{7,6},{8,9},{9,8},{10,11... | collective-permute-start | bytes 245768 | tf_op jit(solution)/shard_map/ppermute | solution.py:415
  2.3 0.4 %shard_map.140 = (f32[2,32,128]{2,1,0:T(8,128)S(1)}, f32[2,32,128]{2,1,0:T(8,128)S(1)}, f32[2,32,128]{2,1,0:T(8,128)S(1)}, f32[2,32,128]{2,1,0:T(8,128)S(1)}, f3...) custom-call(f32[2,32,128]{2,1,0:T(8,128)S(1)} %get-tuple-element.31.sat, ...), custom_call_target="tpu_custom_call" | custom-call | tf_op jit(solution)/shard_map/pallas_call | solution.py:383
  2.7 0.5 %collective-permute-done.from_chip = f32[5,32,128]{2,1,0:T(8,128)S(1)} collective-permute-done((f32[5,32,128]{2,1,0:T(8,128)S(1)}, f32[5,32,128]{2,1,0:T(8,128)S(1)}, u32[]{:S(2)}, u32[]{:S(2)}) %collective-permute-start) | collective-permute-done | bytes 81952 | tf_op jit(solution)/shard_map/ppermute | solution.py:415
  3.2 0.9 %shard_map.141 = (f32[16,72,128]{2,1,0:T(8,128)}, f32[4,32,128]{2,1,0:T(8,128)S(1)}) custom-call(f32[2,32,128]{2,1,0:T(8,128)S(1)} %get-tuple-element.30.press, f32[2,32,128]{2,1,0:T(8,128)S(1)} %get-tuple-element.31.sat, f32[2,32,128]{2,1,0:T(8,128)S(1)} %get-tuple-element.32.lamw, f32[2,32,128]{2,1,0:T(8,128)S(1)} %get-tuple-element.33.lamo, ...), custom_call_target="tpu_custom_call" | custom-call | tf_op jit(solution)/shard_map/pallas_call | solution.py:383
  4.1 7.3 %all-to-all-start = ((f32[16,72,128]{2,1,0:T(8,128)}), f32[16,72,128]{2,1,0:T(8,128)S(1)}, u32[]{:S(2)}, u32[]{:S(2)}) async-start(f32[16,72,128]{2,1,0:T(8,128)} %get-tuple-element.51), calls=%async_computation | async-start | bytes 1179648 | tf_op jit(solution)/shard_map/all_to_all | solution.py:427
  11.4 0.7 %collective-permute-start.1 = (f32[4,32,128]{2,1,0:T(8,128)S(1)}, f32[4,32,128]{2,1,0:T(8,128)S(1)}, u32[]{:S(2)}, u32[]{:S(2)}) collective-permute-start(f32[4,32,128]{2,1,0:T(8,128)S(1)} %get-tuple-element.50), channel_id=1, source_target_pairs={{1,2},{2,1},{3,4},{4,3},{5,6},{6,5},{7,8},{8,7},{9,10},{10,9},{11,... | collective-permute-start | bytes 196616 | tf_op jit(solution)/shard_map/ppermute | solution.py:428
  12.1 0.0 collective-permute-done.1.from_outside
  12.1 0.2 shard_map.142._.partial
  12.3 14.7 %all-to-all-done = f32[16,72,128]{2,1,0:T(8,128)S(1)} async-done(((f32[16,72,128]{2,1,0:T(8,128)}), f32[16,72,128]{2,1,0:T(8,128)S(1)}, u32[]{:S(2)}, u32[]{:S(2)}) %all-to-all-start) | async-done | bytes 589856 | tf_op jit(solution)/shard_map/all_to_all | solution.py:427
  27.0 0.1 shard_map.143
  27.1 0.1 collective-permute-start.2
  27.1 1.0 %shard_map.144 = (f32[2,32,128]{2,1,0:T(8,128)}, f32[1,16]{1,0:T(1,128)}) custom-call(f32[2,32,128]{2,1,0:T(8,128)S(1)} %shard_map.142._.partial, f32[2,32,128]{2,1,0:T(8,128)S(1)} %get-tuple-element.31.sat, f32[2,32,128]{2,1,0:T(8,128)S(1)} %get-tuple-element.32.lamw, f32[2,32,128]{2,1,0:T(8,128)S(1)} %get-tuple-element.33.lamo, ...), custom_call_target="tpu_custom_call" | custom-call | tf_op jit(solution)/shard_map/pallas_call | solution.py:383
  28.1 0.7 %collective-permute-done.2.other = f32[640,128]{1,0:T(8,128)S(1)} collective-permute-done((f32[640,128]{1,0:T(8,128)S(1)}, f32[640,128]{1,0:T(8,128)S(1)}, u32[]{:S(2)}, u32[]{:S(2)}) %collective-permute-start.2) | collective-permute-done | bytes 327712 | tf_op jit(solution)/shard_map/ppermute | solution.py:441
  28.8 1.2 %shard_map.145 = f32[2,32,128]{2,1,0:T(8,128)} custom-call(f32[5,256,128]{2,1,0:T(8,128)S(1)} %get-tuple-element.55.own, f32[640,128]{1,0:T(8,128)S(1)} %collective-permute-done.2.other), custom_call_target="tpu_custom_call" | custom-call | tf_op jit(solution)/shard_map/pallas_call | solution.py:383
Async XLA Ops:
  1.8 1.4 %collective-permute-start = (f32[5,32,128]{2,1,0:T(8,128)S(1)}, f32[5,32,128]{2,1,0:T(8,128)S(1)}, u32[]{:S(2)}, u32[]{:S(2)}) collective-permute-start(f32[5,32,128]{2,1,0:T(8,128)S(1)} %get-tuple-element.43), channel_id=1, source_target_pairs={{0,1},{1,0},{2,3},{3,2},{4,5},{5,4},{6,7},{7,6},{8,9},{9,8},{10,11... | collective-permute-start | bytes 245768 | tf_op jit(solution)/shard_map/ppermute | solution.py:415
  4.1 22.8 %all-to-all-start = ((f32[16,72,128]{2,1,0:T(8,128)}), f32[16,72,128]{2,1,0:T(8,128)S(1)}, u32[]{:S(2)}, u32[]{:S(2)}) async-start(f32[16,72,128]{2,1,0:T(8,128)} %get-tuple-element.51), calls=%async_computation | async-start | bytes 1179648 | tf_op jit(solution)/shard_map/all_to_all | solution.py:427
  11.4 0.7 %collective-permute-start.1 = (f32[4,32,128]{2,1,0:T(8,128)S(1)}, f32[4,32,128]{2,1,0:T(8,128)S(1)}, u32[]{:S(2)}, u32[]{:S(2)}) collective-permute-start(f32[4,32,128]{2,1,0:T(8,128)S(1)} %get-tuple-element.50), channel_id=1, source_target_pairs={{1,2},{2,1},{3,4},{4,3},{5,6},{6,5},{7,8},{8,7},{9,10},{10,9},{11,... | collective-permute-start | bytes 196616 | tf_op jit(solution)/shard_map/ppermute | solution.py:428
  27.1 1.7 %collective-permute-start.2 = (f32[640,128]{1,0:T(8,128)S(1)}, f32[640,128]{1,0:T(8,128)S(1)}, u32[]{:S(2)}, u32[]{:S(2)}) collective-permute-start(f32[640,128]{1,0:T(8,128)S(1)} %get-tuple-element.56), channel_id=1, source_target_pairs={{0,1},{1,0},{2,3},{3,2},{4,5},{5,4},{6,7},{7,6},{8,9},{9,8},{10,11... | collective-permute-start | bytes 983048 | tf_op jit(solution)/shard_map/ppermute | solution.py:441

commit v7 on v6

--- a/solution.py
+++ b/solution.py
@@ -17,10 +17,10 @@
 TILE = 8
 HALO = 3
 ROWS = 5
-RHS, DIAG, CY, CZ, INNER, SAT, LAMW, LAMO, PERMX, CHIP = 0, 2, 4, 6, 8, 9, 10, 11, 12, 13
-FIELDS = 14
-WELL_ROW = FIELDS * ROWS
-CHUNK = WELL_ROW + 2
+NEAR_RHS, NEAR_DIAG, CHIP, WELL_ROW = 0, 5, 10, 15
+REST = 16
+FAR_RHS, FAR_DIAG, CY, CZ, INNER, SAT, LAMW, LAMO, PERMX = (REST + ROWS * i for i in (0, 1, 2, 4, 6, 7, 8, 9, 10))
+CHUNK = REST + 11 * ROWS + 1
 
 
 def mobilities(s):
@@ -93,17 +93,40 @@
         copy.wait()
 
 
+def pad(ref, value, outside):
+    ny = value.shape[0]
+    edge = jnp.full((TILE, LANES), outside, jnp.float32)
+    ref[:TILE] = edge
+    ref[TILE : TILE + ny] = value
+    ref[TILE + ny :] = edge
+
+
+def for_chunks(groups, store):
+    def chip(c, _):
+        for parity in range(2):
+            store(2 * c + parity, TILE + 4 * c - HALO + ROWS * parity)
+        return 0
+
+    if groups <= 16:
+        for c in range(groups // 2):
+            chip(c, 0)
+    else:
+        lax.fori_loop(0, groups // 2, chip, 0)
+
+
 def cell_kernel(
-    groups, sat, lamw, lamo, permx, permy, permz, pore, cell, well, index, bhp,
-    rhs_out, diag_out, cy_out, cz_out, inner_out, weight, well_rows,
+    groups, press, sat, lamw, lamo, permx, permy, permz, pore, cell, well, index, bhp,
+    near_rhs, near_diag, outer, weight, well_rows, packed, padded, chunks, sem,
 ):
     ny = sat.shape[1]
+    far = core()
+    first = far == 0
     cells = cell[...]
     row_marks = marks(cells // LANES, 2 * ny)
     lane_marks = marks(cells % LANES, LANES)
     perf_weight = scatter_cells(index[...], row_marks, lane_marks)
     weight[...] = perf_weight
-    flows, layers, rhs, diag = [], [], [], []
+    flows, layers, rhs, diag, couplings = [], [], [], [], [[], []]
     for x in range(2):
         s, lw, lo = sat[x], lamw[x], lamo[x]
         mw, mo = mobilities(s)
@@ -113,19 +136,34 @@
         w = perf_weight[x * ny : (x + 1) * ny]
         rhs.append(flow * w)
         diag.append(compressibility * pore[x] + (mw + mo) * w)
-        for k, axis, out in ((permy[x], 0, cy_out), (permz[x], 1, cz_out)):
+        for axis, k in enumerate((permy[x], permz[x])):
             there = tuple(upper(f, axis) for f in layers[x])
             g, c = face(layers[x], there, 0.5 * transmissibility(k, axis))
             rhs[x] += g - lower(g, axis)
             diag[x] += c + lower(c, axis)
-            out[x] = c
+            couplings[axis].append(c)
     k, kn = permx[0], permx[1]
-    g, c = face(layers[0], layers[1], k * kn / (k + kn))
-    inner_out[...] = c
-    for x in range(2):
-        rhs_out[x] = rhs[x] + (1 - 2 * x) * g
-        diag_out[x] = diag[x] + c
-
+    g, inner = face(layers[0], layers[1], k * kn / (k + kn))
+    rhs = rhs[0] + g, rhs[1] - g
+    diag = diag[0] + inner, diag[1] + inner
+    near_rhs[...] = jnp.where(first, rhs[1], rhs[0])
+    near_diag[...] = jnp.where(first, diag[1], diag[0])
+    values = [jnp.where(first, rhs[0], rhs[1]), jnp.where(first, diag[0], diag[1]), *couplings[0], *couplings[1], inner]
+    values += [sat[far], lamw[far], lamo[far], permx[far]]
+    for f, value in enumerate(values):
+        pad(padded.at[f], value, 1.0 if REST + f * ROWS in (FAR_DIAG, PERMX) else 0.0)
+
+    def store(d, start):
+        for f in range(len(values)):
+            chunks[d, f * ROWS : (f + 1) * ROWS] = padded[f, pl.ds(start, ROWS)]
+        chunks[d, len(values) * ROWS :] = jnp.zeros((1, LANES), jnp.float32)
+
+    for_chunks(groups, store)
+    copy = pltpu.make_async_copy(chunks, packed.at[:, REST:], sem)
+    copy.start()
+
+    for i, ref in enumerate((press, lamw, lamo, permx)):
+        outer[i] = ref[far]
     flow_parts = jnp.concatenate(split(jnp.concatenate(flows)))
     row_parts = jnp.concatenate([row_marks.astype(jnp.bfloat16)] * 3)
     by_lane = dot(flow_parts, row_parts, ((0,), (0,)))
@@ -135,52 +173,27 @@
     places = marks(well[...] % wells_each + wells_each, LANES)
     well_rows[...] = scatter_cells(inflow, owners, places)
     well_rows[:, :wells_each] = jnp.broadcast_to(bhp[...], (groups, wells_each))
-
-
-def pack_kernel(
-    groups, press, sat, lamw, lamo, permx, from_chip, rhs, diag, cy, cz, inner, well_rows,
-    packed, outer, padded,
-):
-    ny = sat.shape[1]
-    near, far = 1 - core(), core()
+    copy.wait()
+
+
+def pack_kernel(groups, sat, lamw, lamo, permx, from_chip, near_rhs, near_diag, well_rows, _, packed, padded, chunks, sem):
+    near = 1 - core()
     k, kn = permx[near], from_chip[4]
     here = (lamw[near], lamo[near], *mobilities(sat[near]))
     there = (from_chip[2], from_chip[3], *mobilities(from_chip[1]))
     g, c = face(here, there, k * kn / (k + kn))
-    for i, ref in enumerate((press, lamw, lamo, permx)):
-        outer[i] = ref[far]
-
-    values = [None] * FIELDS
-    for x in range(2):
-        touches = near == x
-        values[RHS + x] = rhs[x] + jnp.where(touches, g, 0.0)
-        values[DIAG + x] = diag[x] + jnp.where(touches, c, 0.0)
-        values[CY + x] = cy[x]
-        values[CZ + x] = cz[x]
-    values[INNER] = inner[...]
-    values[SAT], values[LAMW], values[LAMO], values[PERMX] = sat[far], lamw[far], lamo[far], permx[far]
-    values[CHIP] = c
-    for f, value in enumerate(values):
-        edge = jnp.full((TILE, LANES), 1.0 if f in (DIAG, DIAG + 1, PERMX) else 0.0, jnp.float32)
-        padded[f, :TILE] = edge
-        padded[f, TILE : TILE + ny] = value
-        padded[f, TILE + ny :] = edge
-
-    def chip(c, _):
-        for parity in range(2):
-            d = 2 * c + parity
-            start = TILE + 4 * c - HALO + ROWS * parity
-            for f in range(FIELDS):
-                packed[d, f * ROWS : (f + 1) * ROWS] = padded[f, pl.ds(start, ROWS)]
-            packed[d, WELL_ROW : WELL_ROW + 1] = well_rows[pl.ds(d, 1)]
-            packed[d, WELL_ROW + 1 :] = jnp.zeros((1, LANES), jnp.float32)
-        return 0
-
-    if groups <= 16:
-        for c in range(groups // 2):
-            chip(c, 0)
-    else:
-        lax.fori_loop(0, groups // 2, chip, 0)
+    for i, (value, outside) in enumerate(((near_rhs[...] + g, 0.0), (near_diag[...] + c, 1.0), (c, 0.0))):
+        pad(padded.at[i], value, outside)
+
+    def store(d, start):
+        for i in range(3):
+            chunks[d, i * ROWS : (i + 1) * ROWS] = padded[i, pl.ds(start, ROWS)]
+        chunks[d, WELL_ROW : WELL_ROW + 1] = well_rows[pl.ds(d, 1)]
+
+    for_chunks(groups, store)
+    copy = pltpu.make_async_copy(chunks, packed.at[:, :REST], sem)
+    copy.start()
+    copy.wait()
 
 
 def sat_parts(here, there, trans):
@@ -250,7 +263,7 @@
 
     def body(parity):
         def tile(s, field):
-            start = s * CHUNK + field * ROWS - HALO * parity
+            start = s * CHUNK + field - HALO * parity
             inside = min(max(start, 0), total - TILE)
             rows = received[inside : inside + TILE]
             return rows if inside == start else pltpu.roll(rows, (inside - start) % TILE, 0)
@@ -260,7 +273,8 @@
         waiting = []
         for x in range(count):
             s = x // 2
-            rhs, diag = tile(s, RHS + x % 2), tile(s, DIAG + x % 2)
+            near = x % 4 in (1, 2)
+            rhs, diag = tile(s, NEAR_RHS if near else FAR_RHS), tile(s, NEAR_DIAG if near else FAR_DIAG)
             if below is not None:
                 rhs, diag = rhs - below[0], diag + below[1]
             below = None
@@ -269,15 +283,15 @@
             elif x % 4 == 1:
                 link = tile(s, CHIP)
             elif x < count - 1:
-                near, far = (
+                here, there = (
                     (tile(t, LAMW), tile(t, LAMO), *mobilities(tile(t, SAT)), tile(t, PERMX)) for t in (s, s + 1)
                 )
-                k, kn = near[4], far[4]
-                below = face(near[:4], far[:4], k * kn / (k + kn))
+                k, kn = here[4], there[4]
+                below = face(here[:4], there[:4], k * kn / (k + kn))
                 rhs, diag, link = rhs + below[0], diag + below[1], below[1]
             else:
                 link = jnp.zeros_like(rhs)
-            fields = (rhs, diag, link, tile(s, CY + x % 2), tile(s, CZ + x % 2))
+            fields = (rhs, diag, link, tile(s, CY + x % 2 * ROWS), tile(s, CZ + x % 2 * ROWS))
             for f, value in enumerate(fields):
                 own[f, x * TILE : (x + 1) * TILE] = value
             waiting += fields
@@ -377,15 +391,21 @@
             out[y, x : x + 1] = u[x][HALO + y : HALO + y + 1]
 
 
-def call(kernel, outs, *args, scratch=(), in_hbm=0):
+def call(kernel, outs, *args, scratch=(), in_hbm=0, out_hbm=0, aliases=None):
     places = [pltpu.VMEM] * (len(args) - in_hbm) + [pltpu.HBM] * in_hbm
     args = [pltpu.with_memory_space_constraint(v, place) if place == pltpu.HBM else v for v, place in zip(args, places)]
+    results = [pltpu.VMEM] * (len(outs) - out_hbm) + [pltpu.HBM] * out_hbm
+
+    def shaped(shape, place):
+        return pltpu.HBM(shape, jnp.float32) if place == pltpu.HBM else jax.ShapeDtypeStruct(shape, jnp.float32)
+
     return pl.pallas_call(
         kernel,
-        out_shape=tuple(o if isinstance(o, jax.ShapeDtypeStruct) else jax.ShapeDtypeStruct(o, jnp.float32) for o in outs),
+        out_shape=tuple(shaped(o, place) if isinstance(o, tuple) else o for o, place in zip(outs, results)),
         in_specs=[pl.BlockSpec(memory_space=place) for place in places],
-        out_specs=tuple(pl.BlockSpec(memory_space=pltpu.VMEM) for _ in outs),
+        out_specs=tuple(pl.BlockSpec(memory_space=place) for place in results),
         scratch_shapes=[pltpu.VMEM(o, jnp.float32) if isinstance(o, tuple) else o for o in scratch],
+        input_output_aliases=aliases or {},
         compiler_params=pltpu.CompilerParams(vmem_limit_bytes=40 << 20),
     )(*args)
 
@@ -413,16 +433,22 @@
     )
     press, sat, lamw, lamo, permx, permy, permz, pore, cell, well, index, bhp = loaded
     from_chip = lax.ppermute(chip_edge, "gx", chip_pairs)
-    rhs, diag, cy, cz, inner, weight, well_rows = call(
+    plane = (ny, LANES)
+    chunk = (groups, CHUNK, LANES)
+    near_rhs, near_diag, outer, weight, well_rows, packed = call(
         functools.partial(cell_kernel, groups),
-        [box] * 4 + [(ny, LANES), (2 * ny, LANES), (groups, LANES)],
-        sat, lamw, lamo, permx, permy, permz, pore, cell, well, index, bhp,
-    )
-    packed, outer = call(
-        functools.partial(pack_kernel, groups),
-        [(groups, CHUNK, LANES), (4, ny, LANES)],
-        press, sat, lamw, lamo, permx, from_chip, rhs, diag, cy, cz, inner, well_rows,
-        scratch=[(FIELDS, ny + 2 * TILE, LANES)],
+        [plane, plane, (4, ny, LANES), (2 * ny, LANES), (groups, LANES), chunk],
+        press, sat, lamw, lamo, permx, permy, permz, pore, cell, well, index, bhp,
+        scratch=[(11, ny + 2 * TILE, LANES), (groups, CHUNK - REST, LANES), pltpu.SemaphoreType.DMA],
+        out_hbm=1,
+    )
+    (packed,) = call(
+        functools.partial(pack_kernel, groups), [chunk],
+        sat, lamw, lamo, permx, from_chip, near_rhs, near_diag, well_rows, packed,
+        scratch=[(3, ny + 2 * TILE, LANES), (groups, REST, LANES), pltpu.SemaphoreType.DMA],
+        in_hbm=1,
+        out_hbm=1,
+        aliases={8: 0},
     )
     received = lax.all_to_all(packed, "gx", split_axis=0, concat_axis=0, tiled=True)
     from_outside = lax.ppermute(outer, "gx", outer_pairs)

time: 30.3 us -> 30.1 us (level)
  waiting for transfers between devices: 15.9 us -> 15.3 us
  Pallas kernels: 4.87 us -> 5.37 us
    ppermute x1, waiting for transfers between devices: 0.53 us -> 0.01 us  [on_device(): from_chip = lax.ppermute(chip_edge, 'gx', chip_pairs)]
    pallas_call x7, Pallas kernels: 4.87 us -> 5.37 us  [call(): pl.pallas_call(kernel, out_shape=tuple((shaped(o, place) if isinstance(o,...]
  transfers between devices with their start and end apart: 4 -> 4, of which waited for: 3 -> 2; matrix products, arithmetic and copies ran while one was open for 0% -> 0% of each run, Pallas kernels for 5% -> 8%
where the time goes in v7:
time: 30.1 us; the launch traced here: 29.8 us
  waiting for transfers between devices  15.3 us (51%)
  starting transfers between devices  8.34 us (28%)
  Pallas kernels  5.37 us (18%)
  between operations  0.71 us (2%)
    all_to_all x1, waiting for transfers between devices, on_device(): lax.all_to_all(packed, 'gx', split_axis=0, concat_axis=0, tiled=True)  14.7 us
    all_to_all x1, starting transfers between devices, on_device(): lax.all_to_all(packed, 'gx', split_axis=0, concat_axis=0, tiled=True)  7.08 us
    pallas_call x7, Pallas kernels, call(): pl.pallas_call(kernel, out_shape=tuple((shaped(o, place) if isinstance(o,...  5.37 us
    ppermute x1, starting transfers between devices, on_device(): from_outside = lax.ppermute(outer, 'gx', outer_pairs)  0.66 us
    ppermute x1, waiting for transfers between devices, on_device(): other = lax.ppermute(send, 'gx', chip_pairs)  0.65 us
  transfers between devices with their start and end apart: 4, of which 2 were waited for; matrix products, arithmetic and copies ran while one was open for 0% of the time, Pallas kernels for 8%

profile of v7, /device:TPU:0, one launch (start us, length us, event | category | flops | bytes accessed | tf_op | source)
XLA Modules:
  0.0 29.8 jit_solution(2199069267576370845)
XLA Ops:
  0.6 1.1 %shard_map.139 = (f32[2,32,128]{2,1,0:T(8,128)S(1)}, f32[2,32,128]{2,1,0:T(8,128)S(1)}, f32[2,32,128]{2,1,0:T(8,128)S(1)}, f32[2,32,128]{2,1,0:T(8,128)S(1)}, f3...) custom-call(f32[2,32,128]{2,1,0:T(8,128)} %refs_0_.1, ...), custom_call_target="tpu_custom_call" | custom-call | tf_op jit(solution)/shard_map/pallas_call | solution.py:402
  1.8 0.5 %collective-permute-start = (f32[5,32,128]{2,1,0:T(8,128)S(1)}, f32[5,32,128]{2,1,0:T(8,128)S(1)}, u32[]{:S(2)}, u32[]{:S(2)}) collective-permute-start(f32[5,32,128]{2,1,0:T(8,128)S(1)} %get-tuple-element.40), channel_id=1, source_target_pairs={{0,1},{1,0},{2,3},{3,2},{4,5},{5,4},{6,7},{7,6},{8,9},{9,8},{10,11... | collective-permute-start | bytes 245768 | tf_op jit(solution)/shard_map/ppermute | solution.py:435
  2.3 1.1 %shard_map.140 = (f32[32,128]{1,0:T(8,128)S(1)}, f32[32,128]{1,0:T(8,128)S(1)}, f32[4,32,128]{2,1,0:T(8,128)S(1)}, f32[64,128]{1,0:T(8,128)S(1)}, f32[16,128]{1,0:T(8,128)S(1)}, /*index=5*/f32[16,72,128]{2,1,0:T(8,128)}) custom-call(f32[2,32,128]{2,1,0:T(8,128)S(1)} %get-tuple-element.27.press, f32[2,32,128]{2,1,0:T(8,128)S(1)} %get-tuple-element.28.sat, ...), custom_call_target="tpu_custom_call" | custom-call | tf_op jit(solution)/shard_map/pallas_call | solution.py:402
  3.4 0.0 collective-permute-done.from_chip
  3.4 0.7 %shard_map.142 = f32[16,72,128]{2,1,0:T(8,128)} custom-call(f32[2,32,128]{2,1,0:T(8,128)S(1)} %get-tuple-element.28.sat, f32[2,32,128]{2,1,0:T(8,128)S(1)} %get-tuple-element.29.lamw, f32[2,32,128]{2,1,0:T(8,128)S(1)} %get-tuple-element.30.lamo, f32[2,32,128]{2,1,0:T(8,128)S(1)} %get-tuple-element.31.permx, ...), custom_call_target="tpu_custom_call", output_to_operand_aliasing={{}: (8, {})} | custom-call | tf_op jit(solution)/shard_map/pallas_call | solution.py:402
  4.2 7.1 %all-to-all-start = ((f32[16,72,128]{2,1,0:T(8,128)}), f32[16,72,128]{2,1,0:T(8,128)S(1)}, u32[]{:S(2)}, u32[]{:S(2)}) async-start(f32[16,72,128]{2,1,0:T(8,128)} %shard_map.142), calls=%async_computation | async-start | bytes 1179648 | tf_op jit(solution)/shard_map/all_to_all | solution.py:453
  11.2 0.7 %collective-permute-start.1 = (f32[4,32,128]{2,1,0:T(8,128)S(1)}, f32[4,32,128]{2,1,0:T(8,128)S(1)}, u32[]{:S(2)}, u32[]{:S(2)}) collective-permute-start(f32[4,32,128]{2,1,0:T(8,128)S(1)} %get-tuple-element.41), channel_id=1, source_target_pairs={{1,2},{2,1},{3,4},{4,3},{5,6},{6,5},{7,8},{8,7},{9,10},{10,9},{11,... | collective-permute-start | bytes 196616 | tf_op jit(solution)/shard_map/ppermute | solution.py:454
  11.9 0.0 collective-permute-done.1.from_outside
  11.9 0.2 shard_map.141._.partial
  12.1 14.7 %all-to-all-done = f32[16,72,128]{2,1,0:T(8,128)S(1)} async-done(((f32[16,72,128]{2,1,0:T(8,128)}), f32[16,72,128]{2,1,0:T(8,128)S(1)}, u32[]{:S(2)}, u32[]{:S(2)}) %all-to-all-start) | async-done | bytes 589856 | tf_op jit(solution)/shard_map/all_to_all | solution.py:453
  26.8 0.1 shard_map.143
  26.9 0.1 collective-permute-start.2
  27.0 1.0 %shard_map.144 = (f32[2,32,128]{2,1,0:T(8,128)}, f32[1,16]{1,0:T(1,128)}) custom-call(f32[2,32,128]{2,1,0:T(8,128)S(1)} %shard_map.141._.partial, f32[2,32,128]{2,1,0:T(8,128)S(1)} %get-tuple-element.28.sat, f32[2,32,128]{2,1,0:T(8,128)S(1)} %get-tuple-element.29.lamw, f32[2,32,128]{2,1,0:T(8,128)S(1)} %get-tuple-element.30.lamo, ...), custom_call_target="tpu_custom_call" | custom-call | tf_op jit(solution)/shard_map/pallas_call | solution.py:402
  27.9 0.7 %collective-permute-done.2.other = f32[640,128]{1,0:T(8,128)S(1)} collective-permute-done((f32[640,128]{1,0:T(8,128)S(1)}, f32[640,128]{1,0:T(8,128)S(1)}, u32[]{:S(2)}, u32[]{:S(2)}) %collective-permute-start.2) | collective-permute-done | bytes 327712 | tf_op jit(solution)/shard_map/ppermute | solution.py:467
  28.6 1.2 %shard_map.145 = f32[2,32,128]{2,1,0:T(8,128)} custom-call(f32[5,256,128]{2,1,0:T(8,128)S(1)} %get-tuple-element.49.own, f32[640,128]{1,0:T(8,128)S(1)} %collective-permute-done.2.other), custom_call_target="tpu_custom_call" | custom-call | tf_op jit(solution)/shard_map/pallas_call | solution.py:402
Async XLA Ops:
  1.8 1.6 %collective-permute-start = (f32[5,32,128]{2,1,0:T(8,128)S(1)}, f32[5,32,128]{2,1,0:T(8,128)S(1)}, u32[]{:S(2)}, u32[]{:S(2)}) collective-permute-start(f32[5,32,128]{2,1,0:T(8,128)S(1)} %get-tuple-element.40), channel_id=1, source_target_pairs={{0,1},{1,0},{2,3},{3,2},{4,5},{5,4},{6,7},{7,6},{8,9},{9,8},{10,11... | collective-permute-start | bytes 245768 | tf_op jit(solution)/shard_map/ppermute | solution.py:435
  4.2 22.6 %all-to-all-start = ((f32[16,72,128]{2,1,0:T(8,128)}), f32[16,72,128]{2,1,0:T(8,128)S(1)}, u32[]{:S(2)}, u32[]{:S(2)}) async-start(f32[16,72,128]{2,1,0:T(8,128)} %shard_map.142), calls=%async_computation | async-start | bytes 1179648 | tf_op jit(solution)/shard_map/all_to_all | solution.py:453
  11.2 0.7 %collective-permute-start.1 = (f32[4,32,128]{2,1,0:T(8,128)S(1)}, f32[4,32,128]{2,1,0:T(8,128)S(1)}, u32[]{:S(2)}, u32[]{:S(2)}) collective-permute-start(f32[4,32,128]{2,1,0:T(8,128)S(1)} %get-tuple-element.41), channel_id=1, source_target_pairs={{1,2},{2,1},{3,4},{4,3},{5,6},{6,5},{7,8},{8,7},{9,10},{10,9},{11,... | collective-permute-start | bytes 196616 | tf_op jit(solution)/shard_map/ppermute | solution.py:454
  26.9 1.7 %collective-permute-start.2 = (f32[640,128]{1,0:T(8,128)S(1)}, f32[640,128]{1,0:T(8,128)S(1)}, u32[]{:S(2)}, u32[]{:S(2)}) collective-permute-start(f32[640,128]{1,0:T(8,128)S(1)} %get-tuple-element.50), channel_id=1, source_target_pairs={{0,1},{1,0},{2,3},{3,2},{4,5},{5,4},{6,7},{7,6},{8,9},{9,8},{10,11... | collective-permute-start | bytes 983048 | tf_op jit(solution)/shard_map/ppermute | solution.py:467

commit v8 on v7

--- a/solution.py
+++ b/solution.py
@@ -101,10 +101,16 @@
     ref[TILE + ny :] = edge
 
 
+def position(device, groups):
+    half = groups // 2
+    return 2 * (device % half) + device // half
+
+
 def for_chunks(groups, store):
     def chip(c, _):
         for parity in range(2):
-            store(2 * c + parity, TILE + 4 * c - HALO + ROWS * parity)
+            d = 2 * c + parity
+            store(position(d, groups), d, TILE + 4 * c - HALO + ROWS * parity)
         return 0
 
     if groups <= 16:
@@ -153,10 +159,10 @@
     for f, value in enumerate(values):
         pad(padded.at[f], value, 1.0 if REST + f * ROWS in (FAR_DIAG, PERMX) else 0.0)
 
-    def store(d, start):
+    def store(place, _, start):
         for f in range(len(values)):
-            chunks[d, f * ROWS : (f + 1) * ROWS] = padded[f, pl.ds(start, ROWS)]
-        chunks[d, len(values) * ROWS :] = jnp.zeros((1, LANES), jnp.float32)
+            chunks[place, f * ROWS : (f + 1) * ROWS] = padded[f, pl.ds(start, ROWS)]
+        chunks[place, len(values) * ROWS :] = jnp.zeros((1, LANES), jnp.float32)
 
     for_chunks(groups, store)
     copy = pltpu.make_async_copy(chunks, packed.at[:, REST:], sem)
@@ -185,10 +191,10 @@
     for i, (value, outside) in enumerate(((near_rhs[...] + g, 0.0), (near_diag[...] + c, 1.0), (c, 0.0))):
         pad(padded.at[i], value, outside)
 
-    def store(d, start):
+    def store(place, d, start):
         for i in range(3):
-            chunks[d, i * ROWS : (i + 1) * ROWS] = padded[i, pl.ds(start, ROWS)]
-        chunks[d, WELL_ROW : WELL_ROW + 1] = well_rows[pl.ds(d, 1)]
+            chunks[place, i * ROWS : (i + 1) * ROWS] = padded[i, pl.ds(start, ROWS)]
+        chunks[place, WELL_ROW : WELL_ROW + 1] = well_rows[pl.ds(d, 1)]
 
     for_chunks(groups, store)
     copy = pltpu.make_async_copy(chunks, packed.at[:, :REST], sem)
@@ -263,7 +269,7 @@
 
     def body(parity):
         def tile(s, field):
-            start = s * CHUNK + field - HALO * parity
+            start = position(s, groups) * CHUNK + field - HALO * parity
             inside = min(max(start, 0), total - TILE)
             rows = received[inside : inside + TILE]
             return rows if inside == start else pltpu.roll(rows, (inside - start) % TILE, 0)
@@ -304,7 +310,8 @@
     for parity in range(2):
         pl.when(core() == parity)(functools.partial(body, parity))
     for s in range(groups):
-        well_rows[s : s + 1] = received[s * CHUNK + WELL_ROW : s * CHUNK + WELL_ROW + 1]
+        at = position(s, groups) * CHUNK + WELL_ROW
+        well_rows[s : s + 1] = received[at : at + 1]
 
 
 def solver(diag, link, levels):
@@ -450,7 +457,8 @@
         out_hbm=1,
         aliases={8: 0},
     )
-    received = lax.all_to_all(packed, "gx", split_axis=0, concat_axis=0, tiled=True)
+    order = sorted(range(groups), key=lambda device: position(device, groups))
+    received = lax.all_to_all(packed, "gx", split_axis=0, concat_axis=0, axis_index_groups=[order], tiled=True)
     from_outside = lax.ppermute(outer, "gx", outer_pairs)
     (partial,) = call(
         sat_kernel, [box],

time: 30.1 us -> 31.2 us (1.037)
  waiting for transfers between devices: 15.3 us -> 16.2 us
    all_to_all x1, waiting for transfers between devices: 14.7 us -> 15.8 us  [on_device(): lax.all_to_all(packed, 'gx', split_axis=0, concat_axis=0, axis_index_grou...]
  transfers between devices with their start and end apart: 4 -> 4, of which waited for: 2 -> 2; matrix products, arithmetic and copies ran while one was open for 0% -> 0% of each run, Pallas kernels for 8% -> 7%
where the time goes in v8:
time: 31.2 us; the launch traced here: 30.9 us
  waiting for transfers between devices  16.2 us (52%)
  starting transfers between devices  8.6 us (28%)
  Pallas kernels  5.37 us (17%)
  between operations  0.71 us (2%)
    all_to_all x1, waiting for transfers between devices, on_device(): lax.all_to_all(packed, 'gx', split_axis=0, concat_axis=0, axis_index_grou...  15.8 us
    all_to_all x1, starting transfers between devices, on_device(): lax.all_to_all(packed, 'gx', split_axis=0, concat_axis=0, axis_index_grou...  7.08 us
    pallas_call x7, Pallas kernels, call(): pl.pallas_call(kernel, out_shape=tuple((shaped(o, place) if isinstance(o,...  5.37 us
    ppermute x1, starting transfers between devices, on_device(): from_outside = lax.ppermute(outer, 'gx', outer_pairs)  0.66 us
  transfers between devices with their start and end apart: 4, of which 2 were waited for; matrix products, arithmetic and copies ran while one was open for 0% of the time, Pallas kernels for 7%

profile of v8, /device:TPU:0, one launch (start us, length us, event | category | flops | bytes accessed | tf_op | source)
XLA Modules:
  0.0 30.9 jit_solution(14835133132505698817)
XLA Ops:
  0.6 1.1 %shard_map.139 = (f32[2,32,128]{2,1,0:T(8,128)S(1)}, f32[2,32,128]{2,1,0:T(8,128)S(1)}, f32[2,32,128]{2,1,0:T(8,128)S(1)}, f32[2,32,128]{2,1,0:T(8,128)S(1)}, f3...) custom-call(f32[2,32,128]{2,1,0:T(8,128)} %refs_0_.1, ...), custom_call_target="tpu_custom_call" | custom-call | tf_op jit(solution)/shard_map/pallas_call | solution.py:409
  1.8 0.5 %collective-permute-start = (f32[5,32,128]{2,1,0:T(8,128)S(1)}, f32[5,32,128]{2,1,0:T(8,128)S(1)}, u32[]{:S(2)}, u32[]{:S(2)}) collective-permute-start(f32[5,32,128]{2,1,0:T(8,128)S(1)} %get-tuple-element.40), channel_id=1, source_target_pairs={{0,1},{1,0},{2,3},{3,2},{4,5},{5,4},{6,7},{7,6},{8,9},{9,8},{10,11... | collective-permute-start | bytes 245768 | tf_op jit(solution)/shard_map/ppermute | solution.py:442
  2.3 1.1 %shard_map.140 = (f32[32,128]{1,0:T(8,128)S(1)}, f32[32,128]{1,0:T(8,128)S(1)}, f32[4,32,128]{2,1,0:T(8,128)S(1)}, f32[64,128]{1,0:T(8,128)S(1)}, f32[16,128]{1,0:T(8,128)S(1)}, /*index=5*/f32[16,72,128]{2,1,0:T(8,128)}) custom-call(f32[2,32,128]{2,1,0:T(8,128)S(1)} %get-tuple-element.27.press, f32[2,32,128]{2,1,0:T(8,128)S(1)} %get-tuple-element.28.sat, ...), custom_call_target="tpu_custom_call" | custom-call | tf_op jit(solution)/shard_map/pallas_call | solution.py:409
  3.4 0.0 collective-permute-done.from_chip
  3.4 0.7 %shard_map.142 = f32[16,72,128]{2,1,0:T(8,128)} custom-call(f32[2,32,128]{2,1,0:T(8,128)S(1)} %get-tuple-element.28.sat, f32[2,32,128]{2,1,0:T(8,128)S(1)} %get-tuple-element.29.lamw, f32[2,32,128]{2,1,0:T(8,128)S(1)} %get-tuple-element.30.lamo, f32[2,32,128]{2,1,0:T(8,128)S(1)} %get-tuple-element.31.permx, ...), custom_call_target="tpu_custom_call", output_to_operand_aliasing={{}: (8, {})} | custom-call | tf_op jit(solution)/shard_map/pallas_call | solution.py:409
  4.2 7.1 %all-to-all-start = ((f32[16,72,128]{2,1,0:T(8,128)}), f32[16,72,128]{2,1,0:T(8,128)S(1)}, u32[]{:S(2)}, u32[]{:S(2)}) async-start(f32[16,72,128]{2,1,0:T(8,128)} %shard_map.142), calls=%async_computation | async-start | bytes 1179648 | tf_op jit(solution)/shard_map/all_to_all | solution.py:461
  11.2 0.7 %collective-permute-start.1 = (f32[4,32,128]{2,1,0:T(8,128)S(1)}, f32[4,32,128]{2,1,0:T(8,128)S(1)}, u32[]{:S(2)}, u32[]{:S(2)}) collective-permute-start(f32[4,32,128]{2,1,0:T(8,128)S(1)} %get-tuple-element.41), channel_id=1, source_target_pairs={{1,2},{2,1},{3,4},{4,3},{5,6},{6,5},{7,8},{8,7},{9,10},{10,9},{11,... | collective-permute-start | bytes 196616 | tf_op jit(solution)/shard_map/ppermute | solution.py:462
  11.9 0.0 collective-permute-done.1.from_outside
  11.9 0.2 shard_map.141._.partial
  12.1 15.8 %all-to-all-done = f32[16,72,128]{2,1,0:T(8,128)S(1)} async-done(((f32[16,72,128]{2,1,0:T(8,128)}), f32[16,72,128]{2,1,0:T(8,128)S(1)}, u32[]{:S(2)}, u32[]{:S(2)}) %all-to-all-start) | async-done | bytes 589856 | tf_op jit(solution)/shard_map/all_to_all | solution.py:461
  28.0 0.1 shard_map.143
  28.0 0.3 %collective-permute-start.2 = (f32[640,128]{1,0:T(8,128)S(1)}, f32[640,128]{1,0:T(8,128)S(1)}, u32[]{:S(2)}, u32[]{:S(2)}) collective-permute-start(f32[640,128]{1,0:T(8,128)S(1)} %get-tuple-element.50), channel_id=1, source_target_pairs={{0,1},{1,0},{2,3},{3,2},{4,5},{5,4},{6,7},{7,6},{8,9},{9,8},{10,11... | collective-permute-start | bytes 983048 | tf_op jit(solution)/shard_map/ppermute | solution.py:475
  28.4 1.0 %shard_map.144 = (f32[2,32,128]{2,1,0:T(8,128)}, f32[1,16]{1,0:T(1,128)}) custom-call(f32[2,32,128]{2,1,0:T(8,128)S(1)} %shard_map.141._.partial, f32[2,32,128]{2,1,0:T(8,128)S(1)} %get-tuple-element.28.sat, f32[2,32,128]{2,1,0:T(8,128)S(1)} %get-tuple-element.29.lamw, f32[2,32,128]{2,1,0:T(8,128)S(1)} %get-tuple-element.30.lamo, ...), custom_call_target="tpu_custom_call" | custom-call | tf_op jit(solution)/shard_map/pallas_call | solution.py:409
  29.3 0.4 %collective-permute-done.2.other = f32[640,128]{1,0:T(8,128)S(1)} collective-permute-done((f32[640,128]{1,0:T(8,128)S(1)}, f32[640,128]{1,0:T(8,128)S(1)}, u32[]{:S(2)}, u32[]{:S(2)}) %collective-permute-start.2) | collective-permute-done | bytes 327712 | tf_op jit(solution)/shard_map/ppermute | solution.py:475
  29.7 1.2 %shard_map.145 = f32[2,32,128]{2,1,0:T(8,128)} custom-call(f32[5,256,128]{2,1,0:T(8,128)S(1)} %get-tuple-element.49.own, f32[640,128]{1,0:T(8,128)S(1)} %collective-permute-done.2.other), custom_call_target="tpu_custom_call" | custom-call | tf_op jit(solution)/shard_map/pallas_call | solution.py:409
Async XLA Ops:
  1.8 1.6 %collective-permute-start = (f32[5,32,128]{2,1,0:T(8,128)S(1)}, f32[5,32,128]{2,1,0:T(8,128)S(1)}, u32[]{:S(2)}, u32[]{:S(2)}) collective-permute-start(f32[5,32,128]{2,1,0:T(8,128)S(1)} %get-tuple-element.40), channel_id=1, source_target_pairs={{0,1},{1,0},{2,3},{3,2},{4,5},{5,4},{6,7},{7,6},{8,9},{9,8},{10,11... | collective-permute-start | bytes 245768 | tf_op jit(solution)/shard_map/ppermute | solution.py:442
  4.2 23.8 %all-to-all-start = ((f32[16,72,128]{2,1,0:T(8,128)}), f32[16,72,128]{2,1,0:T(8,128)S(1)}, u32[]{:S(2)}, u32[]{:S(2)}) async-start(f32[16,72,128]{2,1,0:T(8,128)} %shard_map.142), calls=%async_computation | async-start | bytes 1179648 | tf_op jit(solution)/shard_map/all_to_all | solution.py:461
  11.2 0.7 %collective-permute-start.1 = (f32[4,32,128]{2,1,0:T(8,128)S(1)}, f32[4,32,128]{2,1,0:T(8,128)S(1)}, u32[]{:S(2)}, u32[]{:S(2)}) collective-permute-start(f32[4,32,128]{2,1,0:T(8,128)S(1)} %get-tuple-element.41), channel_id=1, source_target_pairs={{1,2},{2,1},{3,4},{4,3},{5,6},{6,5},{7,8},{8,7},{9,10},{10,9},{11,... | collective-permute-start | bytes 196616 | tf_op jit(solution)/shard_map/ppermute | solution.py:462
  28.0 1.7 %collective-permute-start.2 = (f32[640,128]{1,0:T(8,128)S(1)}, f32[640,128]{1,0:T(8,128)S(1)}, u32[]{:S(2)}, u32[]{:S(2)}) collective-permute-start(f32[640,128]{1,0:T(8,128)S(1)} %get-tuple-element.50), channel_id=1, source_target_pairs={{0,1},{1,0},{2,3},{3,2},{4,5},{5,4},{6,7},{7,6},{8,9},{9,8},{10,11... | collective-permute-start | bytes 983048 | tf_op jit(solution)/shard_map/ppermute | solution.py:475

commit v9 on v8

--- a/solution.py
+++ b/solution.py
@@ -102,8 +102,7 @@
 
 
 def position(device, groups):
-    half = groups // 2
-    return 2 * (device % half) + device // half
+    return groups - 1 - device
 
 
 def for_chunks(groups, store):

time: 31.2 us -> 30.3 us (0.971)
  waiting for transfers between devices: 16.2 us -> 13.2 us
  starting transfers between devices: 8.6 us -> 10.7 us
    all_to_all x1, waiting for transfers between devices: 15.8 us -> 12.9 us  [on_device(): lax.all_to_all(packed, 'gx', split_axis=0, concat_axis=0, axis_index_grou...]
    all_to_all x1, starting transfers between devices: 7.08 us -> 9.14 us  [on_device(): lax.all_to_all(packed, 'gx', split_axis=0, concat_axis=0, axis_index_grou...]
where the time goes in v9:
time: 30.3 us; the launch traced here: 30 us
  waiting for transfers between devices  13.2 us (44%)
  starting transfers between devices  10.7 us (35%)
  Pallas kernels  5.37 us (18%)
  between operations  0.7 us (2%)
    all_to_all x1, waiting for transfers between devices, on_device(): lax.all_to_all(packed, 'gx', split_axis=0, concat_axis=0, axis_index_grou...  12.9 us
    all_to_all x1, starting transfers between devices, on_device(): lax.all_to_all(packed, 'gx', split_axis=0, concat_axis=0, axis_index_grou...  9.14 us
    pallas_call x7, Pallas kernels, call(): pl.pallas_call(kernel, out_shape=tuple((shaped(o, place) if isinstance(o,...  5.37 us
    ppermute x1, starting transfers between devices, on_device(): from_outside = lax.ppermute(outer, 'gx', outer_pairs)  0.65 us
  transfers between devices with their start and end apart: 4, of which 2 were waited for; matrix products, arithmetic and copies ran while one was open for 0% of the time, Pallas kernels for 7%

profile of v9, /device:TPU:0, one launch (start us, length us, event | category | flops | bytes accessed | tf_op | source)
XLA Modules:
  0.0 30.0 jit_solution(11188298830747486801)
XLA Ops:
  0.6 1.1 %shard_map.139 = (f32[2,32,128]{2,1,0:T(8,128)S(1)}, f32[2,32,128]{2,1,0:T(8,128)S(1)}, f32[2,32,128]{2,1,0:T(8,128)S(1)}, f32[2,32,128]{2,1,0:T(8,128)S(1)}, f3...) custom-call(f32[2,32,128]{2,1,0:T(8,128)} %refs_0_.1, ...), custom_call_target="tpu_custom_call" | custom-call | tf_op jit(solution)/shard_map/pallas_call | solution.py:408
  1.8 0.5 %collective-permute-start = (f32[5,32,128]{2,1,0:T(8,128)S(1)}, f32[5,32,128]{2,1,0:T(8,128)S(1)}, u32[]{:S(2)}, u32[]{:S(2)}) collective-permute-start(f32[5,32,128]{2,1,0:T(8,128)S(1)} %get-tuple-element.40), channel_id=1, source_target_pairs={{0,1},{1,0},{2,3},{3,2},{4,5},{5,4},{6,7},{7,6},{8,9},{9,8},{10,11... | collective-permute-start | bytes 245768 | tf_op jit(solution)/shard_map/ppermute | solution.py:441
  2.3 1.1 %shard_map.140 = (f32[32,128]{1,0:T(8,128)S(1)}, f32[32,128]{1,0:T(8,128)S(1)}, f32[4,32,128]{2,1,0:T(8,128)S(1)}, f32[64,128]{1,0:T(8,128)S(1)}, f32[16,128]{1,0:T(8,128)S(1)}, /*index=5*/f32[16,72,128]{2,1,0:T(8,128)}) custom-call(f32[2,32,128]{2,1,0:T(8,128)S(1)} %get-tuple-element.27.press, f32[2,32,128]{2,1,0:T(8,128)S(1)} %get-tuple-element.28.sat, ...), custom_call_target="tpu_custom_call" | custom-call | tf_op jit(solution)/shard_map/pallas_call | solution.py:408
  3.4 0.0 collective-permute-done.from_chip
  3.4 0.7 %shard_map.142 = f32[16,72,128]{2,1,0:T(8,128)} custom-call(f32[2,32,128]{2,1,0:T(8,128)S(1)} %get-tuple-element.28.sat, f32[2,32,128]{2,1,0:T(8,128)S(1)} %get-tuple-element.29.lamw, f32[2,32,128]{2,1,0:T(8,128)S(1)} %get-tuple-element.30.lamo, f32[2,32,128]{2,1,0:T(8,128)S(1)} %get-tuple-element.31.permx, ...), custom_call_target="tpu_custom_call", output_to_operand_aliasing={{}: (8, {})} | custom-call | tf_op jit(solution)/shard_map/pallas_call | solution.py:408
  4.2 9.1 %all-to-all-start = ((f32[16,72,128]{2,1,0:T(8,128)}), f32[16,72,128]{2,1,0:T(8,128)S(1)}, u32[]{:S(2)}, u32[]{:S(2)}) async-start(f32[16,72,128]{2,1,0:T(8,128)} %shard_map.142), calls=%async_computation | async-start | bytes 1179648 | tf_op jit(solution)/shard_map/all_to_all | solution.py:460
  13.3 0.7 %collective-permute-start.1 = (f32[4,32,128]{2,1,0:T(8,128)S(1)}, f32[4,32,128]{2,1,0:T(8,128)S(1)}, u32[]{:S(2)}, u32[]{:S(2)}) collective-permute-start(f32[4,32,128]{2,1,0:T(8,128)S(1)} %get-tuple-element.41), channel_id=1, source_target_pairs={{1,2},{2,1},{3,4},{4,3},{5,6},{6,5},{7,8},{8,7},{9,10},{10,9},{11,... | collective-permute-start | bytes 196616 | tf_op jit(solution)/shard_map/ppermute | solution.py:461
  14.0 0.0 collective-permute-done.1.from_outside
  14.0 0.2 shard_map.141._.partial
  14.1 12.9 %all-to-all-done = f32[16,72,128]{2,1,0:T(8,128)S(1)} async-done(((f32[16,72,128]{2,1,0:T(8,128)}), f32[16,72,128]{2,1,0:T(8,128)S(1)}, u32[]{:S(2)}, u32[]{:S(2)}) %all-to-all-start) | async-done | bytes 589856 | tf_op jit(solution)/shard_map/all_to_all | solution.py:460
  27.0 0.1 shard_map.143
  27.1 0.4 %collective-permute-start.2 = (f32[640,128]{1,0:T(8,128)S(1)}, f32[640,128]{1,0:T(8,128)S(1)}, u32[]{:S(2)}, u32[]{:S(2)}) collective-permute-start(f32[640,128]{1,0:T(8,128)S(1)} %get-tuple-element.50), channel_id=1, source_target_pairs={{0,1},{1,0},{2,3},{3,2},{4,5},{5,4},{6,7},{7,6},{8,9},{9,8},{10,11... | collective-permute-start | bytes 983048 | tf_op jit(solution)/shard_map/ppermute | solution.py:474
  27.5 1.0 %shard_map.144 = (f32[2,32,128]{2,1,0:T(8,128)}, f32[1,16]{1,0:T(1,128)}) custom-call(f32[2,32,128]{2,1,0:T(8,128)S(1)} %shard_map.141._.partial, f32[2,32,128]{2,1,0:T(8,128)S(1)} %get-tuple-element.28.sat, f32[2,32,128]{2,1,0:T(8,128)S(1)} %get-tuple-element.29.lamw, f32[2,32,128]{2,1,0:T(8,128)S(1)} %get-tuple-element.30.lamo, ...), custom_call_target="tpu_custom_call" | custom-call | tf_op jit(solution)/shard_map/pallas_call | solution.py:408
  28.5 0.3 %collective-permute-done.2.other = f32[640,128]{1,0:T(8,128)S(1)} collective-permute-done((f32[640,128]{1,0:T(8,128)S(1)}, f32[640,128]{1,0:T(8,128)S(1)}, u32[]{:S(2)}, u32[]{:S(2)}) %collective-permute-start.2) | collective-permute-done | bytes 327712 | tf_op jit(solution)/shard_map/ppermute | solution.py:474
  28.8 1.2 %shard_map.145 = f32[2,32,128]{2,1,0:T(8,128)} custom-call(f32[5,256,128]{2,1,0:T(8,128)S(1)} %get-tuple-element.49.own, f32[640,128]{1,0:T(8,128)S(1)} %collective-permute-done.2.other), custom_call_target="tpu_custom_call" | custom-call | tf_op jit(solution)/shard_map/pallas_call | solution.py:408
Async XLA Ops:
  1.8 1.6 %collective-permute-start = (f32[5,32,128]{2,1,0:T(8,128)S(1)}, f32[5,32,128]{2,1,0:T(8,128)S(1)}, u32[]{:S(2)}, u32[]{:S(2)}) collective-permute-start(f32[5,32,128]{2,1,0:T(8,128)S(1)} %get-tuple-element.40), channel_id=1, source_target_pairs={{0,1},{1,0},{2,3},{3,2},{4,5},{5,4},{6,7},{7,6},{8,9},{9,8},{10,11... | collective-permute-start | bytes 245768 | tf_op jit(solution)/shard_map/ppermute | solution.py:441
  4.2 22.9 %all-to-all-start = ((f32[16,72,128]{2,1,0:T(8,128)}), f32[16,72,128]{2,1,0:T(8,128)S(1)}, u32[]{:S(2)}, u32[]{:S(2)}) async-start(f32[16,72,128]{2,1,0:T(8,128)} %shard_map.142), calls=%async_computation | async-start | bytes 1179648 | tf_op jit(solution)/shard_map/all_to_all | solution.py:460
  13.3 0.7 %collective-permute-start.1 = (f32[4,32,128]{2,1,0:T(8,128)S(1)}, f32[4,32,128]{2,1,0:T(8,128)S(1)}, u32[]{:S(2)}, u32[]{:S(2)}) collective-permute-start(f32[4,32,128]{2,1,0:T(8,128)S(1)} %get-tuple-element.41), channel_id=1, source_target_pairs={{1,2},{2,1},{3,4},{4,3},{5,6},{6,5},{7,8},{8,7},{9,10},{10,9},{11,... | collective-permute-start | bytes 196616 | tf_op jit(solution)/shard_map/ppermute | solution.py:461
  27.1 1.7 %collective-permute-start.2 = (f32[640,128]{1,0:T(8,128)S(1)}, f32[640,128]{1,0:T(8,128)S(1)}, u32[]{:S(2)}, u32[]{:S(2)}) collective-permute-start(f32[640,128]{1,0:T(8,128)S(1)} %get-tuple-element.50), channel_id=1, source_target_pairs={{0,1},{1,0},{2,3},{3,2},{4,5},{5,4},{6,7},{7,6},{8,9},{9,8},{10,11... | collective-permute-start | bytes 983048 | tf_op jit(solution)/shard_map/ppermute | solution.py:474

commit v10 on v7

--- a/solution.py
+++ b/solution.py
@@ -18,9 +18,9 @@
 HALO = 3
 ROWS = 5
 NEAR_RHS, NEAR_DIAG, CHIP, WELL_ROW = 0, 5, 10, 15
-REST = 16
-FAR_RHS, FAR_DIAG, CY, CZ, INNER, SAT, LAMW, LAMO, PERMX = (REST + ROWS * i for i in (0, 1, 2, 4, 6, 7, 8, 9, 10))
-CHUNK = REST + 11 * ROWS + 1
+LATE = 16
+FAR_RHS, FAR_DIAG, CY, CZ, INNER, SAT, LAMW, LAMO, PERMX = (ROWS * i for i in (0, 1, 2, 4, 6, 7, 8, 9, 10))
+EARLY = 11 * ROWS + 1
 
 
 def mobilities(s):
@@ -151,7 +151,7 @@
     values = [jnp.where(first, rhs[0], rhs[1]), jnp.where(first, diag[0], diag[1]), *couplings[0], *couplings[1], inner]
     values += [sat[far], lamw[far], lamo[far], permx[far]]
     for f, value in enumerate(values):
-        pad(padded.at[f], value, 1.0 if REST + f * ROWS in (FAR_DIAG, PERMX) else 0.0)
+        pad(padded.at[f], value, 1.0 if f * ROWS in (FAR_DIAG, PERMX) else 0.0)
 
     def store(d, start):
         for f in range(len(values)):
@@ -159,7 +159,7 @@
         chunks[d, len(values) * ROWS :] = jnp.zeros((1, LANES), jnp.float32)
 
     for_chunks(groups, store)
-    copy = pltpu.make_async_copy(chunks, packed.at[:, REST:], sem)
+    copy = pltpu.make_async_copy(chunks, packed, sem)
     copy.start()
 
     for i, ref in enumerate((press, lamw, lamo, permx)):
@@ -176,7 +176,7 @@
     copy.wait()
 
 
-def pack_kernel(groups, sat, lamw, lamo, permx, from_chip, near_rhs, near_diag, well_rows, _, packed, padded, chunks, sem):
+def pack_kernel(groups, sat, lamw, lamo, permx, from_chip, near_rhs, near_diag, well_rows, packed, padded):
     near = 1 - core()
     k, kn = permx[near], from_chip[4]
     here = (lamw[near], lamo[near], *mobilities(sat[near]))
@@ -187,13 +187,10 @@
 
     def store(d, start):
         for i in range(3):
-            chunks[d, i * ROWS : (i + 1) * ROWS] = padded[i, pl.ds(start, ROWS)]
-        chunks[d, WELL_ROW : WELL_ROW + 1] = well_rows[pl.ds(d, 1)]
+            packed[d, i * ROWS : (i + 1) * ROWS] = padded[i, pl.ds(start, ROWS)]
+        packed[d, WELL_ROW : WELL_ROW + 1] = well_rows[pl.ds(d, 1)]
 
     for_chunks(groups, store)
-    copy = pltpu.make_async_copy(chunks, packed.at[:, :REST], sem)
-    copy.start()
-    copy.wait()
 
 
 def sat_parts(here, there, trans):
@@ -256,17 +253,19 @@
     return lax.broadcasted_iota(jnp.int32, (TILE, LANES), 0)
 
 
-def face_kernel(received, _, own, send, well_rows):
-    total = received.shape[0]
-    groups = total // CHUNK
+def face_kernel(early, late, _, own, send, well_rows):
+    groups = early.shape[0] // EARLY
     low = sublane() < 4
 
     def body(parity):
-        def tile(s, field):
-            start = s * CHUNK + field - HALO * parity
-            inside = min(max(start, 0), total - TILE)
-            rows = received[inside : inside + TILE]
+        def tile(s, field, source=early, chunk=EARLY):
+            start = s * chunk + field - HALO * parity
+            inside = min(max(start, 0), groups * chunk - TILE)
+            rows = source[inside : inside + TILE]
             return rows if inside == start else pltpu.roll(rows, (inside - start) % TILE, 0)
+
+        def late_tile(s, field):
+            return tile(s, field, late, LATE)
 
         count = 2 * groups
         below = None
@@ -274,14 +273,15 @@
         for x in range(count):
             s = x // 2
             near = x % 4 in (1, 2)
-            rhs, diag = tile(s, NEAR_RHS if near else FAR_RHS), tile(s, NEAR_DIAG if near else FAR_DIAG)
+            rhs = late_tile(s, NEAR_RHS) if near else tile(s, FAR_RHS)
+            diag = late_tile(s, NEAR_DIAG) if near else tile(s, FAR_DIAG)
             if below is not None:
                 rhs, diag = rhs - below[0], diag + below[1]
             below = None
             if x % 2 == 0:
                 link = tile(s, INNER)
             elif x % 4 == 1:
-                link = tile(s, CHIP)
+                link = late_tile(s, CHIP)
             elif x < count - 1:
                 here, there = (
                     (tile(t, LAMW), tile(t, LAMO), *mobilities(tile(t, SAT)), tile(t, PERMX)) for t in (s, s + 1)
@@ -304,7 +304,7 @@
     for parity in range(2):
         pl.when(core() == parity)(functools.partial(body, parity))
     for s in range(groups):
-        well_rows[s : s + 1] = received[s * CHUNK + WELL_ROW : s * CHUNK + WELL_ROW + 1]
+        well_rows[s : s + 1] = late[s * LATE + WELL_ROW : s * LATE + WELL_ROW + 1]
 
 
 def solver(diag, link, levels):
@@ -391,7 +391,7 @@
             out[y, x : x + 1] = u[x][HALO + y : HALO + y + 1]
 
 
-def call(kernel, outs, *args, scratch=(), in_hbm=0, out_hbm=0, aliases=None):
+def call(kernel, outs, *args, scratch=(), in_hbm=0, out_hbm=0):
     places = [pltpu.VMEM] * (len(args) - in_hbm) + [pltpu.HBM] * in_hbm
     args = [pltpu.with_memory_space_constraint(v, place) if place == pltpu.HBM else v for v, place in zip(args, places)]
     results = [pltpu.VMEM] * (len(outs) - out_hbm) + [pltpu.HBM] * out_hbm
@@ -405,7 +405,6 @@
         in_specs=[pl.BlockSpec(memory_space=place) for place in places],
         out_specs=tuple(pl.BlockSpec(memory_space=place) for place in results),
         scratch_shapes=[pltpu.VMEM(o, jnp.float32) if isinstance(o, tuple) else o for o in scratch],
-        input_output_aliases=aliases or {},
         compiler_params=pltpu.CompilerParams(vmem_limit_bytes=40 << 20),
     )(*args)
 
@@ -434,23 +433,20 @@
     press, sat, lamw, lamo, permx, permy, permz, pore, cell, well, index, bhp = loaded
     from_chip = lax.ppermute(chip_edge, "gx", chip_pairs)
     plane = (ny, LANES)
-    chunk = (groups, CHUNK, LANES)
     near_rhs, near_diag, outer, weight, well_rows, packed = call(
         functools.partial(cell_kernel, groups),
-        [plane, plane, (4, ny, LANES), (2 * ny, LANES), (groups, LANES), chunk],
+        [plane, plane, (4, ny, LANES), (2 * ny, LANES), (groups, LANES), (groups, EARLY, LANES)],
         press, sat, lamw, lamo, permx, permy, permz, pore, cell, well, index, bhp,
-        scratch=[(11, ny + 2 * TILE, LANES), (groups, CHUNK - REST, LANES), pltpu.SemaphoreType.DMA],
+        scratch=[(11, ny + 2 * TILE, LANES), (groups, EARLY, LANES), pltpu.SemaphoreType.DMA],
         out_hbm=1,
     )
+    early = lax.all_to_all(packed, "gx", split_axis=0, concat_axis=0, tiled=True)
     (packed,) = call(
-        functools.partial(pack_kernel, groups), [chunk],
-        sat, lamw, lamo, permx, from_chip, near_rhs, near_diag, well_rows, packed,
-        scratch=[(3, ny + 2 * TILE, LANES), (groups, REST, LANES), pltpu.SemaphoreType.DMA],
-        in_hbm=1,
-        out_hbm=1,
-        aliases={8: 0},
-    )
-    received = lax.all_to_all(packed, "gx", split_axis=0, concat_axis=0, tiled=True)
+        functools.partial(pack_kernel, groups), [(groups, LATE, LANES)],
+        sat, lamw, lamo, permx, from_chip, near_rhs, near_diag, well_rows,
+        scratch=[(3, ny + 2 * TILE, LANES)],
+    )
+    late = lax.all_to_all(packed, "gx", split_axis=0, concat_axis=0, tiled=True)
     from_outside = lax.ppermute(outer, "gx", outer_pairs)
     (partial,) = call(
         sat_kernel, [box],
@@ -461,7 +457,8 @@
     own, send, well_rows = call(
         face_kernel,
         [(5, count * TILE, LANES), (5 * count // 2 * TILE, LANES), (groups, LANES)],
-        received.reshape(groups * CHUNK, LANES),
+        early.reshape(groups * EARLY, LANES),
+        late.reshape(groups * LATE, LANES),
         partial,
     )
     other = lax.ppermute(send, "gx", chip_pairs)

time: 30.1 us -> 38.4 us (1.28)
  blocking collectives: 0 us -> 14.8 us
  starting transfers between devices: 8.34 us -> 4.92 us
  waiting for transfers between devices: 15.3 us -> 12.9 us
  Pallas kernels: 5.37 us -> 4.7 us
    all_to_all x0 -> x1, blocking collectives: none -> 14.8 us  [on_device(): late = lax.all_to_all(packed, 'gx', split_axis=0, concat_axis=0, tiled=True)]
    all_to_all x1, starting transfers between devices: 7.08 us -> 3.56 us  [on_device(): lax.all_to_all(packed, 'gx', split_axis=0, concat_axis=0, tiled=True)]
    all_to_all x1, waiting for transfers between devices: 14.7 us -> 12.3 us  [on_device(): lax.all_to_all(packed, 'gx', split_axis=0, concat_axis=0, tiled=True)]
    pallas_call x7, Pallas kernels: 5.37 us -> 4.7 us  [call(): pl.pallas_call(kernel, out_shape=tuple((shaped(o, place) if isinstance(o,...]
  transfers between devices with their start and end apart: 4 -> 4, of which waited for: 2 -> 2; matrix products, arithmetic and copies ran while one was open for 0% -> 0% of each run, Pallas kernels for 8% -> 6%
where the time goes in v10:
time: 38.4 us; the launch traced here: 38 us
  blocking collectives  14.8 us (39%)
  waiting for transfers between devices  12.9 us (34%)
  starting transfers between devices  4.92 us (13%)
  Pallas kernels  4.7 us (12%)
  between operations  0.71 us (2%)
    all_to_all x1, blocking collectives, on_device(): late = lax.all_to_all(packed, 'gx', split_axis=0, concat_axis=0, tiled=True)  14.8 us
    all_to_all x1, waiting for transfers between devices, on_device(): lax.all_to_all(packed, 'gx', split_axis=0, concat_axis=0, tiled=True)  12.3 us
    pallas_call x7, Pallas kernels, call(): pl.pallas_call(kernel, out_shape=tuple((shaped(o, place) if isinstance(o,...  4.7 us
    all_to_all x1, starting transfers between devices, on_device(): lax.all_to_all(packed, 'gx', split_axis=0, concat_axis=0, tiled=True)  3.56 us
  transfers between devices with their start and end apart: 4, of which 2 were waited for; matrix products, arithmetic and copies ran while one was open for 0% of the time, Pallas kernels for 6%

profile of v10, /device:TPU:0, one launch (start us, length us, event | category | flops | bytes accessed | tf_op | source)
XLA Modules:
  0.0 38.0 jit_solution(13034393368611226096)
XLA Ops:
  0.6 1.1 %shard_map.139 = (f32[2,32,128]{2,1,0:T(8,128)S(1)}, f32[2,32,128]{2,1,0:T(8,128)S(1)}, f32[2,32,128]{2,1,0:T(8,128)S(1)}, f32[2,32,128]{2,1,0:T(8,128)S(1)}, f3...) custom-call(f32[2,32,128]{2,1,0:T(8,128)} %refs_0_.1, ...), custom_call_target="tpu_custom_call" | custom-call | tf_op jit(solution)/shard_map/pallas_call | solution.py:402
  1.8 0.5 %collective-permute-start = (f32[5,32,128]{2,1,0:T(8,128)S(1)}, f32[5,32,128]{2,1,0:T(8,128)S(1)}, u32[]{:S(2)}, u32[]{:S(2)}) collective-permute-start(f32[5,32,128]{2,1,0:T(8,128)S(1)} %get-tuple-element.40), channel_id=1, source_target_pairs={{0,1},{1,0},{2,3},{3,2},{4,5},{5,4},{6,7},{7,6},{8,9},{9,8},{10,11... | collective-permute-start | bytes 245768 | tf_op jit(solution)/shard_map/ppermute | solution.py:434
  2.3 1.1 %shard_map.140 = (f32[32,128]{1,0:T(8,128)S(1)}, f32[32,128]{1,0:T(8,128)S(1)}, f32[4,32,128]{2,1,0:T(8,128)S(1)}, f32[64,128]{1,0:T(8,128)S(1)}, f32[16,128]{1,0:T(8,128)S(1)}, /*index=5*/f32[16,56,128]{2,1,0:T(8,128)}) custom-call(f32[2,32,128]{2,1,0:T(8,128)S(1)} %get-tuple-element.27.press, f32[2,32,128]{2,1,0:T(8,128)S(1)} %get-tuple-element.28.sat, ...), custom_call_target="tpu_custom_call" | custom-call | tf_op jit(solution)/shard_map/pallas_call | solution.py:402
  3.4 0.0 collective-permute-done.from_chip
  3.5 14.8 %all_to_all.10 = f32[16,16,128]{2,1,0:T(8,128)S(1)} all-to-all(f32[16,16,128]{2,1,0:T(8,128)S(1)} %shard_map.142), channel_id=1, replica_groups=mesh['members'=2,'gx'=16] {'gx'}, dimensions={0} | all-to-all | bytes 262144 | tf_op jit(solution)/shard_map/all_to_all | solution.py:449
  18.3 3.6 %all-to-all-start = ((f32[16,56,128]{2,1,0:T(8,128)}), f32[16,56,128]{2,1,0:T(8,128)S(1)}, u32[]{:S(2)}, u32[]{:S(2)}) async-start(f32[16,56,128]{2,1,0:T(8,128)} %get-tuple-element.42), calls=%async_computation | async-start | bytes 917504 | tf_op jit(solution)/shard_map/all_to_all | solution.py:443
  21.8 0.7 %collective-permute-start.1 = (f32[4,32,128]{2,1,0:T(8,128)S(1)}, f32[4,32,128]{2,1,0:T(8,128)S(1)}, u32[]{:S(2)}, u32[]{:S(2)}) collective-permute-start(f32[4,32,128]{2,1,0:T(8,128)S(1)} %get-tuple-element.41), channel_id=1, source_target_pairs={{1,2},{2,1},{3,4},{4,3},{5,6},{6,5},{7,8},{8,7},{9,10},{10,9},{11,... | collective-permute-start | bytes 196616 | tf_op jit(solution)/shard_map/ppermute | solution.py:450
  22.5 0.0 collective-permute-done.1.from_outside
  22.5 0.2 shard_map.141._.partial
  22.7 12.3 %all-to-all-done = f32[16,56,128]{2,1,0:T(8,128)S(1)} async-done(((f32[16,56,128]{2,1,0:T(8,128)}), f32[16,56,128]{2,1,0:T(8,128)S(1)}, u32[]{:S(2)}, u32[]{:S(2)}) %all-to-all-start) | async-done | bytes 458784 | tf_op jit(solution)/shard_map/all_to_all | solution.py:443
  35.1 0.1 shard_map.143
  35.1 0.2 collective-permute-start.2
  35.3 1.0 %shard_map.144 = (f32[2,32,128]{2,1,0:T(8,128)}, f32[1,16]{1,0:T(1,128)}) custom-call(f32[2,32,128]{2,1,0:T(8,128)S(1)} %shard_map.141._.partial, f32[2,32,128]{2,1,0:T(8,128)S(1)} %get-tuple-element.28.sat, f32[2,32,128]{2,1,0:T(8,128)S(1)} %get-tuple-element.29.lamw, f32[2,32,128]{2,1,0:T(8,128)S(1)} %get-tuple-element.30.lamo, ...), custom_call_target="tpu_custom_call" | custom-call | tf_op jit(solution)/shard_map/pallas_call | solution.py:402
  36.3 0.6 %collective-permute-done.2.other = f32[640,128]{1,0:T(8,128)S(1)} collective-permute-done((f32[640,128]{1,0:T(8,128)S(1)}, f32[640,128]{1,0:T(8,128)S(1)}, u32[]{:S(2)}, u32[]{:S(2)}) %collective-permute-start.2) | collective-permute-done | bytes 327712 | tf_op jit(solution)/shard_map/ppermute | solution.py:464
  36.8 1.2 %shard_map.145 = f32[2,32,128]{2,1,0:T(8,128)} custom-call(f32[5,256,128]{2,1,0:T(8,128)S(1)} %get-tuple-element.49.own, f32[640,128]{1,0:T(8,128)S(1)} %collective-permute-done.2.other), custom_call_target="tpu_custom_call" | custom-call | tf_op jit(solution)/shard_map/pallas_call | solution.py:402
  (1 shorter events, 0.0 us)
Async XLA Ops:
  1.8 1.6 %collective-permute-start = (f32[5,32,128]{2,1,0:T(8,128)S(1)}, f32[5,32,128]{2,1,0:T(8,128)S(1)}, u32[]{:S(2)}, u32[]{:S(2)}) collective-permute-start(f32[5,32,128]{2,1,0:T(8,128)S(1)} %get-tuple-element.40), channel_id=1, source_target_pairs={{0,1},{1,0},{2,3},{3,2},{4,5},{5,4},{6,7},{7,6},{8,9},{9,8},{10,11... | collective-permute-start | bytes 245768 | tf_op jit(solution)/shard_map/ppermute | solution.py:434
  18.3 16.8 %all-to-all-start = ((f32[16,56,128]{2,1,0:T(8,128)}), f32[16,56,128]{2,1,0:T(8,128)S(1)}, u32[]{:S(2)}, u32[]{:S(2)}) async-start(f32[16,56,128]{2,1,0:T(8,128)} %get-tuple-element.42), calls=%async_computation | async-start | bytes 917504 | tf_op jit(solution)/shard_map/all_to_all | solution.py:443
  21.8 0.7 %collective-permute-start.1 = (f32[4,32,128]{2,1,0:T(8,128)S(1)}, f32[4,32,128]{2,1,0:T(8,128)S(1)}, u32[]{:S(2)}, u32[]{:S(2)}) collective-permute-start(f32[4,32,128]{2,1,0:T(8,128)S(1)} %get-tuple-element.41), channel_id=1, source_target_pairs={{1,2},{2,1},{3,4},{4,3},{5,6},{6,5},{7,8},{8,7},{9,10},{10,9},{11,... | collective-permute-start | bytes 196616 | tf_op jit(solution)/shard_map/ppermute | solution.py:450
  35.1 1.7 %collective-permute-start.2 = (f32[640,128]{1,0:T(8,128)S(1)}, f32[640,128]{1,0:T(8,128)S(1)}, u32[]{:S(2)}, u32[]{:S(2)}) collective-permute-start(f32[640,128]{1,0:T(8,128)S(1)} %get-tuple-element.50), channel_id=1, source_target_pairs={{0,1},{1,0},{2,3},{3,2},{4,5},{5,4},{6,7},{7,6},{8,9},{9,8},{10,11... | collective-permute-start | bytes 983048 | tf_op jit(solution)/shard_map/ppermute | solution.py:464

commit v11 on v9

--- a/solution.py
+++ b/solution.py
@@ -102,7 +102,7 @@
 
 
 def position(device, groups):
-    return groups - 1 - device
+    return device % 4 * (groups // 4) + device // 4
 
 
 def for_chunks(groups, store):

time: 30.3 us -> 31.6 us (1.043)
  waiting for transfers between devices: 13.2 us -> 16.9 us
  starting transfers between devices: 10.7 us -> 8.33 us
    all_to_all x1, waiting for transfers between devices: 12.9 us -> 16.2 us  [on_device(): lax.all_to_all(packed, 'gx', split_axis=0, concat_axis=0, axis_index_grou...]
    all_to_all x1, starting transfers between devices: 9.14 us -> 7.08 us  [on_device(): lax.all_to_all(packed, 'gx', split_axis=0, concat_axis=0, axis_index_grou...]
    ppermute x1, starting transfers between devices: 0.43 us -> 0.07 us  [on_device(): other = lax.ppermute(send, 'gx', chip_pairs)]
    ppermute x1, waiting for transfers between devices: 0.3 us -> 0.65 us  [on_device(): other = lax.ppermute(send, 'gx', chip_pairs)]
where the time goes in v11:
time: 31.6 us; the launch traced here: 31.3 us
  waiting for transfers between devices  16.9 us (53%)
  starting transfers between devices  8.33 us (26%)
  Pallas kernels  5.37 us (17%)
  between operations  0.72 us (2%)
    all_to_all x1, waiting for transfers between devices, on_device(): lax.all_to_all(packed, 'gx', split_axis=0, concat_axis=0, axis_index_grou...  16.2 us
    all_to_all x1, starting transfers between devices, on_device(): lax.all_to_all(packed, 'gx', split_axis=0, concat_axis=0, axis_index_grou...  7.08 us
    pallas_call x7, Pallas kernels, call(): pl.pallas_call(kernel, out_shape=tuple((shaped(o, place) if isinstance(o,...  5.37 us
    ppermute x1, starting transfers between devices, on_device(): from_outside = lax.ppermute(outer, 'gx', outer_pairs)  0.66 us
    ppermute x1, waiting for transfers between devices, on_device(): other = lax.ppermute(send, 'gx', chip_pairs)  0.65 us
  transfers between devices with their start and end apart: 4, of which 2 were waited for; matrix products, arithmetic and copies ran while one was open for 0% of the time, Pallas kernels for 7%

profile of v11, /device:TPU:0, one launch (start us, length us, event | category | flops | bytes accessed | tf_op | source)
XLA Modules:
  0.0 31.3 jit_solution(11025792401910120725)
XLA Ops:
  0.6 1.1 %shard_map.139 = (f32[2,32,128]{2,1,0:T(8,128)S(1)}, f32[2,32,128]{2,1,0:T(8,128)S(1)}, f32[2,32,128]{2,1,0:T(8,128)S(1)}, f32[2,32,128]{2,1,0:T(8,128)S(1)}, f3...) custom-call(f32[2,32,128]{2,1,0:T(8,128)} %refs_0_.1, ...), custom_call_target="tpu_custom_call" | custom-call | tf_op jit(solution)/shard_map/pallas_call | solution.py:408
  1.8 0.5 %collective-permute-start = (f32[5,32,128]{2,1,0:T(8,128)S(1)}, f32[5,32,128]{2,1,0:T(8,128)S(1)}, u32[]{:S(2)}, u32[]{:S(2)}) collective-permute-start(f32[5,32,128]{2,1,0:T(8,128)S(1)} %get-tuple-element.40), channel_id=1, source_target_pairs={{0,1},{1,0},{2,3},{3,2},{4,5},{5,4},{6,7},{7,6},{8,9},{9,8},{10,11... | collective-permute-start | bytes 245768 | tf_op jit(solution)/shard_map/ppermute | solution.py:441
  2.3 1.1 %shard_map.140 = (f32[32,128]{1,0:T(8,128)S(1)}, f32[32,128]{1,0:T(8,128)S(1)}, f32[4,32,128]{2,1,0:T(8,128)S(1)}, f32[64,128]{1,0:T(8,128)S(1)}, f32[16,128]{1,0:T(8,128)S(1)}, /*index=5*/f32[16,72,128]{2,1,0:T(8,128)}) custom-call(f32[2,32,128]{2,1,0:T(8,128)S(1)} %get-tuple-element.27.press, f32[2,32,128]{2,1,0:T(8,128)S(1)} %get-tuple-element.28.sat, ...), custom_call_target="tpu_custom_call" | custom-call | tf_op jit(solution)/shard_map/pallas_call | solution.py:408
  3.4 0.0 collective-permute-done.from_chip
  3.4 0.7 %shard_map.142 = f32[16,72,128]{2,1,0:T(8,128)} custom-call(f32[2,32,128]{2,1,0:T(8,128)S(1)} %get-tuple-element.28.sat, f32[2,32,128]{2,1,0:T(8,128)S(1)} %get-tuple-element.29.lamw, f32[2,32,128]{2,1,0:T(8,128)S(1)} %get-tuple-element.30.lamo, f32[2,32,128]{2,1,0:T(8,128)S(1)} %get-tuple-element.31.permx, ...), custom_call_target="tpu_custom_call", output_to_operand_aliasing={{}: (8, {})} | custom-call | tf_op jit(solution)/shard_map/pallas_call | solution.py:408
  4.2 7.1 %all-to-all-start = ((f32[16,72,128]{2,1,0:T(8,128)}), f32[16,72,128]{2,1,0:T(8,128)S(1)}, u32[]{:S(2)}, u32[]{:S(2)}) async-start(f32[16,72,128]{2,1,0:T(8,128)} %shard_map.142), calls=%async_computation | async-start | bytes 1179648 | tf_op jit(solution)/shard_map/all_to_all | solution.py:460
  11.2 0.7 %collective-permute-start.1 = (f32[4,32,128]{2,1,0:T(8,128)S(1)}, f32[4,32,128]{2,1,0:T(8,128)S(1)}, u32[]{:S(2)}, u32[]{:S(2)}) collective-permute-start(f32[4,32,128]{2,1,0:T(8,128)S(1)} %get-tuple-element.41), channel_id=1, source_target_pairs={{1,2},{2,1},{3,4},{4,3},{5,6},{6,5},{7,8},{8,7},{9,10},{10,9},{11,... | collective-permute-start | bytes 196616 | tf_op jit(solution)/shard_map/ppermute | solution.py:461
  11.9 0.0 collective-permute-done.1.from_outside
  11.9 0.2 shard_map.141._.partial
  12.1 16.2 %all-to-all-done = f32[16,72,128]{2,1,0:T(8,128)S(1)} async-done(((f32[16,72,128]{2,1,0:T(8,128)}), f32[16,72,128]{2,1,0:T(8,128)S(1)}, u32[]{:S(2)}, u32[]{:S(2)}) %all-to-all-start) | async-done | bytes 589856 | tf_op jit(solution)/shard_map/all_to_all | solution.py:460
  28.3 0.1 shard_map.143
  28.4 0.1 collective-permute-start.2
  28.5 1.0 %shard_map.144 = (f32[2,32,128]{2,1,0:T(8,128)}, f32[1,16]{1,0:T(1,128)}) custom-call(f32[2,32,128]{2,1,0:T(8,128)S(1)} %shard_map.141._.partial, f32[2,32,128]{2,1,0:T(8,128)S(1)} %get-tuple-element.28.sat, f32[2,32,128]{2,1,0:T(8,128)S(1)} %get-tuple-element.29.lamw, f32[2,32,128]{2,1,0:T(8,128)S(1)} %get-tuple-element.30.lamo, ...), custom_call_target="tpu_custom_call" | custom-call | tf_op jit(solution)/shard_map/pallas_call | solution.py:408
  29.5 0.7 %collective-permute-done.2.other = f32[640,128]{1,0:T(8,128)S(1)} collective-permute-done((f32[640,128]{1,0:T(8,128)S(1)}, f32[640,128]{1,0:T(8,128)S(1)}, u32[]{:S(2)}, u32[]{:S(2)}) %collective-permute-start.2) | collective-permute-done | bytes 327712 | tf_op jit(solution)/shard_map/ppermute | solution.py:474
  30.1 1.2 %shard_map.145 = f32[2,32,128]{2,1,0:T(8,128)} custom-call(f32[5,256,128]{2,1,0:T(8,128)S(1)} %get-tuple-element.49.own, f32[640,128]{1,0:T(8,128)S(1)} %collective-permute-done.2.other), custom_call_target="tpu_custom_call" | custom-call | tf_op jit(solution)/shard_map/pallas_call | solution.py:408
Async XLA Ops:
  1.8 1.6 %collective-permute-start = (f32[5,32,128]{2,1,0:T(8,128)S(1)}, f32[5,32,128]{2,1,0:T(8,128)S(1)}, u32[]{:S(2)}, u32[]{:S(2)}) collective-permute-start(f32[5,32,128]{2,1,0:T(8,128)S(1)} %get-tuple-element.40), channel_id=1, source_target_pairs={{0,1},{1,0},{2,3},{3,2},{4,5},{5,4},{6,7},{7,6},{8,9},{9,8},{10,11... | collective-permute-start | bytes 245768 | tf_op jit(solution)/shard_map/ppermute | solution.py:441
  4.2 24.2 %all-to-all-start = ((f32[16,72,128]{2,1,0:T(8,128)}), f32[16,72,128]{2,1,0:T(8,128)S(1)}, u32[]{:S(2)}, u32[]{:S(2)}) async-start(f32[16,72,128]{2,1,0:T(8,128)} %shard_map.142), calls=%async_computation | async-start | bytes 1179648 | tf_op jit(solution)/shard_map/all_to_all | solution.py:460
  11.2 0.7 %collective-permute-start.1 = (f32[4,32,128]{2,1,0:T(8,128)S(1)}, f32[4,32,128]{2,1,0:T(8,128)S(1)}, u32[]{:S(2)}, u32[]{:S(2)}) collective-permute-start(f32[4,32,128]{2,1,0:T(8,128)S(1)} %get-tuple-element.41), channel_id=1, source_target_pairs={{1,2},{2,1},{3,4},{4,3},{5,6},{6,5},{7,8},{8,7},{9,10},{10,9},{11,... | collective-permute-start | bytes 196616 | tf_op jit(solution)/shard_map/ppermute | solution.py:461
  28.4 1.7 %collective-permute-start.2 = (f32[640,128]{1,0:T(8,128)S(1)}, f32[640,128]{1,0:T(8,128)S(1)}, u32[]{:S(2)}, u32[]{:S(2)}) collective-permute-start(f32[640,128]{1,0:T(8,128)S(1)} %get-tuple-element.50), channel_id=1, source_target_pairs={{0,1},{1,0},{2,3},{3,2},{4,5},{5,4},{6,7},{7,6},{8,9},{9,8},{10,11... | collective-permute-start | bytes 983048 | tf_op jit(solution)/shard_map/ppermute | solution.py:474

commit v12 on v7

--- a/solution.py
+++ b/solution.py
@@ -248,8 +248,8 @@
     grad_bhp[...] = total[:, wells_each : 2 * wells_each]
 
 
-def swap(x):
-    return pltpu.roll(x, 4, 0)
+def turned(x, by):
+    return pltpu.roll(x, by % TILE, 0) if by % TILE else x
 
 
 def sublane():
@@ -259,7 +259,7 @@
 def face_kernel(received, _, own, send, well_rows):
     total = received.shape[0]
     groups = total // CHUNK
-    low = sublane() < 4
+    row = sublane()
 
     def body(parity):
         def tile(s, field):
@@ -270,7 +270,6 @@
 
         count = 2 * groups
         below = None
-        waiting = []
         for x in range(count):
             s = x // 2
             near = x % 4 in (1, 2)
@@ -294,12 +293,12 @@
             fields = (rhs, diag, link, tile(s, CY + x % 2 * ROWS), tile(s, CZ + x % 2 * ROWS))
             for f, value in enumerate(fields):
                 own[f, x * TILE : (x + 1) * TILE] = value
-            waiting += fields
-            while len(waiting) >= 2:
-                a, b = waiting[:2]
-                waiting = waiting[2:]
-                at = ((5 * x + 5 - len(waiting)) // 2 - 1) * TILE
-                send[at : at + TILE] = jnp.where(low, pltpu.roll(a, TILE - 2, 0), pltpu.roll(b, 2, 0))
+            rhs, diag, link, cy, cz = fields
+            start = HALO - 1 + parity
+            send[2 * x * TILE : (2 * x + 1) * TILE] = jnp.where(
+                row < 3, turned(rhs, -start), jnp.where(row < 6, turned(diag, 3 - start), turned(cz, 3))
+            )
+            send[(2 * x + 1) * TILE : (2 * x + 2) * TILE] = jnp.where(row < 3, turned(link, -start), turned(cy, 3 - start))
 
     for parity in range(2):
         pl.when(core() == parity)(functools.partial(body, parity))
@@ -371,11 +370,10 @@
     first = core() == 0
     kept = jnp.logical_and(row >= jnp.where(first, 0, HALO), row < jnp.where(first, ROWS, TILE))
     fields = [[], [], [], [], []]
-    for i in range(5 * count // 2):
-        packed = other[i * TILE : (i + 1) * TILE]
-        turned = swap(packed)
-        for n, value in ((2 * i, jnp.where(first, turned, packed)), (2 * i + 1, jnp.where(first, packed, turned))):
-            x, f = n // 5, n % 5
+    for x in range(count):
+        one, two = (other[i * TILE : (i + 1) * TILE] for i in (2 * x, 2 * x + 1))
+        for f, (packed, by, otherwise) in enumerate(((one, 5, 0), (one, 2, 5), (two, 5, 0), (two, 2, 5), (one, 7, 3))):
+            value = jnp.where(first, turned(packed, by), turned(packed, otherwise))
             fields[f].append(jnp.where(kept, own[f, x * TILE : (x + 1) * TILE], value))
     rhs, diag, link, cy, cz = fields
     solve = solver(diag, link, REDUCTIONS)
@@ -460,7 +458,7 @@
     count = 2 * groups
     own, send, well_rows = call(
         face_kernel,
-        [(5, count * TILE, LANES), (5 * count // 2 * TILE, LANES), (groups, LANES)],
+        [(5, count * TILE, LANES), (2 * count * TILE, LANES), (groups, LANES)],
         received.reshape(groups * CHUNK, LANES),
         partial,
     )

time: 30.1 us -> 30 us (level)
  no operation moved by 1% of the time
where the time goes in v12:
time: 30 us; the launch traced here: 29.7 us
  waiting for transfers between devices  15.3 us (51%)
  starting transfers between devices  8.33 us (28%)
  Pallas kernels  5.37 us (18%)
  between operations  0.72 us (2%)
    all_to_all x1, waiting for transfers between devices, on_device(): lax.all_to_all(packed, 'gx', split_axis=0, concat_axis=0, tiled=True)  14.7 us
    all_to_all x1, starting transfers between devices, on_device(): lax.all_to_all(packed, 'gx', split_axis=0, concat_axis=0, tiled=True)  7.08 us
    pallas_call x7, Pallas kernels, call(): pl.pallas_call(kernel, out_shape=tuple((shaped(o, place) if isinstance(o,...  5.37 us
    ppermute x1, starting transfers between devices, on_device(): from_outside = lax.ppermute(outer, 'gx', outer_pairs)  0.66 us
  transfers between devices with their start and end apart: 4, of which 2 were waited for; matrix products, arithmetic and copies ran while one was open for 0% of the time, Pallas kernels for 8%

profile of v12, /device:TPU:0, one launch (start us, length us, event | category | flops | bytes accessed | tf_op | source)
XLA Modules:
  0.0 29.7 jit_solution(8380340821760007769)
XLA Ops:
  0.6 1.1 %shard_map.139 = (f32[2,32,128]{2,1,0:T(8,128)S(1)}, f32[2,32,128]{2,1,0:T(8,128)S(1)}, f32[2,32,128]{2,1,0:T(8,128)S(1)}, f32[2,32,128]{2,1,0:T(8,128)S(1)}, f3...) custom-call(f32[2,32,128]{2,1,0:T(8,128)} %refs_0_.1, ...), custom_call_target="tpu_custom_call" | custom-call | tf_op jit(solution)/shard_map/pallas_call | solution.py:400
  1.8 0.5 %collective-permute-start = (f32[5,32,128]{2,1,0:T(8,128)S(1)}, f32[5,32,128]{2,1,0:T(8,128)S(1)}, u32[]{:S(2)}, u32[]{:S(2)}) collective-permute-start(f32[5,32,128]{2,1,0:T(8,128)S(1)} %get-tuple-element.40), channel_id=1, source_target_pairs={{0,1},{1,0},{2,3},{3,2},{4,5},{5,4},{6,7},{7,6},{8,9},{9,8},{10,11... | collective-permute-start | bytes 245768 | tf_op jit(solution)/shard_map/ppermute | solution.py:433
  2.3 1.1 %shard_map.140 = (f32[32,128]{1,0:T(8,128)S(1)}, f32[32,128]{1,0:T(8,128)S(1)}, f32[4,32,128]{2,1,0:T(8,128)S(1)}, f32[64,128]{1,0:T(8,128)S(1)}, f32[16,128]{1,0:T(8,128)S(1)}, /*index=5*/f32[16,72,128]{2,1,0:T(8,128)}) custom-call(f32[2,32,128]{2,1,0:T(8,128)S(1)} %get-tuple-element.27.press, f32[2,32,128]{2,1,0:T(8,128)S(1)} %get-tuple-element.28.sat, ...), custom_call_target="tpu_custom_call" | custom-call | tf_op jit(solution)/shard_map/pallas_call | solution.py:400
  3.4 0.0 collective-permute-done.from_chip
  3.4 0.7 %shard_map.142 = f32[16,72,128]{2,1,0:T(8,128)} custom-call(f32[2,32,128]{2,1,0:T(8,128)S(1)} %get-tuple-element.28.sat, f32[2,32,128]{2,1,0:T(8,128)S(1)} %get-tuple-element.29.lamw, f32[2,32,128]{2,1,0:T(8,128)S(1)} %get-tuple-element.30.lamo, f32[2,32,128]{2,1,0:T(8,128)S(1)} %get-tuple-element.31.permx, ...), custom_call_target="tpu_custom_call", output_to_operand_aliasing={{}: (8, {})} | custom-call | tf_op jit(solution)/shard_map/pallas_call | solution.py:400
  4.2 7.1 %all-to-all-start = ((f32[16,72,128]{2,1,0:T(8,128)}), f32[16,72,128]{2,1,0:T(8,128)S(1)}, u32[]{:S(2)}, u32[]{:S(2)}) async-start(f32[16,72,128]{2,1,0:T(8,128)} %shard_map.142), calls=%async_computation | async-start | bytes 1179648 | tf_op jit(solution)/shard_map/all_to_all | solution.py:451
  11.2 0.7 %collective-permute-start.1 = (f32[4,32,128]{2,1,0:T(8,128)S(1)}, f32[4,32,128]{2,1,0:T(8,128)S(1)}, u32[]{:S(2)}, u32[]{:S(2)}) collective-permute-start(f32[4,32,128]{2,1,0:T(8,128)S(1)} %get-tuple-element.41), channel_id=1, source_target_pairs={{1,2},{2,1},{3,4},{4,3},{5,6},{6,5},{7,8},{8,7},{9,10},{10,9},{11,... | collective-permute-start | bytes 196616 | tf_op jit(solution)/shard_map/ppermute | solution.py:452
  11.9 0.0 collective-permute-done.1.from_outside
  11.9 0.2 shard_map.141._.partial
  12.1 14.7 %all-to-all-done = f32[16,72,128]{2,1,0:T(8,128)S(1)} async-done(((f32[16,72,128]{2,1,0:T(8,128)}), f32[16,72,128]{2,1,0:T(8,128)S(1)}, u32[]{:S(2)}, u32[]{:S(2)}) %all-to-all-start) | async-done | bytes 589856 | tf_op jit(solution)/shard_map/all_to_all | solution.py:451
  26.8 0.1 shard_map.143
  26.9 0.1 collective-permute-start.2
  27.0 1.0 %shard_map.144 = (f32[2,32,128]{2,1,0:T(8,128)}, f32[1,16]{1,0:T(1,128)}) custom-call(f32[2,32,128]{2,1,0:T(8,128)S(1)} %shard_map.141._.partial, f32[2,32,128]{2,1,0:T(8,128)S(1)} %get-tuple-element.28.sat, f32[2,32,128]{2,1,0:T(8,128)S(1)} %get-tuple-element.29.lamw, f32[2,32,128]{2,1,0:T(8,128)S(1)} %get-tuple-element.30.lamo, ...), custom_call_target="tpu_custom_call" | custom-call | tf_op jit(solution)/shard_map/pallas_call | solution.py:400
  27.9 0.6 %collective-permute-done.2.other = f32[512,128]{1,0:T(8,128)S(1)} collective-permute-done((f32[512,128]{1,0:T(8,128)S(1)}, f32[512,128]{1,0:T(8,128)S(1)}, u32[]{:S(2)}, u32[]{:S(2)}) %collective-permute-start.2) | collective-permute-done | bytes 262176 | tf_op jit(solution)/shard_map/ppermute | solution.py:465
  28.5 1.2 %shard_map.145 = f32[2,32,128]{2,1,0:T(8,128)} custom-call(f32[5,256,128]{2,1,0:T(8,128)S(1)} %get-tuple-element.49.own, f32[512,128]{1,0:T(8,128)S(1)} %collective-permute-done.2.other), custom_call_target="tpu_custom_call" | custom-call | tf_op jit(solution)/shard_map/pallas_call | solution.py:400
Async XLA Ops:
  1.8 1.6 %collective-permute-start = (f32[5,32,128]{2,1,0:T(8,128)S(1)}, f32[5,32,128]{2,1,0:T(8,128)S(1)}, u32[]{:S(2)}, u32[]{:S(2)}) collective-permute-start(f32[5,32,128]{2,1,0:T(8,128)S(1)} %get-tuple-element.40), channel_id=1, source_target_pairs={{0,1},{1,0},{2,3},{3,2},{4,5},{5,4},{6,7},{7,6},{8,9},{9,8},{10,11... | collective-permute-start | bytes 245768 | tf_op jit(solution)/shard_map/ppermute | solution.py:433
  4.2 22.6 %all-to-all-start = ((f32[16,72,128]{2,1,0:T(8,128)}), f32[16,72,128]{2,1,0:T(8,128)S(1)}, u32[]{:S(2)}, u32[]{:S(2)}) async-start(f32[16,72,128]{2,1,0:T(8,128)} %shard_map.142), calls=%async_computation | async-start | bytes 1179648 | tf_op jit(solution)/shard_map/all_to_all | solution.py:451
  11.2 0.7 %collective-permute-start.1 = (f32[4,32,128]{2,1,0:T(8,128)S(1)}, f32[4,32,128]{2,1,0:T(8,128)S(1)}, u32[]{:S(2)}, u32[]{:S(2)}) collective-permute-start(f32[4,32,128]{2,1,0:T(8,128)S(1)} %get-tuple-element.41), channel_id=1, source_target_pairs={{1,2},{2,1},{3,4},{4,3},{5,6},{6,5},{7,8},{8,7},{9,10},{10,9},{11,... | collective-permute-start | bytes 196616 | tf_op jit(solution)/shard_map/ppermute | solution.py:452
  26.9 1.6 %collective-permute-start.2 = (f32[512,128]{1,0:T(8,128)S(1)}, f32[512,128]{1,0:T(8,128)S(1)}, u32[]{:S(2)}, u32[]{:S(2)}) collective-permute-start(f32[512,128]{1,0:T(8,128)S(1)} %get-tuple-element.50), channel_id=1, source_target_pairs={{0,1},{1,0},{2,3},{3,2},{4,5},{5,4},{6,7},{7,6},{8,9},{9,8},{10,11... | collective-permute-start | bytes 786440 | tf_op jit(solution)/shard_map/ppermute | solution.py:465

commit v13 on v12

--- a/solution.py
+++ b/solution.py
@@ -11,7 +11,7 @@
 oil_viscosity = 2.0
 compressibility = 0.2
 SWEEPS = 4
-REDUCTIONS = 2
+REDUCTIONS = 3
 
 LANES = 128
 TILE = 8

time: 30 us -> 30 us (level)
  no operation moved by 1% of the time
where the time goes in v13:
time: 30 us; the launch traced here: 29.7 us
  waiting for transfers between devices  15.3 us (51%)
  starting transfers between devices  8.33 us (28%)
  Pallas kernels  5.39 us (18%)
  between operations  0.72 us (2%)
    all_to_all x1, waiting for transfers between devices, on_device(): lax.all_to_all(packed, 'gx', split_axis=0, concat_axis=0, tiled=True)  14.7 us
    all_to_all x1, starting transfers between devices, on_device(): lax.all_to_all(packed, 'gx', split_axis=0, concat_axis=0, tiled=True)  7.08 us
    pallas_call x7, Pallas kernels, call(): pl.pallas_call(kernel, out_shape=tuple((shaped(o, place) if isinstance(o,...  5.39 us
    ppermute x1, starting transfers between devices, on_device(): from_outside = lax.ppermute(outer, 'gx', outer_pairs)  0.66 us
  transfers between devices with their start and end apart: 4, of which 2 were waited for; matrix products, arithmetic and copies ran while one was open for 0% of the time, Pallas kernels for 8%

profile of v13, /device:TPU:0, one launch (start us, length us, event | category | flops | bytes accessed | tf_op | source)
XLA Modules:
  0.0 29.7 jit_solution(5705991974365924596)
XLA Ops:
  0.6 1.1 %shard_map.139 = (f32[2,32,128]{2,1,0:T(8,128)S(1)}, f32[2,32,128]{2,1,0:T(8,128)S(1)}, f32[2,32,128]{2,1,0:T(8,128)S(1)}, f32[2,32,128]{2,1,0:T(8,128)S(1)}, f3...) custom-call(f32[2,32,128]{2,1,0:T(8,128)} %refs_0_.1, ...), custom_call_target="tpu_custom_call" | custom-call | tf_op jit(solution)/shard_map/pallas_call | solution.py:400
  1.8 0.5 %collective-permute-start = (f32[5,32,128]{2,1,0:T(8,128)S(1)}, f32[5,32,128]{2,1,0:T(8,128)S(1)}, u32[]{:S(2)}, u32[]{:S(2)}) collective-permute-start(f32[5,32,128]{2,1,0:T(8,128)S(1)} %get-tuple-element.40), channel_id=1, source_target_pairs={{0,1},{1,0},{2,3},{3,2},{4,5},{5,4},{6,7},{7,6},{8,9},{9,8},{10,11... | collective-permute-start | bytes 245768 | tf_op jit(solution)/shard_map/ppermute | solution.py:433
  2.3 1.1 %shard_map.140 = (f32[32,128]{1,0:T(8,128)S(1)}, f32[32,128]{1,0:T(8,128)S(1)}, f32[4,32,128]{2,1,0:T(8,128)S(1)}, f32[64,128]{1,0:T(8,128)S(1)}, f32[16,128]{1,0:T(8,128)S(1)}, /*index=5*/f32[16,72,128]{2,1,0:T(8,128)}) custom-call(f32[2,32,128]{2,1,0:T(8,128)S(1)} %get-tuple-element.27.press, f32[2,32,128]{2,1,0:T(8,128)S(1)} %get-tuple-element.28.sat, ...), custom_call_target="tpu_custom_call" | custom-call | tf_op jit(solution)/shard_map/pallas_call | solution.py:400
  3.4 0.0 collective-permute-done.from_chip
  3.4 0.7 %shard_map.142 = f32[16,72,128]{2,1,0:T(8,128)} custom-call(f32[2,32,128]{2,1,0:T(8,128)S(1)} %get-tuple-element.28.sat, f32[2,32,128]{2,1,0:T(8,128)S(1)} %get-tuple-element.29.lamw, f32[2,32,128]{2,1,0:T(8,128)S(1)} %get-tuple-element.30.lamo, f32[2,32,128]{2,1,0:T(8,128)S(1)} %get-tuple-element.31.permx, ...), custom_call_target="tpu_custom_call", output_to_operand_aliasing={{}: (8, {})} | custom-call | tf_op jit(solution)/shard_map/pallas_call | solution.py:400
  4.2 7.1 %all-to-all-start = ((f32[16,72,128]{2,1,0:T(8,128)}), f32[16,72,128]{2,1,0:T(8,128)S(1)}, u32[]{:S(2)}, u32[]{:S(2)}) async-start(f32[16,72,128]{2,1,0:T(8,128)} %shard_map.142), calls=%async_computation | async-start | bytes 1179648 | tf_op jit(solution)/shard_map/all_to_all | solution.py:451
  11.2 0.7 %collective-permute-start.1 = (f32[4,32,128]{2,1,0:T(8,128)S(1)}, f32[4,32,128]{2,1,0:T(8,128)S(1)}, u32[]{:S(2)}, u32[]{:S(2)}) collective-permute-start(f32[4,32,128]{2,1,0:T(8,128)S(1)} %get-tuple-element.41), channel_id=1, source_target_pairs={{1,2},{2,1},{3,4},{4,3},{5,6},{6,5},{7,8},{8,7},{9,10},{10,9},{11,... | collective-permute-start | bytes 196616 | tf_op jit(solution)/shard_map/ppermute | solution.py:452
  11.9 0.0 collective-permute-done.1.from_outside
  11.9 0.2 shard_map.141._.partial
  12.1 14.7 %all-to-all-done = f32[16,72,128]{2,1,0:T(8,128)S(1)} async-done(((f32[16,72,128]{2,1,0:T(8,128)}), f32[16,72,128]{2,1,0:T(8,128)S(1)}, u32[]{:S(2)}, u32[]{:S(2)}) %all-to-all-start) | async-done | bytes 589856 | tf_op jit(solution)/shard_map/all_to_all | solution.py:451
  26.8 0.1 shard_map.143
  26.9 0.1 collective-permute-start.2
  27.0 1.0 %shard_map.144 = (f32[2,32,128]{2,1,0:T(8,128)}, f32[1,16]{1,0:T(1,128)}) custom-call(f32[2,32,128]{2,1,0:T(8,128)S(1)} %shard_map.141._.partial, f32[2,32,128]{2,1,0:T(8,128)S(1)} %get-tuple-element.28.sat, f32[2,32,128]{2,1,0:T(8,128)S(1)} %get-tuple-element.29.lamw, f32[2,32,128]{2,1,0:T(8,128)S(1)} %get-tuple-element.30.lamo, ...), custom_call_target="tpu_custom_call" | custom-call | tf_op jit(solution)/shard_map/pallas_call | solution.py:400
  27.9 0.6 %collective-permute-done.2.other = f32[512,128]{1,0:T(8,128)S(1)} collective-permute-done((f32[512,128]{1,0:T(8,128)S(1)}, f32[512,128]{1,0:T(8,128)S(1)}, u32[]{:S(2)}, u32[]{:S(2)}) %collective-permute-start.2) | collective-permute-done | bytes 262176 | tf_op jit(solution)/shard_map/ppermute | solution.py:465
  28.5 1.2 %shard_map.145 = f32[2,32,128]{2,1,0:T(8,128)} custom-call(f32[5,256,128]{2,1,0:T(8,128)S(1)} %get-tuple-element.49.own, f32[512,128]{1,0:T(8,128)S(1)} %collective-permute-done.2.other), custom_call_target="tpu_custom_call" | custom-call | tf_op jit(solution)/shard_map/pallas_call | solution.py:400
Async XLA Ops:
  1.8 1.6 %collective-permute-start = (f32[5,32,128]{2,1,0:T(8,128)S(1)}, f32[5,32,128]{2,1,0:T(8,128)S(1)}, u32[]{:S(2)}, u32[]{:S(2)}) collective-permute-start(f32[5,32,128]{2,1,0:T(8,128)S(1)} %get-tuple-element.40), channel_id=1, source_target_pairs={{0,1},{1,0},{2,3},{3,2},{4,5},{5,4},{6,7},{7,6},{8,9},{9,8},{10,11... | collective-permute-start | bytes 245768 | tf_op jit(solution)/shard_map/ppermute | solution.py:433
  4.2 22.6 %all-to-all-start = ((f32[16,72,128]{2,1,0:T(8,128)}), f32[16,72,128]{2,1,0:T(8,128)S(1)}, u32[]{:S(2)}, u32[]{:S(2)}) async-start(f32[16,72,128]{2,1,0:T(8,128)} %shard_map.142), calls=%async_computation | async-start | bytes 1179648 | tf_op jit(solution)/shard_map/all_to_all | solution.py:451
  11.2 0.7 %collective-permute-start.1 = (f32[4,32,128]{2,1,0:T(8,128)S(1)}, f32[4,32,128]{2,1,0:T(8,128)S(1)}, u32[]{:S(2)}, u32[]{:S(2)}) collective-permute-start(f32[4,32,128]{2,1,0:T(8,128)S(1)} %get-tuple-element.41), channel_id=1, source_target_pairs={{1,2},{2,1},{3,4},{4,3},{5,6},{6,5},{7,8},{8,7},{9,10},{10,9},{11,... | collective-permute-start | bytes 196616 | tf_op jit(solution)/shard_map/ppermute | solution.py:452
  26.9 1.6 %collective-permute-start.2 = (f32[512,128]{1,0:T(8,128)S(1)}, f32[512,128]{1,0:T(8,128)S(1)}, u32[]{:S(2)}, u32[]{:S(2)}) collective-permute-start(f32[512,128]{1,0:T(8,128)S(1)} %get-tuple-element.50), channel_id=1, source_target_pairs={{0,1},{1,0},{2,3},{3,2},{4,5},{5,4},{6,7},{7,6},{8,9},{9,8},{10,11... | collective-permute-start | bytes 786440 | tf_op jit(solution)/shard_map/ppermute | solution.py:465
